TPU v7x, 32 devices: a whole 2x2x4 slice. The times are simulated.
32 devices in a mesh: dp: 8 (over y, x, core), tensor: 4 (over z).
Axes of the slice: x: 2, y: 2, z: 4, core: 2. Of those that a mesh axis runs over, the one named last changes fastest.
Arguments:
- layer_input: bfloat16 [8192, 2048], P('dp'), may hold values from -6 to 6
- output_cotangent: bfloat16 [8192, 2048], P('dp'), may hold values from -6 to 6
- block_ids: int32 [8, 1024], P('dp'), may hold values from 0 to 5, never falling along the last dimension, each value on 1 to 256 neighbouring positions
- attention_gain: bfloat16 [2048], P('dp'), may hold values from 0.5 to 1.5
- query_weight: bfloat16 [2048, 2048], P('dp', 'tensor'), may hold values from -0.125 to 0.125
- key_weight: bfloat16 [2048, 2048], P('dp', 'tensor'), may hold values from -0.125 to 0.125
- value_weight: bfloat16 [2048, 2048], P('dp', 'tensor'), may hold values from -0.125 to 0.125
- output_weight: bfloat16 [2048, 2048], P('tensor', 'dp'), may hold values from -0.5 to 0.5
- feedforward_gain: bfloat16 [2048], P('dp'), may hold values from 0.5 to 1.5
- gate_weight: bfloat16 [2048, 8192], P('dp', 'tensor'), may hold values from -0.125 to 0.125
- up_weight: bfloat16 [2048, 8192], P('dp', 'tensor'), may hold values from -0.125 to 0.125
- down_weight: bfloat16 [8192, 2048], P('tensor', 'dp'), may hold values from -0.0625 to 0.0625
Outputs:
- layer_output: bfloat16 [8192, 2048], P('dp')
- input_grad: float32 [8192, 2048], P('dp')
- attention_gain_grad: float32 [2048], P('dp')
- query_weight_grad: float32 [2048, 2048], P('dp', 'tensor')
- key_weight_grad: float32 [2048, 2048], P('dp', 'tensor')
- value_weight_grad: float32 [2048, 2048], P('dp', 'tensor')
- output_weight_grad: float32 [2048, 2048], P('tensor', 'dp')
- feedforward_gain_grad: float32 [2048], P('dp')
- gate_weight_grad: float32 [2048, 8192], P('dp', 'tensor')
- up_weight_grad: float32 [2048, 8192], P('dp', 'tensor')
- down_weight_grad: float32 [8192, 2048], P('tensor', 'dp')
- head_maxima: float32 [32], replicated
- query_clipped: bfloat16 [2048, 2048], P('dp', 'tensor')
- key_clipped: bfloat16 [2048, 2048], P('dp', 'tensor')
Inputs may be any that keep to these rules, and one draw needn't show every extreme that they name: `block_ids`: within each sequence the ids never fall; each id covers 1 to 256 consecutive tokens and some id exactly 256.
All inputs are finite; a program needn't handle non-finite values.
Results may differ from a plain program's by a relative error of at most 0.022.
Values may be sent and summed in bfloat16 or wider, within the bound.
No kernel may reach another device: no remote copies, remote signals or barrier semaphores. Data moves between devices by JAX's collectives and lax.ppermute only.
A program may use at most 256 MiB of HBM per device.

v0:
```python
import jax
import jax.numpy as jnp
from jax import lax
from jax.sharding import PartitionSpec as P

HEADS = 32
HEAD_DIM = 64


norm_epsilon = 1e-05
rope_theta = 130000.0
clip_tau = 2.0
neg_big = -1e30


def rope_tables(length, head_dim):
    half_dim = head_dim // 2
    inverse = rope_theta ** (-(2.0 * jnp.arange(half_dim, dtype=jnp.float32)) / head_dim)
    angles = jnp.arange(length, dtype=jnp.float32)[:, None] * inverse[None, :]
    angles = jnp.concatenate([angles, angles], -1)
    return (jnp.cos(angles)[:, None, :], jnp.sin(angles)[:, None, :])


def rotate_heads(values, cosine, sine):
    half_dim = values.shape[-1] // 2
    turned = jnp.concatenate([-values[..., half_dim:], values[..., :half_dim]], -1)
    return values * cosine + turned * sine


def unrotate_heads(grads, cosine, sine):
    half_dim = grads.shape[-1] // 2
    sined = grads * sine
    return grads * cosine + jnp.concatenate([sined[..., half_dim:], -sined[..., :half_dim]], -1)


def normalize(values, gain):
    inverse = lax.rsqrt(jnp.mean(values * values, -1, keepdims=True) + norm_epsilon)
    return (inverse, values * inverse * gain.astype(jnp.float32))


def norm_back(d_normed, values, inverse, gain):
    scaled = d_normed * gain.astype(jnp.float32)
    return inverse * scaled - values * inverse**3 * jnp.mean(scaled * values, -1, keepdims=True)


def attend_forward(parts):
    query_block, key_block, value_block, block_row = parts
    factor = query_block.shape[-1] ** (-0.5)
    scores = (
        jnp.einsum("qhd,khd->hqk", query_block, key_block, preferred_element_type=jnp.float32)
        * factor
    )
    visible = block_row[None, :] <= block_row[:, None]
    masked = jnp.where(visible[None], scores, neg_big)
    peak = jnp.max(masked, -1, keepdims=True)
    expo = jnp.exp(masked - peak)
    summed = jnp.sum(expo, -1, keepdims=True)
    probs = (expo / summed).astype(jnp.bfloat16)
    mixed = jnp.einsum(
        "hqk,khd->qhd", probs, value_block, preferred_element_type=jnp.float32
    ).astype(jnp.bfloat16)
    return (mixed, (peak + jnp.log(summed))[..., 0], jnp.max(peak[..., 0], -1))


def attend_backward(parts):
    query_block, key_block, value_block, block_row, log_total, d_mixed = parts
    factor = query_block.shape[-1] ** (-0.5)
    scores = (
        jnp.einsum("qhd,khd->hqk", query_block, key_block, preferred_element_type=jnp.float32)
        * factor
    )
    visible = block_row[None, :] <= block_row[:, None]
    masked = jnp.where(visible[None], scores, neg_big)
    probs = jnp.exp(masked - log_total[..., None])
    d_values = jnp.einsum(
        "hqk,qhd->khd", probs.astype(jnp.bfloat16), d_mixed, preferred_element_type=jnp.float32
    )
    d_probs = jnp.einsum("qhd,khd->hqk", d_mixed, value_block, preferred_element_type=jnp.float32)
    center = jnp.sum(probs * d_probs, -1, keepdims=True)
    d_scores = (probs * (d_probs - center)).astype(jnp.bfloat16)
    d_queries = (
        jnp.einsum("hqk,khd->qhd", d_scores, key_block, preferred_element_type=jnp.float32) * factor
    )
    d_keys = (
        jnp.einsum("hqk,qhd->khd", d_scores, query_block, preferred_element_type=jnp.float32)
        * factor
    )
    return (d_queries, d_keys, d_values)


def local(
    layer_input,
    output_cotangent,
    block_ids,
    attention_gain,
    query_weight,
    key_weight,
    value_weight,
    output_weight,
    feedforward_gain,
    gate_weight,
    up_weight,
    down_weight,
):
    seq_count = block_ids.shape[0]
    seq_len = block_ids.shape[1]
    tok_count = layer_input.shape[0]
    gathered = (
        lax.all_gather(attention_gain, "dp", axis=0, tiled=True),
        lax.all_gather(query_weight, "dp", axis=0, tiled=True),
        lax.all_gather(key_weight, "dp", axis=0, tiled=True),
        lax.all_gather(value_weight, "dp", axis=0, tiled=True),
        lax.all_gather(output_weight, "dp", axis=1, tiled=True),
        lax.all_gather(feedforward_gain, "dp", axis=0, tiled=True),
        lax.all_gather(gate_weight, "dp", axis=0, tiled=True),
        lax.all_gather(up_weight, "dp", axis=0, tiled=True),
        lax.all_gather(down_weight, "dp", axis=1, tiled=True),
    )
    (
        gain_one,
        query_full,
        key_full,
        value_full,
        output_full,
        gain_two,
        gate_full,
        up_full,
        down_full,
    ) = gathered
    heads_here = query_full.shape[1] // HEAD_DIM
    shape_four = (seq_count, seq_len, heads_here, HEAD_DIM)
    cosine, sine = rope_tables(seq_len, HEAD_DIM)
    position = lax.axis_index("tensor")
    inputs = layer_input.astype(jnp.float32)
    inv_one, pre_one = normalize(inputs, gain_one)
    normed_one = pre_one.astype(jnp.bfloat16)
    queries = rotate_heads(
        jnp.dot(normed_one, query_full, preferred_element_type=jnp.float32).reshape(shape_four),
        cosine,
        sine,
    ).astype(jnp.bfloat16)
    keys = rotate_heads(
        jnp.dot(normed_one, key_full, preferred_element_type=jnp.float32).reshape(shape_four),
        cosine,
        sine,
    ).astype(jnp.bfloat16)
    values = (
        jnp.dot(normed_one, value_full, preferred_element_type=jnp.float32)
        .astype(jnp.bfloat16)
        .reshape(shape_four)
    )
    attended, log_total, peaks = lax.map(attend_forward, (queries, keys, values, block_ids))
    attended_flat = attended.reshape(tok_count, -1)
    attn_part = jnp.dot(attended_flat, output_full, preferred_element_type=jnp.float32)
    resid = inputs + lax.psum(attn_part, "tensor")
    inv_two, pre_two = normalize(resid, gain_two)
    normed_two = pre_two.astype(jnp.bfloat16)
    gate_pre = jnp.dot(normed_two, gate_full, preferred_element_type=jnp.float32)
    up_pre = jnp.dot(normed_two, up_full, preferred_element_type=jnp.float32)
    sigma = jax.nn.sigmoid(gate_pre)
    swish = gate_pre * sigma
    hidden = (swish * up_pre).astype(jnp.bfloat16)
    mlp_part = jnp.dot(hidden, down_full, preferred_element_type=jnp.float32)
    layer_output = (
        resid + lax.psum(mlp_part.astype(jnp.bfloat16), "tensor").astype(jnp.float32)
    ).astype(jnp.bfloat16)
    cotangent = output_cotangent.astype(jnp.float32)
    d_hidden = jnp.einsum(
        "td,fd->tf", output_cotangent, down_full, preferred_element_type=jnp.float32
    )
    down_grad = jnp.einsum(
        "tf,td->fd", hidden, output_cotangent, preferred_element_type=jnp.float32
    )
    d_gate = (d_hidden * up_pre * sigma * (1.0 + gate_pre * (1.0 - sigma))).astype(jnp.bfloat16)
    d_up = (d_hidden * swish).astype(jnp.bfloat16)
    gate_grad = jnp.einsum("td,tf->df", normed_two, d_gate, preferred_element_type=jnp.float32)
    up_grad = jnp.einsum("td,tf->df", normed_two, d_up, preferred_element_type=jnp.float32)
    mlp_back = jnp.einsum(
        "tf,df->td", d_gate, gate_full, preferred_element_type=jnp.float32
    ) + jnp.einsum("tf,df->td", d_up, up_full, preferred_element_type=jnp.float32)
    d_normed_two = lax.psum(mlp_back, "tensor")
    gain_two_grad = jnp.sum(d_normed_two * resid * inv_two, 0)
    d_resid = cotangent + norm_back(d_normed_two, resid, inv_two, gain_two)
    d_attn = d_resid.astype(jnp.bfloat16)
    output_grad = jnp.einsum("te,td->ed", attended_flat, d_attn, preferred_element_type=jnp.float32)
    d_attended = (
        jnp.einsum("td,ed->te", d_attn, output_full, preferred_element_type=jnp.float32)
        .astype(jnp.bfloat16)
        .reshape(shape_four)
    )
    d_queries, d_keys, d_values = lax.map(
        attend_backward, (queries, keys, values, block_ids, log_total, d_attended)
    )
    d_query_lin = (
        unrotate_heads(d_queries, cosine, sine).reshape(tok_count, -1).astype(jnp.bfloat16)
    )
    d_key_lin = unrotate_heads(d_keys, cosine, sine).reshape(tok_count, -1).astype(jnp.bfloat16)
    d_value_lin = d_values.reshape(tok_count, -1).astype(jnp.bfloat16)
    query_grad = jnp.einsum(
        "td,te->de", normed_one, d_query_lin, preferred_element_type=jnp.float32
    )
    key_grad = jnp.einsum("td,te->de", normed_one, d_key_lin, preferred_element_type=jnp.float32)
    value_grad = jnp.einsum(
        "td,te->de", normed_one, d_value_lin, preferred_element_type=jnp.float32
    )
    attn_back = jnp.einsum("te,de->td", d_query_lin, query_full, preferred_element_type=jnp.float32)
    attn_back = attn_back + jnp.einsum(
        "te,de->td", d_key_lin, key_full, preferred_element_type=jnp.float32
    )
    attn_back = attn_back + jnp.einsum(
        "te,de->td", d_value_lin, value_full, preferred_element_type=jnp.float32
    )
    d_normed_one = lax.psum(attn_back.astype(jnp.bfloat16), "tensor").astype(jnp.float32)
    gain_one_grad = jnp.sum(d_normed_one * inputs * inv_one, 0)
    input_grad = d_resid + norm_back(d_normed_one, inputs, inv_one, gain_one)
    summed = (
        lax.psum_scatter(
            gain_one_grad.astype(jnp.bfloat16), "dp", scatter_dimension=0, tiled=True
        ).astype(jnp.float32),
        lax.psum_scatter(
            query_grad.astype(jnp.bfloat16), "dp", scatter_dimension=0, tiled=True
        ).astype(jnp.float32),
        lax.psum_scatter(
            key_grad.astype(jnp.bfloat16), "dp", scatter_dimension=0, tiled=True
        ).astype(jnp.float32),
        lax.psum_scatter(
            value_grad.astype(jnp.bfloat16), "dp", scatter_dimension=0, tiled=True
        ).astype(jnp.float32),
        lax.psum_scatter(
            output_grad.astype(jnp.bfloat16), "dp", scatter_dimension=1, tiled=True
        ).astype(jnp.float32),
        lax.psum_scatter(
            gain_two_grad.astype(jnp.bfloat16), "dp", scatter_dimension=0, tiled=True
        ).astype(jnp.float32),
        lax.psum_scatter(
            gate_grad.astype(jnp.bfloat16), "dp", scatter_dimension=0, tiled=True
        ).astype(jnp.float32),
        lax.psum_scatter(
            up_grad.astype(jnp.bfloat16), "dp", scatter_dimension=0, tiled=True
        ).astype(jnp.float32),
        lax.psum_scatter(
            down_grad.astype(jnp.bfloat16), "dp", scatter_dimension=1, tiled=True
        ).astype(jnp.float32),
    )
    local_peak = jnp.max(peaks, 0)
    owner = jnp.arange(HEADS) // heads_here
    spread_peak = jnp.where(owner == position, jnp.tile(local_peak, HEADS // heads_here), neg_big)
    head_maxima = lax.pmax(spread_peak, ("dp", "tensor"))
    factor = jnp.sqrt(clip_tau / jnp.maximum(head_maxima, clip_tau))
    mine = lax.dynamic_slice_in_dim(factor, position * heads_here, heads_here)
    columns = jnp.repeat(mine, HEAD_DIM)
    query_clipped = (query_weight.astype(jnp.float32) * columns[None, :]).astype(jnp.bfloat16)
    key_clipped = (key_weight.astype(jnp.float32) * columns[None, :]).astype(jnp.bfloat16)
    return (
        layer_output,
        input_grad,
        summed[0],
        summed[1],
        summed[2],
        summed[3],
        summed[4],
        summed[5],
        summed[6],
        summed[7],
        summed[8],
        head_maxima,
        query_clipped,
        key_clipped,
    )


def solution(mesh):
    in_specs = (
        P("dp", None),
        P("dp", None),
        P("dp", None),
        P("dp"),
        P("dp", "tensor"),
        P("dp", "tensor"),
        P("dp", "tensor"),
        P("tensor", "dp"),
        P("dp"),
        P("dp", "tensor"),
        P("dp", "tensor"),
        P("tensor", "dp"),
    )
    out_specs = (
        P("dp", None),
        P("dp", None),
        P("dp"),
        P("dp", "tensor"),
        P("dp", "tensor"),
        P("dp", "tensor"),
        P("tensor", "dp"),
        P("dp"),
        P("dp", "tensor"),
        P("dp", "tensor"),
        P("tensor", "dp"),
        P(),
        P("dp", "tensor"),
        P("dp", "tensor"),
    )
    return jax.shard_map(local, mesh=mesh, in_specs=in_specs, out_specs=out_specs, check_vma=False)
```

profile of v0, /device:TPU:0, one launch (start us, length us, event | category | flops | bytes accessed | tf_op | source)
XLA Modules:
  0.0 1715.0 jit_solution(610153105649933168)
XLA Ops:
  14.4 10.3 all-gather
  27.9 12.6 all-gather.14.cloned.1.call-done
  47.4 23.0 %all-gather.12.cloned.1.call-done = bf16[2048,512]{1,0:T(8,128)(2,1)} async-done(((bf16[256,512]{1,0:T(8,128)(2,1)}), bf16[2048,512]{1,0:T(8,128)(2,1)}) %all-gather.12.cloned.1.call-update) | async-done | bytes 2097168 | tf_op jit(solution)/shard_map/all_gather | solution.py:110
  77.3 14.0 fusion.50
  91.3 13.4 fusion
  111.1 14.0 fusion.34
  139.7 8.8 all-gather.1
  148.5 280.0 %all-reduce.8.cloned.1.call-done = f32[1024,2048]{1,0:T(8,128)} async-done(((f32[1024,2048]{1,0:T(8,128)}), f32[1024,2048]{1,0:T(8,128)}) %all-reduce.8.cloned.1.call-update) | async-done | bytes 8388624 | tf_op jit(solution)/shard_map/psum | solution.py:155
  440.6 43.1 %all-gather.20.cloned.1.call-done = bf16[2048,2048]{1,0:T(8,128)(2,1)} async-done(((bf16[256,2048]{1,0:T(8,128)(2,1)}), bf16[2048,2048]{1,0:T(8,128)(2,1)}) %all-gather.20.cloned.1.call-update) | async-done | bytes 8388624 | tf_op jit(solution)/shard_map/all_gather | solution.py:116
  483.7 14.9 fusion.53
  498.6 41.4 %all-gather.18.cloned.1.call-done = bf16[2048,2048]{1,0:T(8,128)(2,1)} async-done(((bf16[256,2048]{1,0:T(8,128)(2,1)}), bf16[2048,2048]{1,0:T(8,128)(2,1)}) %all-gather.18.cloned.1.call-update) | async-done | bytes 8388624 | tf_op jit(solution)/shard_map/all_gather | solution.py:115
  540.0 14.6 fusion.52
  554.6 43.3 %all-gather.22.cloned.1.call-done = bf16[2048,2048]{1,0:T(8,128)(2,1)} async-done(((bf16[2048,256]{1,0:T(8,128)(2,1)}), bf16[2048,2048]{1,0:T(8,128)(2,1)}) %all-gather.22.cloned.1.call-update) | async-done | bytes 8388624 | tf_op jit(solution)/shard_map/all_gather | solution.py:117
  597.9 21.8 %multiply_convert_fusion.1 = (bf16[1024,2048]{1,0:T(8,128)(2,1)}, bf16[1024,2048]{1,0:T(8,128)(2,1)}, bf16[1024,2048]{1,0:T(8,128)(2,1)}) fusion(f32[1024,2048]{1,0:T(8,128)} %fusion.52, f32[1024,2048]{1,0:T(8,128)} %fusion.53, bf16[1024,2048]{1,0:T(8,128)(2,1)} %param.13, bf16[2048,2048]{1,0:T(8,128)(2,1)} %all-gather.22.cloned.1.call-done), kind=kOutput, calls=%fused_computation.32 | convolution fusion | flops 8621391872 | bytes 41943040 | tf_op jit(solution)/shard_map/td,fd->tf/dot_general | solution.py:168
  619.7 12.9 fusion.54
  632.6 13.6 convolution_add_fusion
  646.2 290.9 %all-reduce.10.cloned.1.call-done = f32[1024,2048]{1,0:T(8,128)} async-done(((f32[1024,2048]{1,0:T(8,128)}), f32[1024,2048]{1,0:T(8,128)}) %all-reduce.10.cloned.1.call-update) | async-done | bytes 8388624 | tf_op jit(solution)/shard_map/psum | solution.py:181
  964.8 14.1 fusion.28
  985.7 22.6 %fusion.49 = (f32[8]{0:T(128)S(1)}, f32[8,1024]{1,0:T(8,128)S(1)}, f32[8,1024,1024]{1,2,0:T(8,128)}) fusion(f32[8,1024,1024]{1,2,0:T(8,128)} %get-tuple-element.108, f32[8,1024]{1,0:T(8,128)S(1)} %log_add_fusion, bf16[1024,8,64]{0,2,1:T(8,128)(2,1)S(1)} %bitcast.101, bf16[1024,8,64]{0,2,1:T(8,128)(2,1)S(1)} %bitcast.105), kind=kOutput, calls=%fused_computation.111 | convolution fusion | flops 1107288064 | bytes 69271584 | tf_op jit(solution)/shard_map/while/body/eval_jaxpr/qhd,khd->hqk/dot_general | solution.py:78
  1008.8 29.6 %multiply_convert_fusion = bf16[8,1024,1024]{1,2,0:T(8,128)(2,1)} fusion(f32[8,1024,1024]{1,2,0:T(8,128)} %get-tuple-element.109, f32[8,1024,1024]{1,2,0:T(8,128)} %get-tuple-element.108, f32[8,1024]{1,0:T(8,128)S(1)} %get-tuple-element.59, f32[8,1024]{1,0:T(8,128)S(1)} %log_add_fusion), kind=kLoop, calls=%fused_computation | loop fusion | flops 33554432 | bytes 83951616 | tf_op jit(solution)/shard_map/while/body/eval_jaxpr/convert_element_type | solution.py:80
  1038.4 11.5 fusion.57
  1072.9 14.4 convolution_convert_fusion
  1087.4 14.1 convolution_convert_fusion.1
  1101.7 14.1 convolution_convert_fusion.2
  1115.9 14.2 convolution_convert_fusion.3
  1142.9 39.6 %pmax.7 = f32[32]{0:T(128)S(1)} all-reduce(f32[32]{0:T(128)S(1)} %compare_select_fusion), channel_id=1, replica_groups=mesh['dp'=8,'tensor'=4] {'dp','tensor'}, use_global_device_ids=true, to_apply=%region_23.24 | all-reduce | flops 32 | bytes 256 | tf_op jit(solution)/shard_map/pmax | solution.py:248
  1190.9 36.2 %reduce-scatter.20.cloned.1.call-done = bf16[2048,256]{1,0:T(8,128)(2,1)} async-done(((bf16[2048,2048]{1,0:T(8,128)(2,1)}), bf16[2048,256]{1,0:T(8,128)(2,1)}) %reduce-scatter.20.cloned.1.call-update) | async-done | bytes 1048592 | tf_op jit(solution)/shard_map/reduce_scatter | solution.py:241
  1229.8 72.3 %reduce-scatter.18.cloned.1.call-done = bf16[256,2048]{1,0:T(8,128)(2,1)} async-done(((bf16[2048,2048]{1,0:T(8,128)(2,1)}), bf16[256,2048]{1,0:T(8,128)(2,1)}) %reduce-scatter.18.cloned.1.call-update) | async-done | bytes 1048592 | tf_op jit(solution)/shard_map/reduce_scatter | solution.py:238
  1304.9 71.8 %reduce-scatter.16.cloned.1.call-done = bf16[256,2048]{1,0:T(8,128)(2,1)} async-done(((bf16[2048,2048]{1,0:T(8,128)(2,1)}), bf16[256,2048]{1,0:T(8,128)(2,1)}) %reduce-scatter.16.cloned.1.call-update) | async-done | bytes 1048592 | tf_op jit(solution)/shard_map/reduce_scatter | solution.py:235
  1379.5 292.0 %all-reduce.12.cloned.1.call-done = (bf16[1024,2048]{1,0:T(8,128)(2,1)}, bf16[1024,2048]{1,0:T(8,128)(2,1)}) async-done(((bf16[1024,2048]{1,0:T(8,128)(2,1)}, bf16[1024,2048]{1,0:T(8,128)(2,1)}), (bf16[1024,2048]{1,0:T(8,128)(2,1)}, bf16[1024,2048]{1,0:T(8,128)(2,1)})) %all-reduce.12.cloned.1.call-update) | async-done | bytes 8388624 | tf_op jit(solution)/shard_map/psum | solution.py:165
  1683.3 13.9 all-reduce.2
  1698.6 9.5 fusion.8
  (165 shorter events, 157.1 us)
Async XLA Ops:
  7.2 33.4 %all-gather.14.cloned.1.call-start = ((), (), s32[]{:S(2)}) async-start(), calls=%async_computation.9 | async-start | bytes 2359296 | tf_op jit(solution)/shard_map/all_gather | solution.py:111
  7.9 62.4 %all-gather.12.cloned.1.call-start = ((), (), s32[]{:S(2)}) async-start(), calls=%async_computation.8 | async-start | bytes 2359296 | tf_op jit(solution)/shard_map/all_gather | solution.py:110
  8.7 96.0 %all-gather.10.cloned.1.call-start = ((), (), s32[]{:S(2)}) async-start(), calls=%async_computation.7 | async-start | bytes 2359296 | tf_op jit(solution)/shard_map/all_gather | solution.py:112
  9.4 120.7 %all-gather.16.cloned.1.call-start = ((), (), s32[]{:S(2)}) async-start(), calls=%async_computation.10 | async-start | bytes 2359296 | tf_op jit(solution)/shard_map/all_gather | solution.py:113
  10.0 418.5 %all-reduce.8.cloned.1.call-start = ((), (), s32[]{:S(2)}) async-start(), calls=%async_computation.11 | async-start | bytes 16777216 | tf_op jit(solution)/shard_map/psum | solution.py:155
  14.4 90.3 %copy-start.24 = (f32[1024]{0:T(1024)}, f32[1024]{0:T(1024)S(1)}, u32[]{:S(2)}) copy-start(f32[1024]{0:T(1024)S(1)} %get-tuple-element.102) | copy-start | bytes 12292
  24.7 80.0 %copy-start.22 = (f32[8,1,256]{2,1,0:T(1,128)}, f32[8,1,256]{2,1,0:T(1,128)S(1)}, u32[]{:S(2)}) copy-start(f32[8,1,256]{2,1,0:T(1,128)S(1)} %convert_element_type.224) | copy-start | bytes 24580
  77.3 14.0 copy-start.6
  77.3 14.0 copy-start.8
  137.5 346.2 %all-gather.20.cloned.1.call-start = ((), (), s32[]{:S(2)}) async-start(), calls=%async_computation.13 | async-start | bytes 9437184 | tf_op jit(solution)/shard_map/all_gather | solution.py:116
  138.1 401.9 %all-gather.18.cloned.1.call-start = ((), (), s32[]{:S(2)}) async-start(), calls=%async_computation.12 | async-start | bytes 9437184 | tf_op jit(solution)/shard_map/all_gather | solution.py:115
  138.9 459.0 %all-gather.22.cloned.1.call-start = ((), (), s32[]{:S(2)}) async-start(), calls=%async_computation.14 | async-start | bytes 9437184 | tf_op jit(solution)/shard_map/all_gather | solution.py:117
  139.6 797.6 %all-reduce.10.cloned.1.call-start = ((), (), s32[]{:S(2)}) async-start(), calls=%async_computation.15 | async-start | bytes 16777216 | tf_op jit(solution)/shard_map/psum | solution.py:181
  619.7 12.9 copy-start.33
  646.2 537.5 %reduce-scatter.14.cloned.1.call-start = ((), (), s32[]{:S(2)}) async-start(), calls=%async_computation.19 | async-start | bytes 2359296 | tf_op jit(solution)/shard_map/reduce_scatter | solution.py:229
  937.2 9.4 copy-start.9
  958.2 227.3 %reduce-scatter.12.cloned.1.call-start = ((), (), s32[]{:S(2)}) async-start(), calls=%async_computation.18 | async-start | bytes 2359296 | tf_op jit(solution)/shard_map/reduce_scatter | solution.py:226
  964.8 14.1 copy-start.23
  964.8 14.1 copy-start.25
  1008.4 178.9 %reduce-scatter.8.cloned.1.call-start = ((), (), s32[]{:S(2)}) async-start(), calls=%async_computation.16 | async-start | bytes 2359296 | tf_op jit(solution)/shard_map/reduce_scatter | solution.py:220
  1038.4 11.5 copy-start.7
  1049.9 8.8 copy-start.16
  1066.3 122.8 %reduce-scatter.10.cloned.1.call-start = ((), (), s32[]{:S(2)}) async-start(), calls=%async_computation.17 | async-start | bytes 2359296 | tf_op jit(solution)/shard_map/reduce_scatter | solution.py:223
  1072.9 154.2 %reduce-scatter.20.cloned.1.call-start = ((), (), s32[]{:S(2)}) async-start(), calls=%async_computation.22 | async-start | bytes 9437184 | tf_op jit(solution)/shard_map/reduce_scatter | solution.py:241
  1087.3 214.8 %reduce-scatter.18.cloned.1.call-start = ((), (), s32[]{:S(2)}) async-start(), calls=%async_computation.21 | async-start | bytes 9437184 | tf_op jit(solution)/shard_map/reduce_scatter | solution.py:238
  1101.5 275.3 %reduce-scatter.16.cloned.1.call-start = ((), (), s32[]{:S(2)}) async-start(), calls=%async_computation.20 | async-start | bytes 9437184 | tf_op jit(solution)/shard_map/reduce_scatter | solution.py:235
  1115.8 555.7 %all-reduce.12.cloned.1.call-start = ((), (), s32[]{:S(2)}) async-start(), calls=%async_computation.23 | async-start | bytes 16777216 | tf_op jit(solution)/shard_map/psum | solution.py:165
  1115.9 14.3 copy-start.28
  1141.0 41.8 %copy-start.18 = (bf16[256,512]{1,0:T(8,128)(2,1)S(1)}, bf16[256,512]{1,0:T(8,128)(2,1)}, u32[]{:S(2)}) copy-start(bf16[256,512]{1,0:T(8,128)(2,1)} %param.17) | copy-start | bytes 786436
  1141.0 41.8 %copy-start.19 = (bf16[256,512]{1,0:T(8,128)(2,1)S(1)}, bf16[256,512]{1,0:T(8,128)(2,1)}, u32[]{:S(2)}) copy-start(bf16[256,512]{1,0:T(8,128)(2,1)} %param.16) | copy-start | bytes 786436
  1182.6 497.4 %copy-start.32 = (f32[32]{0:T(128)}, f32[32]{0:T(128)S(1)}, u32[]{:S(2)}) copy-start(f32[32]{0:T(128)S(1)} %pmax.7) | copy-start | bytes 388
  1680.0 18.6 %copy-start.26 = (f32[1024]{0:T(1024)S(1)}, f32[1024]{0:T(1024)}, u32[]{:S(2)}) copy-start(f32[1024]{0:T(1024)} %get-tuple-element.101) | copy-start | bytes 12292
  (19 other events, 83.0 us)
Sparse Core Ops, SparseCore 0:
  9.9 30.5 all-gather.13
  42.4 27.8 all-gather.11
  72.2 27.8 all-gather.9
  101.9 28.1 all-gather.15
  137.6 290.8 all-reduce.7
  430.2 53.3 all-gather.19
  485.6 54.3 all-gather.17
  541.9 55.9 all-gather.21
  646.3 290.8 all-reduce.9
  958.3 40.2 reduce-scatter.13
  1008.5 40.7 reduce-scatter.11
  1066.4 40.1 reduce-scatter.7
  1110.8 41.6 reduce-scatter.9
  1155.8 71.2 reduce-scatter.19
  1230.8 71.2 reduce-scatter.17
  1305.5 71.2 reduce-scatter.15
  1380.0 291.5 all-reduce.11
where the time goes:
time: 1720 us
  waiting for transfers between devices  1220 us (71%)
  matrix products  281 us (16%)
  other arithmetic  116 us (7%)
  blocking collectives  72.7 us (4%)
    psum x1, waiting for transfers between devices, local(): lax.psum(mlp_part.astype(jnp.bfloat16), 'tensor').astype(jnp.float32)  292 us
    psum x1, waiting for transfers between devices, local(): d_normed_two = lax.psum(mlp_back, 'tensor')  291 us
    psum x1, waiting for transfers between devices, local(): resid = inputs + lax.psum(attn_part, 'tensor')  280 us
    reduce_scatter x1, waiting for transfers between devices, local(): lax.psum_scatter(up_grad.astype(jnp.bfloat16), 'dp', scatter_dimension=0,...  72.3 us
    reduce_scatter x1, waiting for transfers between devices, local(): lax.psum_scatter(gate_grad.astype(jnp.bfloat16), 'dp', scatter_dimension=...  71.8 us
    all_gather x1, waiting for transfers between devices, local(): lax.all_gather(down_weight, 'dp', axis=1, tiled=True)  43.3 us
    all_gather x1, waiting for transfers between devices, local(): lax.all_gather(up_weight, 'dp', axis=0, tiled=True)  43.1 us
    all_gather x1, waiting for transfers between devices, local(): lax.all_gather(gate_weight, 'dp', axis=0, tiled=True)  41.4 us
  transfers between devices with their start and end apart: 17, of which 12 were waited for; matrix products, arithmetic and copies ran while one was open for 18% of the time, Pallas kernels for 0%

commit v1 on v0

v1 whole, which is shorter than its diff:
```python
import jax
import jax.numpy as jnp
import numpy as np
from jax import lax
from jax.experimental import pallas as pl
from jax.experimental.pallas import tpu as pltpu
from jax.sharding import PartitionSpec as P

HEAD_DIM = 64
BLOCK = 256
LANES = 128
norm_epsilon = 1e-05
rope_theta = 130000.0
clip_tau = 2.0
neg_big = -1e30
f32 = jnp.float32
bf16 = jnp.bfloat16


def mm(a, b):
    return lax.dot_general(a, b, (((1,), (0,)), ((), ())), preferred_element_type=f32)


def mm_nt(a, b):
    return lax.dot_general(a, b, (((1,), (1,)), ((), ())), preferred_element_type=f32)


def mm_tn(a, b):
    return lax.dot_general(a, b, (((0,), (0,)), ((), ())), preferred_element_type=f32)


def rope_tables(length):
    half_dim = HEAD_DIM // 2
    inverse = rope_theta ** (-(2.0 * np.arange(half_dim)) / HEAD_DIM)
    angles = np.tile(np.arange(length)[:, None] * inverse[None, :], (1, LANES // half_dim))
    return jnp.asarray(np.cos(angles), f32), jnp.asarray(np.sin(angles), f32)


def first_half(shape):
    return lax.broadcasted_iota(jnp.int32, shape, 1) % HEAD_DIM < HEAD_DIM // 2


def rotate(values, cosine, sine):
    ahead = pltpu.roll(values, LANES - HEAD_DIM // 2, 1)
    behind = pltpu.roll(values, HEAD_DIM // 2, 1)
    return values * cosine + jnp.where(first_half(values.shape), -ahead, behind) * sine


def unrotate(grads, cosine, sine):
    sined = grads * sine
    ahead = pltpu.roll(sined, LANES - HEAD_DIM // 2, 1)
    behind = pltpu.roll(sined, HEAD_DIM // 2, 1)
    return grads * cosine + jnp.where(first_half(grads.shape), ahead, -behind)


def of_head(values, head):
    lane = lax.broadcasted_iota(jnp.int32, values.shape, 1)
    return jnp.where(lane // HEAD_DIM == head, values, jnp.zeros_like(values))


def hide(scores, ends, start):
    tail = scores[start:]
    key = lax.broadcasted_iota(jnp.int32, tail.shape, 0) + start
    tail = jnp.where(key < ends, tail, neg_big)
    return jnp.concatenate([scores[:start], tail], 0) if start else tail


def fold(combine, values):
    while values.shape[0] % 16 == 0:
        near = values.shape[0] // 2
        values = combine(values[:near], values[near:])
    return values


def forward_kernel(
    q_ref, k_ref, v_ref, cos_ref, sin_ref, end_ref, qo_ref, ko_ref, vo_ref, att_ref, stat_ref
):
    length = q_ref.shape[0]
    cosine, sine = cos_ref[...], sin_ref[...]
    qo_ref[...] = (rotate(q_ref[...], cosine, sine).astype(bf16) * HEAD_DIM ** (-0.5)).astype(bf16)
    ko_ref[...] = rotate(k_ref[...], cosine, sine).astype(bf16)
    values = v_ref[...].astype(bf16)
    vo_ref[...] = values
    lane = lax.broadcasted_iota(jnp.int32, values.shape, 1)
    sides = [jnp.where(lane // HEAD_DIM == head, values, jnp.ones_like(values)) for head in range(2)]
    for start in range(0, length, BLOCK):
        keys = min(length, start + 2 * BLOCK)
        here = slice(start, start + BLOCK)
        tile, ends = qo_ref[here, :], end_ref[:, here]
        mixed = []
        for head in range(2):
            scores = hide(mm_nt(ko_ref[:keys, :], of_head(tile, head)), ends, start)
            peak = jnp.max(fold(jnp.maximum, scores), 0, keepdims=True)
            expo = jnp.exp(scores - peak).astype(bf16)
            product = mm_tn(expo, sides[head][:keys])
            mixed.append(product / pltpu.roll(product, HEAD_DIM, 1))
            row = HEAD_DIM * (1 - head)
            total = jnp.transpose(product)[row : row + 1]
            stat_ref[0, head : head + 1, here] = peak + jnp.log(total)
            stat_ref[0, 2 + head : 3 + head, here] = peak
        att_ref[here, :] = jnp.where(lane[:BLOCK] < HEAD_DIM, mixed[0], mixed[1]).astype(bf16)


def backward_kernel(
    q_ref, k_ref, v_ref, att_ref, da_ref, stat_ref, cos_ref, sin_ref, end_ref, dq_ref, dk_ref, dv_ref, dk_sum, dv_sum
):
    length = q_ref.shape[0]
    turned = jnp.transpose(k_ref[...].astype(f32)).astype(bf16)
    dk_sum[...] = jnp.zeros_like(dk_sum)
    dv_sum[...] = jnp.zeros_like(dv_sum)
    for start in range(0, length, BLOCK):
        keys = min(length, start + 2 * BLOCK)
        here = slice(start, start + BLOCK)
        tile, d_tile = q_ref[here, :], da_ref[here, :]
        ends = end_ref[:, here]
        both = jnp.transpose(att_ref[here, :].astype(f32) * d_tile.astype(f32))
        d_mixed, probs_both, ds_both, tiles, d_tiles = [], [], [], [], []
        for head in range(2):
            tile_head, d_head = of_head(tile, head), of_head(d_tile, head)
            span = slice(head * HEAD_DIM, (head + 1) * HEAD_DIM)
            center = jnp.sum(both[span, :], 0, keepdims=True)
            scores = hide(mm_nt(k_ref[:keys, :], tile_head), ends, start)
            probs = jnp.exp(scores - stat_ref[0, head : head + 1, here])
            d_probs = mm_nt(v_ref[:keys, :], d_head)
            d_scores = (probs * (d_probs - center)).astype(bf16)
            d_mixed.append(mm(turned[span, :keys], d_scores))
            probs_both.append(probs.astype(bf16))
            ds_both.append(d_scores)
            tiles.append(tile_head)
            d_tiles.append(d_head)
        dv_sum[:keys, :] += mm(jnp.concatenate(probs_both, 1), jnp.concatenate(d_tiles, 0))
        dk_sum[:keys, :] += mm(jnp.concatenate(ds_both, 1), jnp.concatenate(tiles, 0))
        d_queries = jnp.transpose(jnp.concatenate(d_mixed, 0)) * HEAD_DIM ** (-0.5)
        dq_ref[here, :] = unrotate(d_queries, cos_ref[here, :], sin_ref[here, :]).astype(bf16)
    dk_ref[...] = unrotate(dk_sum[...], cos_ref[...], sin_ref[...]).astype(bf16)
    dv_ref[...] = dv_sum[...].astype(bf16)


def last_visible(block_row):
    return jnp.sum(block_row[:, None] <= block_row[None, :], 0, dtype=jnp.int32)[None]


def attend_forward(qkv, ends, cosine, sine):
    length, columns = qkv.shape[0], qkv.shape[1] // 3
    pairs = columns // LANES
    spec = lambda base: pl.BlockSpec((length, LANES), lambda p: (0, base + p))
    fixed = lambda shape: pl.BlockSpec(shape, lambda p: (0, 0))
    whole = jax.ShapeDtypeStruct((length, columns), bf16)
    return pl.pallas_call(
        forward_kernel,
        grid=(pairs,),
        in_specs=[spec(0), spec(pairs), spec(2 * pairs)] + [fixed((length, LANES))] * 2 + [fixed((1, length))],
        out_specs=[spec(0)] * 4 + [pl.BlockSpec((1, 8, length), lambda p: (p, 0, 0))],
        out_shape=[whole] * 4 + [jax.ShapeDtypeStruct((pairs, 8, length), f32)],
        compiler_params=pltpu.CompilerParams(vmem_limit_bytes=48 * 2**20),
        cost_estimate=pl.CostEstimate(flops=4 * length * length * columns, bytes_accessed=10 * length * columns * 2, transcendentals=length * length * columns // HEAD_DIM),
        name="attend_forward",
    )(qkv, qkv, qkv, cosine, sine, ends)


def attend_backward(queries, keys, values, attended, d_attended, stats, ends, cosine, sine):
    length, columns = queries.shape
    pairs = columns // LANES
    spec = pl.BlockSpec((length, LANES), lambda p: (0, p))
    fixed = lambda shape: pl.BlockSpec(shape, lambda p: (0, 0))
    whole = jax.ShapeDtypeStruct((length, columns), bf16)
    return pl.pallas_call(
        backward_kernel,
        grid=(pairs,),
        in_specs=[spec] * 5 + [pl.BlockSpec((1, 8, length), lambda p: (p, 0, 0))] + [fixed((length, LANES))] * 2 + [fixed((1, length))],
        out_specs=[spec] * 3,
        out_shape=[whole] * 3,
        scratch_shapes=[pltpu.VMEM((length, LANES), f32)] * 2,
        compiler_params=pltpu.CompilerParams(vmem_limit_bytes=48 * 2**20),
        cost_estimate=pl.CostEstimate(flops=10 * length * length * columns, bytes_accessed=16 * length * columns, transcendentals=length * length * columns // HEAD_DIM),
        name="attend_backward",
    )(queries, keys, values, attended, d_attended, stats, cosine, sine, ends)


def norm_kernel(order_ref, value_ref, hat_ref, same_ref, *, count):
    values = value_ref[...].astype(f32)
    block = value_ref.shape[1] // count
    inverse = lax.rsqrt(jnp.mean(values * values, -1, keepdims=True) + norm_epsilon)
    for place in range(count):
        source = pl.ds(pl.multiple_of(order_ref[place] * block, block), block)
        target = slice(place * block, (place + 1) * block)
        taken = value_ref[:, source]
        same_ref[:, target] = taken
        hat_ref[:, target] = (taken.astype(f32) * inverse).astype(bf16)


def normed_in_order(values, order):
    rows, width = values.shape
    spec = pl.BlockSpec((BLOCK, width), lambda i, order: (i, 0))
    return pl.pallas_call(
        lambda *refs: norm_kernel(*refs, count=order.shape[0]),
        grid_spec=pltpu.PrefetchScalarGridSpec(
            num_scalar_prefetch=1, grid=(rows // BLOCK,), in_specs=[spec], out_specs=[spec] * 2
        ),
        out_shape=[jax.ShapeDtypeStruct(values.shape, bf16)] * 2,
        compiler_params=pltpu.CompilerParams(vmem_limit_bytes=32 * 2**20),
        name="norm_in_order",
    )(order, values)


def move_kernel(order_ref, value_ref, out_ref):
    out_ref[...] = value_ref[...]


def in_order(values, order):
    rows, width = values.shape
    block = (rows, width // order.shape[0])
    return pl.pallas_call(
        move_kernel,
        grid_spec=pltpu.PrefetchScalarGridSpec(
            num_scalar_prefetch=1,
            grid=order.shape,
            in_specs=[pl.BlockSpec(block, lambda p, order: (0, order[p]))],
            out_specs=pl.BlockSpec(block, lambda p, order: (0, p)),
        ),
        out_shape=jax.ShapeDtypeStruct(values.shape, values.dtype),
        name="in_order",
    )(order, values)


def resid_kernel(part_ref, left_ref, right_ref, resid_ref, hat_ref):
    resid = part_ref[...] + mm_nt(left_ref[...], right_ref[...])
    resid_ref[...] = resid
    inverse = lax.rsqrt(jnp.mean(resid * resid, -1, keepdims=True) + norm_epsilon)
    hat_ref[...] = (resid * inverse).astype(bf16)


def resid_and_norm(part, left, right):
    rows, width = part.shape
    spec = pl.BlockSpec((BLOCK, width), lambda i: (i, 0))
    return pl.pallas_call(
        resid_kernel,
        grid=(rows // BLOCK,),
        in_specs=[
            spec,
            pl.BlockSpec((BLOCK, left.shape[1]), lambda i: (i, 0)),
            pl.BlockSpec(right.shape, lambda i: (0, 0)),
        ],
        out_specs=[spec] * 2,
        out_shape=[
            jax.ShapeDtypeStruct(part.shape, f32),
            jax.ShapeDtypeStruct(part.shape, bf16),
        ],
        compiler_params=pltpu.CompilerParams(vmem_limit_bytes=40 * 2**20),
        cost_estimate=pl.CostEstimate(
            flops=2 * rows * width * left.shape[1], bytes_accessed=16 * rows * width, transcendentals=0
        ),
        name="resid_and_norm",
    )(part, left, right)


def after(value, *others):
    return lax.optimization_barrier((value, *others))[0]


def flip(value, mask):
    count = lax.axis_size("dp")
    return lax.ppermute(value, "dp", [(i, i ^ mask) for i in range(count)])


def shift(value, step):
    count = lax.axis_size("tensor")
    return lax.ppermute(value, "tensor", [(i, (i + step) % count) for i in range(count)])


def cross(value, forward):
    masks = (2, 4) if forward else (4, 2)
    return lax.ppermute(value, "dp", [(i, i ^ masks[i % 2]) for i in range(8)])


def gather_order(here, count):
    if count != 8:
        return here ^ jnp.arange(count, dtype=jnp.int32)
    first = jnp.where(here % 2 == 0, 2, 4)
    masks = [0, 1, first, first ^ 1, 6, 7 ^ first, 6 ^ first, 7]
    return here ^ jnp.stack([jnp.asarray(mask, jnp.int32) for mask in masks])


def gather(own):
    count = lax.axis_size("dp")
    if count != 8:
        bit = 1
        while bit < count:
            own = jnp.concatenate([own, flip(own, bit)], 0)
            bit *= 2
        return own, (own,)
    beside = flip(own, 1)
    first = cross(own, True)
    second = cross(beside, True)
    third = cross(first, False)
    most = jnp.concatenate([first, second, third], 0)
    return jnp.concatenate([own, beside, most, flip(most, 1)], 0), (second, third)


def reduced(near, far):
    count = lax.axis_size("dp")
    if count != 8:
        whole = jnp.concatenate([near, far], 0).astype(bf16)
        while count > 1:
            middle = whole.shape[0] // 2
            whole = whole[:middle] + flip(whole[middle:], count // 2)
            count //= 2
        return whole.astype(f32)
    rows = near.shape[0] // 5
    arrived = flip(far.astype(bf16), 1)
    diagonal = (near[4 * rows :] + arrived[2 * rows :].astype(f32)).astype(bf16)
    diagonal = cross(diagonal, False)
    outward = near[2 * rows : 4 * rows] + arrived[: 2 * rows].astype(f32)
    outward = jnp.concatenate(
        [outward[:rows] + diagonal.astype(f32), outward[rows:]], 0
    ).astype(bf16)
    inward = cross(outward, True)
    beside = (near[rows : 2 * rows] + inward[rows:].astype(f32)).astype(bf16)
    return near[:rows] + inward[:rows].astype(f32) + flip(beside, 1).astype(f32)


def ring_gather(own):
    pieces = [own]
    for _ in range(lax.axis_size("tensor") - 1):
        pieces.append(shift(pieces[-1], 1))
    return pieces


def ring_scatter(piece, beside=()):
    count = lax.axis_size("tensor")
    total = piece(1).astype(bf16)
    done = []
    for step in range(2, count + 1):
        arrived = shift(total, 1)
        if step - 2 < len(beside):
            done.append(beside[step - 2](total))
            arrived = after(arrived, done[-1])
        total = arrived.astype(f32) + piece(step % count).astype(f32)
        if step < count:
            total = total.astype(bf16)
    return (total, done) if beside else total


def local(
    layer_input,
    output_cotangent,
    block_ids,
    attention_gain,
    query_weight,
    key_weight,
    value_weight,
    output_weight,
    feedforward_gain,
    gate_weight,
    up_weight,
    down_weight,
):
    tokens, width = layer_input.shape
    here = lax.axis_index("dp")
    place = lax.axis_index("tensor")
    dp_count = lax.axis_size("dp")
    ring = lax.axis_size("tensor")
    part = tokens // ring
    columns = query_weight.shape[1]
    heads_here = columns // HEAD_DIM
    heads = heads_here * ring

    near_order = gather_order(here, dp_count)
    true_order = jnp.argsort(near_order).astype(jnp.int32)

    def token_part(values, owner):
        return lax.dynamic_slice_in_dim(values, owner * part, part, 0)

    gain_one = attention_gain.astype(f32)[:, None]
    gain_two = feedforward_gain.astype(f32)[:, None]
    qkv_weight = jnp.concatenate([query_weight, key_weight, value_weight], 1).astype(f32)
    qkv_all, first = gather((qkv_weight * gain_one).astype(bf16))
    out_own = jnp.transpose(jnp.concatenate(ring_gather(output_weight), 0))
    out_all, first = gather(after(out_own, *first))
    gate_all, first = gather(after((gate_weight.astype(f32) * gain_two).astype(bf16), *first))
    up_all, first = gather(after((up_weight.astype(f32) * gain_two).astype(bf16), *first))
    down_all, first = gather(after(jnp.transpose(down_weight), *first))

    hat, inputs = normed_in_order(layer_input, near_order)
    cot = in_order(output_cotangent, near_order)
    cosine, sine = rope_tables(tokens)
    ends = last_visible(block_ids[0])
    queries, keys, values, attended, stats = attend_forward(mm(hat, qkv_all), ends, cosine, sine)
    pieces = ring_gather(attended)

    local_peak = jnp.max(stats[:, 2:4], -1).reshape(heads_here)
    bit = 1
    while bit < dp_count:
        local_peak = jnp.maximum(local_peak, flip(local_peak, bit))
        bit *= 2
    peak_pieces = jnp.concatenate(
        [local_peak] + [shift(local_peak, step) for step in range(1, ring)]
    )
    order = (place - jnp.arange(heads) // heads_here) % ring * heads_here
    head_maxima = peak_pieces[order + jnp.arange(heads) % heads_here]
    factor = jnp.sqrt(clip_tau / jnp.maximum(local_peak, clip_tau))
    factors = jnp.repeat(factor, HEAD_DIM)[None, :]
    query_clipped = (query_weight.astype(f32) * factors).astype(bf16)
    key_clipped = (key_weight.astype(f32) * factors).astype(bf16)

    most = jnp.concatenate(pieces[:-1], 1)
    resid_most = inputs.astype(f32) + mm_nt(most, out_all[:, : most.shape[1]])
    resid, hat_two = resid_and_norm(resid_most, pieces[-1], out_all[:, most.shape[1] :])
    gate = mm(hat_two, gate_all)
    up = mm(hat_two, up_all)
    sigma = jax.nn.sigmoid(gate)
    swish = gate * sigma
    hidden = (swish * up).astype(bf16)
    d_hidden = mm(cot, down_all)
    d_gate = (d_hidden * up * sigma * (1.0 + gate * (1.0 - sigma))).astype(bf16)
    d_up = (d_hidden * swish).astype(bf16)

    def mid_grad(t):
        owner = (place - t) % ring
        return mm_nt(token_part(d_gate, owner), gate_all) + mm_nt(token_part(d_up, owner), up_all)

    near_width = width // 8 * 5 if dp_count == 8 else width // 2

    def grad_blocks(left, right):
        return mm_tn(left[:, :near_width], right), mm_tn(left[:, near_width:], right).astype(bf16)

    def down_work(ready):
        return grad_blocks(cot, after(hidden, ready))

    def gate_work(ready):
        return grad_blocks(after(hat_two, ready), d_gate)

    def up_work(ready):
        return grad_blocks(after(hat_two, ready), d_up)

    scaled_two, halves = ring_scatter(mid_grad, (down_work, gate_work, up_work))
    down_grad = jnp.transpose(reduced(*halves[0]))
    gate_sum = reduced(*halves[1])
    up_sum = reduced(*halves[2])
    resid_part, cot_part = token_part(resid, place), token_part(cot, place)
    inv_part = lax.rsqrt(jnp.mean(resid_part * resid_part, -1, keepdims=True) + norm_epsilon)
    d_resid = (
        cot_part.astype(f32)
        + inv_part * scaled_two
        - resid_part * inv_part**3 * jnp.mean(scaled_two * resid_part, -1, keepdims=True)
    )
    d_attn = d_resid.astype(bf16)
    d_att = mm(d_attn, out_all).astype(bf16)
    d_pieces = [d_att[:, :columns]] + [
        shift(d_att[:, t * columns : (t + 1) * columns], -t) for t in range(1, ring)
    ]
    d_attended = jnp.zeros((tokens, columns), bf16)
    for t, piece in enumerate(d_pieces):
        d_attended = lax.dynamic_update_slice(d_attended, piece, ((place + t) % ring * part, 0))

    def out_piece(t):
        return mm_nt(token_part(hidden, (place - t) % ring), down_all)

    def spread(values, dtype):
        whole = jnp.zeros((tokens, width), dtype)
        for t, piece in enumerate(ring_gather(values)):
            start = (place - t) % ring * part
            whole = lax.dynamic_update_slice(whole, piece.astype(dtype), (start, 0))
        return whole

    out_part = (resid_part + ring_scatter(out_piece)).astype(bf16)
    layer_output = spread(in_order(out_part, true_order), bf16)

    d_query, d_key, d_value = attend_backward(
        queries, keys, values, attended, d_attended, stats, ends, cosine, sine
    )
    d_qkv = jnp.concatenate([d_query, d_key, d_value], 1)

    def in_grad(t):
        return mm_nt(token_part(d_qkv, (place - t) % ring), qkv_all)

    att_part = jnp.concatenate([token_part(piece, place) for piece in pieces], 1)

    def out_work(ready):
        return grad_blocks(after(d_attn, ready), att_part)

    def qkv_work(ready):
        return grad_blocks(after(hat, ready), d_qkv)

    scaled_one, halves = ring_scatter(in_grad, (qkv_work, out_work))
    qkv_sum = reduced(*halves[0])
    out_sum = jnp.transpose(reduced(*halves[1]))
    output_grad = ring_scatter(lambda t: out_sum[t * columns : (t + 1) * columns])
    input_part = token_part(inputs, place).astype(f32)
    inv_part = lax.rsqrt(jnp.mean(input_part * input_part, -1, keepdims=True) + norm_epsilon)
    input_back = (
        d_resid
        + inv_part * scaled_one
        - input_part * inv_part**3 * jnp.mean(scaled_one * input_part, -1, keepdims=True)
    )
    input_grad = spread(in_order(input_back.astype(bf16), true_order), f32)
    qkv_grad = qkv_sum * gain_one

    gains = jnp.stack(
        [
            jnp.sum(qkv_sum * qkv_weight, 1),
            jnp.sum(gate_sum * gate_weight.astype(f32), 1)
            + jnp.sum(up_sum * up_weight.astype(f32), 1),
        ]
    )
    gain_pieces = jnp.stack([gains] + [shift(gains, step) for step in range(1, ring)])
    gain_sum = jnp.sum(jnp.take(gain_pieces, (place - jnp.arange(ring)) % ring, axis=0), 0)

    return (
        layer_output,
        input_grad,
        gain_sum[0],
        qkv_grad[:, :columns],
        qkv_grad[:, columns : 2 * columns],
        qkv_grad[:, 2 * columns :],
        output_grad,
        gain_sum[1],
        gate_sum * gain_two,
        up_sum * gain_two,
        down_grad,
        head_maxima,
        query_clipped,
        key_clipped,
    )


def solution(mesh):
    in_specs = (
        P("dp", None),
        P("dp", None),
        P("dp", None),
        P("dp"),
        P("dp", "tensor"),
        P("dp", "tensor"),
        P("dp", "tensor"),
        P("tensor", "dp"),
        P("dp"),
        P("dp", "tensor"),
        P("dp", "tensor"),
        P("tensor", "dp"),
    )
    out_specs = (
        P("dp", None),
        P("dp", None),
        P("dp"),
        P("dp", "tensor"),
        P("dp", "tensor"),
        P("dp", "tensor"),
        P("tensor", "dp"),
        P("dp"),
        P("dp", "tensor"),
        P("dp", "tensor"),
        P("tensor", "dp"),
        P(),
        P("dp", "tensor"),
        P("dp", "tensor"),
    )
    return jax.shard_map(local, mesh=mesh, in_specs=in_specs, out_specs=out_specs, check_vma=False)
```

time: 1720 us -> 808 us (0.47)
  waiting for transfers between devices: 1220 us -> 238 us
  local copies, waits for them, and re-layouts: 11.7 us -> 98.2 us
  blocking collectives: 72.7 us -> 0 us
  Pallas kernels: 0 us -> 70.4 us
  starting transfers between devices: 1.68 us -> 62.8 us
  matrix products: 281 us -> 228 us
  other arithmetic: 116 us -> 94 us
    psum x3 -> x0, waiting for transfers between devices: 863 us -> none  [the longest x1 292 us: local(): lax.psum(mlp_part.astype(jnp.bfloat16), 'tensor').astype(jnp.float32)]
    ppermute x0 -> x81, waiting for transfers between devices: none -> 238 us  [the longest x33 172 us: shift(): lax.ppermute(value, 'tensor', [(i, (i + step) % count) for i in range(cou...]
    reduce_scatter x7 -> x0, waiting for transfers between devices: 180 us -> none  [the longest x1 72.3 us: local(): lax.psum_scatter(up_grad.astype(jnp.bfloat16), 'dp', scatter_dimension=0,...]
    all_gather x7 -> x0, waiting for transfers between devices: 169 us -> none  [the longest x1 43.3 us: local(): lax.all_gather(down_weight, 'dp', axis=1, tiled=True)]
    pallas_call x0 -> x7, Pallas kernels: none -> 70.4 us  [the longest x1 22.8 us: attend_backward(): pl.pallas_call(backward_kernel, grid=(pairs,), in_specs=[spec] * 5 + [pl....]
    ppermute x0 -> x81, starting transfers between devices: none -> 62.8 us  [the longest x33 33.4 us: shift(): lax.ppermute(value, 'tensor', [(i, (i + step) % count) for i in range(cou...]
    dot_general x27 -> x32, matrix products: 281 us -> 228 us  [the longest x17 119 us: mm_nt(): lax.dot_general(a, b, (((1,), (1,)), ((), ())), preferred_element_type=f32)]
    unnamed x71 -> x193, local copies, waits for them, and re-layouts: 11.4 us -> 60.1 us
  transfers between devices with their start and end apart: 17 -> 81, of which waited for: 12 -> 31; matrix products, arithmetic and copies ran while one was open for 18% -> 42% of each run, Pallas kernels for 0% -> 9%
where the time goes in v1:
time: 808 us; the launch traced here: 794 us
  waiting for transfers between devices  238 us (29%)
  matrix products  228 us (28%)
  local copies, waits for them, and re-layouts  98.2 us (12%)
  other arithmetic  94 us (12%)
  Pallas kernels  70.4 us (9%)
  starting transfers between devices  62.8 us (8%)
    ppermute x33, waiting for transfers between devices, shift(): lax.ppermute(value, 'tensor', [(i, (i + step) % count) for i in range(cou...  172 us
    dot_general x17, matrix products, mm_nt(): lax.dot_general(a, b, (((1,), (1,)), ((), ())), preferred_element_type=f32)  119 us
    unnamed x193, local copies, waits for them, and re-layouts  60.1 us
    ppermute x25, waiting for transfers between devices, cross(): return lax.ppermute(value, 'dp', [(i, i ^ masks[i % 2]) for i in range(8)])  59.5 us
    dot_general x5, matrix products, mm(): lax.dot_general(a, b, (((1,), (0,)), ((), ())), preferred_element_type=f32)  54.8 us
    dot_general x10, matrix products, mm_tn(): lax.dot_general(a, b, (((0,), (0,)), ((), ())), preferred_element_type=f32)  54.6 us
    ppermute x33, starting transfers between devices, shift(): lax.ppermute(value, 'tensor', [(i, (i + step) % count) for i in range(cou...  33.4 us
    ppermute x25, starting transfers between devices, cross(): return lax.ppermute(value, 'dp', [(i, i ^ masks[i % 2]) for i in range(8)])  25.3 us
  transfers between devices with their start and end apart: 81, of which 31 were waited for; matrix products, arithmetic and copies ran while one was open for 42% of the time, Pallas kernels for 9%

profile of v1, /device:TPU:0, one launch (start us, length us, event | category | flops | bytes accessed | tf_op | source)
XLA Modules:
  0.0 794.1 jit_solution(13749065718035322261)
XLA Ops:
  20.4 7.7 collective-permute-done.8
  29.2 7.3 in_order.4
  55.1 7.2 collective-permute-done.11
  68.8 16.7 %collective-permute-done.13 = bf16[256,2048]{1,0:T(8,128)(2,1)S(1)} collective-permute-done((bf16[256,2048]{1,0:T(8,128)(2,1)S(1)}, bf16[256,2048]{1,0:T(8,128)(2,1)S(1)}, u32[]{:S(2)}, u32[]{:S(2)}) %collective-permute-start.13) | collective-permute-done | bytes 1048608 | tf_op jit(solution)/shard_map/ppermute | solution.py:273
  91.1 9.3 %collective-permute-done.17 = bf16[256,2048]{1,0:T(8,128)(2,1)} collective-permute-done((bf16[256,2048]{1,0:T(8,128)(2,1)S(1)}, bf16[256,2048]{1,0:T(8,128)(2,1)}, u32[]{:S(2)}, u32[]{:S(2)}) %collective-permute-start.17) | collective-permute-done | bytes 1048608 | tf_op jit(solution)/shard_map/ppermute | solution.py:273
  103.7 8.5 %fusion.134.q_ref.k_ref.v_ref = f32[1024,1536]{1,0:T(8,128)} fusion(bf16[1024,2048]{1,0:T(8,128)(2,1)S(1)} %copy-done.16, bf16[2048,1536]{1,0:T(8,128)(2,1)S(1)} %constant_dynamic-update-slice_fusion), kind=kOutput, calls=%fused_computation.292 | convolution fusion | flops 6442450944 | bytes 16777216 | tf_op jit(solution)/shard_map/dot_general | solution.py:21
  112.2 17.5 %attend_forward.1 = (bf16[1024,512]{1,0:T(8,128)(2,1)S(1)}, bf16[1024,512]{1,0:T(8,128)(2,1)S(1)}, bf16[1024,512]{1,0:T(8,128)(2,1)S(1)}, bf16[1024,512]{1,0:T(8,128)(2,1)S(1)}, f32[4,8,1024]{2,1,0:T(8,128)S(1)}) custom-call(f32[1024,1536]{1,0:T(8,128)} %fusion.134.q_ref.k_ref.v_ref, f32[1024,1536]{1,0:T(8,128)} %fusion.134.q_ref.k_ref.v_ref, ...), custom_call_target="tpu_custom_call" | custom-call | flops 2147483648 | bytes 10485760 | tf_op jit(solution)/shard_map/attend_forward/pallas_call | solution.py:149
  147.9 8.2 %collective-permute-done.80 = f32[8]{0:T(128)S(1)} collective-permute-done((f32[8]{0:T(128)S(1)}, f32[8]{0:T(128)S(1)}, u32[]{:S(2)}, u32[]{:S(2)}) %collective-permute-start.80) | collective-permute-done | bytes 64 | tf_op jit(solution)/shard_map/ppermute | solution.py:268
  184.1 14.1 %collective-permute-done.6 = bf16[1024,512]{1,0:T(8,128)(2,1)S(1)} collective-permute-done((bf16[1024,512]{1,0:T(8,128)(2,1)}, bf16[1024,512]{1,0:T(8,128)(2,1)S(1)}, u32[]{:S(2)}, u32[]{:S(2)}) %collective-permute-start.6) | collective-permute-done | bytes 1048608 | tf_op jit(solution)/shard_map/ppermute | solution.py:268
  204.0 11.1 %convert_add_fusion.part_ref = f32[1024,2048]{1,0:T(8,128)} fusion(bf16[1024,2048]{1,0:T(8,128)(2,1)S(1)} %copy-done.6, bf16[2048,2048]{1,0:T(8,128)(2,1)} %constant_dynamic-update-slice_fusion.6, bf16[1024,512]{1,0:T(8,128)(2,1)S(1)} %collective-permute-done.6, bf16[1024,512]{1,0:T(8,128)(2,1)} %collective-permute-done.5, ...), kind=kOutput, calls=%fused_computation.7 | convolution fusion | flops 6456082432 | bytes 22020096 | tf_op jit(solution)/shard_map/dot_general | solution.py:25
  224.9 8.7 %resid_and_norm.1 = (f32[1024,2048]{1,0:T(8,128)}, bf16[1024,2048]{1,0:T(8,128)(2,1)S(1)}) custom-call(f32[1024,2048]{1,0:T(8,128)} %convert_add_fusion.part_ref, bf16[1024,512]{1,0:T(8,128)(2,1)S(1)} %collective-permute-done.15.left_ref, bf16[2048,512]{1,0:T(8,128)(2,1)S(1)} %slice.315.right_ref), custom_call_target="tpu_custom_call" | custom-call | flops 2147483648 | bytes 33554432 | tf_op jit(solution)/shard_map/resid_and_norm/pallas_call | solution.py:236
  238.3 21.2 %collective-permute-done.29 = bf16[256,2048]{0,1:T(8,128)(2,1)S(1)} collective-permute-done((bf16[256,2048]{0,1:T(8,128)(2,1)S(1)}, bf16[256,2048]{0,1:T(8,128)(2,1)S(1)}, u32[]{:S(2)}, u32[]{:S(2)}) %collective-permute-start.29) | collective-permute-done | bytes 1048608 | tf_op jit(solution)/shard_map/ppermute | solution.py:273
  275.4 11.0 %fusion.135 = f32[1024,2048]{1,0:T(8,128)} fusion(bf16[1024,2048]{1,0:T(8,128)(2,1)S(1)} %get-tuple-element.55, bf16[2048,2048]{1,0:T(8,128)(2,1)S(1)} %constant_dynamic-update-slice_fusion.18), kind=kOutput, calls=%fused_computation.293 | convolution fusion | flops 8589934592 | bytes 20971520 | tf_op jit(solution)/shard_map/dot_general | solution.py:21
  289.7 13.2 %fusion.136 = f32[1024,2048]{1,0:T(8,128)} fusion(bf16[1024,2048]{1,0:T(8,128)(2,1)S(1)} %copy-done.24, bf16[2048,2048]{0,1:T(8,128)(2,1)} %constant_dynamic-update-slice_fusion.24), kind=kOutput, calls=%fused_computation.294 | convolution fusion | flops 8589934592 | bytes 20971520 | tf_op jit(solution)/shard_map/dot_general | solution.py:21
  302.9 19.8 %multiply_convert_fusion.1 = (bf16[1024,2048]{1,0:T(8,128)(2,1)}, bf16[1024,2048]{1,0:T(8,128)(2,1)}, bf16[1024,2048]{1,0:T(8,128)(2,1)}) fusion(f32[1024,2048]{1,0:T(8,128)} %fusion.136, f32[1024,2048]{1,0:T(8,128)} %fusion.135, bf16[1024,2048]{1,0:T(8,128)(2,1)S(1)} %get-tuple-element.55, bf16[2048,2048]{1,0:T(8,128)(2,1)} %constant_dynamic-update-slice_fusion.12), kind=kOutput, calls=%fused_computation.3 | convolution fusion | flops 8621391872 | bytes 41943040 | tf_op jit(solution)/shard_map/dot_general | solution.py:21
  353.7 10.4 %fusion.56 = f32[256,2048]{1,0:T(8,128)} fusion(bf16[2048,2048]{1,0:T(8,128)(2,1)} %copy-done.51, bf16[1024,2048]{1,0:T(8,128)(2,1)} %get-tuple-element.135, s32[]{:T(128)S(6)} %select_n.217), kind=kOutput, calls=%fused_computation.141 | convolution fusion | flops 2147483648 | bytes 11534340 | tf_op jit(solution)/shard_map/dot_general | solution.py:25
  364.0 7.4 fusion.59
  371.4 7.5 fusion.64
  378.9 7.9 add_convert_fusion.3
  398.6 8.4 %fusion.16 = f32[1280,2048]{1,0:T(8,128)} fusion(bf16[1024,2048]{1,0:T(8,128)(2,1)S(1)} %copy-done.62, bf16[1024,2048]{1,0:T(8,128)(2,1)S(1)} %get-tuple-element.55), kind=kOutput, calls=%fused_computation.43 | convolution fusion | flops 5368709120 | bytes 17301504 | tf_op jit(solution)/shard_map/dot_general | solution.py:29
  421.9 15.4 %collective-permute-done.32 = bf16[256,2048]{1,0:T(8,128)(2,1)} collective-permute-done((bf16[256,2048]{1,0:T(8,128)(2,1)}, bf16[256,2048]{1,0:T(8,128)(2,1)}, u32[]{:S(2)}, u32[]{:S(2)}) %collective-permute-start.32) | collective-permute-done | bytes 1048608 | tf_op jit(solution)/shard_map/ppermute | solution.py:268
  437.4 7.2 add_convert_fusion.5
  449.7 8.4 %fusion.14 = f32[1280,2048]{1,0:T(8,128)} fusion(bf16[1024,2048]{1,0:T(8,128)(2,1)S(1)} %copy-done.65, bf16[1024,2048]{1,0:T(8,128)(2,1)S(1)} %get-tuple-element.55), kind=kOutput, calls=%fused_computation.41 | convolution fusion | flops 5368709120 | bytes 17301504 | tf_op jit(solution)/shard_map/dot_general | solution.py:29
  466.9 7.9 multiply_reduce_fusion.1
  504.5 7.2 collective-permute-start.34
  514.6 22.8 %attend_backward.1 = (bf16[1024,512]{1,0:T(8,128)(2,1)S(1)}, bf16[1024,512]{1,0:T(8,128)(2,1)S(1)}, bf16[1024,512]{1,0:T(8,128)(2,1)S(1)}) custom-call(bf16[1024,512]{1,0:T(8,128)(2,1)S(1)} %get-tuple-element.57.q_ref, bf16[1024,512]{1,0:T(8,128)(2,1)} %copy-done.18, bf16[1024,512]{1,0:T(8,128)(2,1)} %copy-done.19, bf16[1024,512]{1,0:T(8,128)(2,1)} %copy-done.8, ...), custom_call_target="tpu_custom_call" | custom-call | flops 5368709120 | bytes 8388608 | tf_op jit(solution)/shard_map/attend_backward/pallas_call | solution.py:167
  604.9 17.7 %collective-permute-done.44 = bf16[256,2048]{1,0:T(8,128)(2,1)S(1)} collective-permute-done((bf16[256,2048]{1,0:T(8,128)(2,1)}, bf16[256,2048]{1,0:T(8,128)(2,1)S(1)}, u32[]{:S(2)}, u32[]{:S(2)}) %collective-permute-start.44) | collective-permute-done | bytes 1048608 | tf_op jit(solution)/shard_map/ppermute | solution.py:268
  640.1 16.7 %collective-permute-done.36 = bf16[256,2048]{1,0:T(8,128)(2,1)S(1)} collective-permute-done((bf16[256,2048]{1,0:T(8,128)(2,1)}, bf16[256,2048]{1,0:T(8,128)(2,1)S(1)}, u32[]{:S(2)}, u32[]{:S(2)}) %collective-permute-start.36) | collective-permute-done | bytes 1048608 | tf_op jit(solution)/shard_map/ppermute | solution.py:268
  660.1 17.2 %collective-permute-done.45 = bf16[256,2048]{1,0:T(8,128)(2,1)S(1)} collective-permute-done((bf16[256,2048]{1,0:T(8,128)(2,1)S(1)}, bf16[256,2048]{1,0:T(8,128)(2,1)S(1)}, u32[]{:S(2)}, u32[]{:S(2)}) %collective-permute-start.45) | collective-permute-done | bytes 1048608 | tf_op jit(solution)/shard_map/ppermute | solution.py:268
  709.0 11.2 %collective-permute-done.46 = bf16[256,2048]{1,0:T(8,128)(2,1)} collective-permute-done((bf16[256,2048]{1,0:T(8,128)(2,1)S(1)}, bf16[256,2048]{1,0:T(8,128)(2,1)}, u32[]{:S(2)}, u32[]{:S(2)}) %collective-permute-start.46) | collective-permute-done | bytes 1048608 | tf_op jit(solution)/shard_map/ppermute | solution.py:268
  730.5 13.3 %collective-permute-done.47 = bf16[256,2048]{1,0:T(8,128)(2,1)S(1)} collective-permute-done((bf16[256,2048]{1,0:T(8,128)(2,1)}, bf16[256,2048]{1,0:T(8,128)(2,1)S(1)}, u32[]{:S(2)}, u32[]{:S(2)}) %collective-permute-start.47) | collective-permute-done | bytes 1048608 | tf_op jit(solution)/shard_map/ppermute | solution.py:268
  776.1 8.4 %collective-permute-done.69 = bf16[512,256]{0,1:T(8,128)(2,1)S(1)} collective-permute-done((bf16[512,256]{0,1:T(8,128)(2,1)S(1)}, bf16[512,256]{0,1:T(8,128)(2,1)S(1)}, u32[]{:S(2)}, u32[]{:S(2)}) %collective-permute-start.69) | collective-permute-done | bytes 262176 | tf_op jit(solution)/shard_map/ppermute | solution.py:268
  (475 shorter events, 415.3 us)
Async XLA Ops:
  52.6 38.3 %collective-permute-start.4 = (bf16[768,1536]{1,0:T(8,128)(2,1)S(1)}, bf16[768,1536]{1,0:T(8,128)(2,1)S(1)}, u32[]{:S(2)}, u32[]{:S(2)}) collective-permute-start(bf16[768,1536]{1,0:T(8,128)(2,1)S(1)} %pad_maximum_fusion.4), channel_id=1, source_target_pairs={{0,4},{4,0},{8,12},{12,8},{16,20},{20,16},{24,28},{28,24},{1,5},{5... | collective-permute-start | bytes 7077896 | tf_op jit(solution)/shard_map/ppermute | solution.py:263
  89.1 109.8 %collective-permute-start.14 = (bf16[768,2048]{1,0:T(8,128)(2,1)}, bf16[768,2048]{1,0:T(8,128)(2,1)}, u32[]{:S(2)}, u32[]{:S(2)}) collective-permute-start(bf16[768,2048]{1,0:T(8,128)(2,1)} %pad_maximum_fusion), channel_id=1, source_target_pairs={{0,4},{4,0},{8,12},{12,8},{16,20},{20,16},{24,28},{28,24},{1,5},{5... | collective-permute-start | bytes 9437192 | tf_op jit(solution)/shard_map/ppermute | solution.py:263
  100.4 44.7 %collective-permute-start.19 = (bf16[256,2048]{1,0:T(8,128)(2,1)}, bf16[256,2048]{1,0:T(8,128)(2,1)}, u32[]{:S(2)}, u32[]{:S(2)}) collective-permute-start(bf16[256,2048]{1,0:T(8,128)(2,1)} %collective-permute-done.17), channel_id=1, source_target_pairs={{0,16},{4,12},{8,24},{12,4},{16,0},{20,28},{24,8},{28,20},{1,17},{... | collective-permute-start | bytes 3145736 | tf_op jit(solution)/shard_map/ppermute | solution.py:273
  102.1 43.0 %collective-permute-start.18 = (bf16[256,2048]{1,0:T(8,128)(2,1)}, bf16[256,2048]{1,0:T(8,128)(2,1)}, u32[]{:S(2)}, u32[]{:S(2)}) collective-permute-start(bf16[256,2048]{1,0:T(8,128)(2,1)} %collective-permute-done.16), channel_id=1, source_target_pairs={{0,8},{4,20},{8,0},{12,28},{16,24},{20,4},{24,16},{28,12},{1,9},{5... | collective-permute-start | bytes 3145736 | tf_op jit(solution)/shard_map/ppermute | solution.py:273
  132.7 40.7 %collective-permute-start.5 = (bf16[1024,512]{1,0:T(8,128)(2,1)S(1)}, bf16[1024,512]{1,0:T(8,128)(2,1)}, u32[]{:S(2)}, u32[]{:S(2)}) collective-permute-start(bf16[1024,512]{1,0:T(8,128)(2,1)S(1)} %get-tuple-element.44.att_ref), channel_id=1, source_target_pairs={{0,1},{1,2},{2,3},{3,0},{4,5},{5,6},{6,7},{7,4},{8,9},{9,10},{10,1... | collective-permute-start | bytes 3145736 | tf_op jit(solution)/shard_map/ppermute | solution.py:268
  145.1 32.0 %collective-permute-start.22 = (bf16[256,2048]{1,0:T(8,128)(2,1)S(1)}, bf16[256,2048]{1,0:T(8,128)(2,1)}, u32[]{:S(2)}, u32[]{:S(2)}) collective-permute-start(bf16[256,2048]{1,0:T(8,128)(2,1)S(1)} %get-tuple-element.49), channel_id=1, source_target_pairs={{0,8},{4,20},{8,0},{12,28},{16,24},{20,4},{24,16},{28,12},{1,9},{5... | collective-permute-start | bytes 3145736 | tf_op jit(solution)/shard_map/ppermute | solution.py:273
  146.1 31.6 %collective-permute-start.21 = (bf16[256,2048]{1,0:T(8,128)(2,1)S(1)}, bf16[256,2048]{1,0:T(8,128)(2,1)}, u32[]{:S(2)}, u32[]{:S(2)}) collective-permute-start(bf16[256,2048]{1,0:T(8,128)(2,1)S(1)} %get-tuple-element.49), channel_id=1, source_target_pairs={{0,4},{4,0},{8,12},{12,8},{16,20},{20,16},{24,28},{28,24},{1,5},{5... | collective-permute-start | bytes 3145736 | tf_op jit(solution)/shard_map/ppermute | solution.py:263
  179.3 84.4 %collective-permute-start.20 = (bf16[768,2048]{1,0:T(8,128)(2,1)S(1)}, bf16[768,2048]{1,0:T(8,128)(2,1)}, u32[]{:S(2)}, u32[]{:S(2)}) collective-permute-start(bf16[768,2048]{1,0:T(8,128)(2,1)S(1)} %pad_maximum_fusion.1), channel_id=1, source_target_pairs={{0,4},{4,0},{8,12},{12,8},{16,20},{20,16},{24,28},{28,24},{1,5},{5... | collective-permute-start | bytes 9437192 | tf_op jit(solution)/shard_map/ppermute | solution.py:263
  202.9 30.8 %collective-permute-start.27 = (bf16[256,2048]{0,1:T(8,128)(2,1)S(1)}, bf16[256,2048]{0,1:T(8,128)(2,1)S(1)}, u32[]{:S(2)}, u32[]{:S(2)}) collective-permute-start(bf16[256,2048]{0,1:T(8,128)(2,1)S(1)} %bitcast.68), channel_id=1, source_target_pairs={{0,8},{4,20},{8,0},{12,28},{16,24},{20,4},{24,16},{28,12},{1,9},{5... | collective-permute-start | bytes 3145736 | tf_op jit(solution)/shard_map/ppermute | solution.py:273
  219.8 50.1 %collective-permute-start.25 = (bf16[768,2048]{1,0:T(8,128)(2,1)}, bf16[768,2048]{1,0:T(8,128)(2,1)}, u32[]{:S(2)}, u32[]{:S(2)}) collective-permute-start(bf16[768,2048]{1,0:T(8,128)(2,1)} %pad_maximum_fusion.2), channel_id=1, source_target_pairs={{0,4},{4,0},{8,12},{12,8},{16,20},{20,16},{24,28},{28,24},{1,5},{5... | collective-permute-start | bytes 9437192 | tf_op jit(solution)/shard_map/ppermute | solution.py:263
  341.1 37.8 %collective-permute-start.37 = (bf16[256,2048]{1,0:T(8,128)(2,1)S(1)}, bf16[256,2048]{1,0:T(8,128)(2,1)}, u32[]{:S(2)}, u32[]{:S(2)}) collective-permute-start(bf16[256,2048]{1,0:T(8,128)(2,1)S(1)} %fusion.18), channel_id=1, source_target_pairs={{0,1},{1,2},{2,3},{3,0},{4,5},{5,6},{6,7},{7,4},{8,9},{9,10},{10,1... | collective-permute-start | bytes 3145736 | tf_op jit(solution)/shard_map/ppermute | solution.py:268
  352.9 38.1 %collective-permute-start.31 = (bf16[256,2048]{1,0:T(8,128)(2,1)S(1)}, bf16[256,2048]{1,0:T(8,128)(2,1)S(1)}, u32[]{:S(2)}, u32[]{:S(2)}) collective-permute-start(bf16[256,2048]{1,0:T(8,128)(2,1)S(1)} %convolution_convert_fusion.7), channel_id=1, source_target_pairs={{0,1},{1,2},{2,3},{3,0},{4,5},{5,6},{6,7},{7,4},{8,9},{9,10},{10,1... | collective-permute-start | bytes 3145736 | tf_op jit(solution)/shard_map/ppermute | solution.py:268
  378.9 79.2 %collective-permute-start.71 = (bf16[768,2048]{1,0:T(8,128)(2,1)S(1)}, bf16[768,2048]{1,0:T(8,128)(2,1)}, u32[]{:S(2)}, u32[]{:S(2)}) collective-permute-start(bf16[768,2048]{1,0:T(8,128)(2,1)S(1)} %convolution_convert_fusion.4), channel_id=1, source_target_pairs={{0,4},{4,0},{8,12},{12,8},{16,20},{20,16},{24,28},{28,24},{1,5},{5... | collective-permute-start | bytes 9437192 | tf_op jit(solution)/shard_map/ppermute | solution.py:263
  398.0 39.4 %collective-permute-start.32 = (bf16[256,2048]{1,0:T(8,128)(2,1)}, bf16[256,2048]{1,0:T(8,128)(2,1)}, u32[]{:S(2)}, u32[]{:S(2)}) collective-permute-start(bf16[256,2048]{1,0:T(8,128)(2,1)} %add_convert_fusion.6), channel_id=1, source_target_pairs={{0,1},{1,2},{2,3},{3,0},{4,5},{5,6},{6,7},{7,4},{8,9},{9,10},{10,1... | collective-permute-start | bytes 3145736 | tf_op jit(solution)/shard_map/ppermute | solution.py:268
  411.9 146.2 %collective-permute-start.53 = (bf16[768,2048]{1,0:T(8,128)(2,1)}, bf16[768,2048]{1,0:T(8,128)(2,1)}, u32[]{:S(2)}, u32[]{:S(2)}) collective-permute-start(bf16[768,2048]{1,0:T(8,128)(2,1)} %convolution_convert_fusion.3), channel_id=1, source_target_pairs={{0,4},{4,0},{8,12},{12,8},{16,20},{20,16},{24,28},{28,24},{1,5},{5... | collective-permute-start | bytes 9437192 | tf_op jit(solution)/shard_map/ppermute | solution.py:263
  421.9 45.0 %collective-permute-start.39 = (bf16[256,2048]{1,0:T(8,128)(2,1)S(1)}, bf16[256,2048]{1,0:T(8,128)(2,1)S(1)}, u32[]{:S(2)}, u32[]{:S(2)}) collective-permute-start(bf16[256,2048]{1,0:T(8,128)(2,1)S(1)} %add_convert_fusion.2), channel_id=1, source_target_pairs={{0,1},{1,2},{2,3},{3,0},{4,5},{5,6},{6,7},{7,4},{8,9},{9,10},{10,1... | collective-permute-start | bytes 3145736 | tf_op jit(solution)/shard_map/ppermute | solution.py:268
  444.6 42.0 %collective-permute-start.33 = (bf16[256,2048]{1,0:T(8,128)(2,1)}, bf16[256,2048]{1,0:T(8,128)(2,1)}, u32[]{:S(2)}, u32[]{:S(2)}) collective-permute-start(bf16[256,2048]{1,0:T(8,128)(2,1)} %add_convert_fusion.5), channel_id=1, source_target_pairs={{0,1},{1,2},{2,3},{3,0},{4,5},{5,6},{6,7},{7,4},{8,9},{9,10},{10,1... | collective-permute-start | bytes 3145736 | tf_op jit(solution)/shard_map/ppermute | solution.py:268
  449.7 138.0 %collective-permute-start.57 = (bf16[768,2048]{1,0:T(8,128)(2,1)}, bf16[768,2048]{1,0:T(8,128)(2,1)}, u32[]{:S(2)}, u32[]{:S(2)}) collective-permute-start(bf16[768,2048]{1,0:T(8,128)(2,1)} %convolution_convert_fusion.2), channel_id=1, source_target_pairs={{0,4},{4,0},{8,12},{12,8},{16,20},{20,16},{24,28},{28,24},{1,5},{5... | collective-permute-start | bytes 9437192 | tf_op jit(solution)/shard_map/ppermute | solution.py:263
  482.3 30.3 %collective-permute-start.42 = (bf16[256,512]{1,0:T(8,128)(2,1)S(1)}, bf16[256,512]{1,0:T(8,128)(2,1)}, u32[]{:S(2)}, u32[]{:S(2)}) collective-permute-start(bf16[256,512]{1,0:T(8,128)(2,1)S(1)} %get-tuple-element.146), channel_id=1, source_target_pairs={{0,1},{1,2},{2,3},{3,0},{4,5},{5,6},{6,7},{7,4},{8,9},{9,10},{10,1... | collective-permute-start | bytes 786440 | tf_op jit(solution)/shard_map/ppermute | solution.py:268
  502.3 50.9 %collective-permute-start.72 = (bf16[256,2048]{1,0:T(8,128)(2,1)}, bf16[256,2048]{1,0:T(8,128)(2,1)}, u32[]{:S(2)}, u32[]{:S(2)}) collective-permute-start(bf16[256,2048]{1,0:T(8,128)(2,1)} %fusion.29), channel_id=1, source_target_pairs={{0,16},{4,12},{8,24},{12,4},{16,0},{20,28},{24,8},{28,20},{1,17},{... | collective-permute-start | bytes 3145736 | tf_op jit(solution)/shard_map/ppermute | solution.py:273
  504.5 60.1 %collective-permute-start.34 = (bf16[256,2048]{1,0:T(8,128)(2,1)S(1)}, bf16[256,2048]{1,0:T(8,128)(2,1)}, u32[]{:S(2)}, u32[]{:S(2)}) collective-permute-start(bf16[256,2048]{1,0:T(8,128)(2,1)S(1)} %copy-done.26), channel_id=1, source_target_pairs={{0,1},{1,2},{2,3},{3,0},{4,5},{5,6},{6,7},{7,4},{8,9},{9,10},{10,1... | collective-permute-start | bytes 3145736 | tf_op jit(solution)/shard_map/ppermute | solution.py:268
  553.2 75.4 %collective-permute-start.49 = (bf16[768,1536]{1,0:T(8,128)(2,1)}, bf16[768,1536]{1,0:T(8,128)(2,1)}, u32[]{:S(2)}, u32[]{:S(2)}) collective-permute-start(bf16[768,1536]{1,0:T(8,128)(2,1)} %convolution_convert_fusion), channel_id=1, source_target_pairs={{0,4},{4,0},{8,12},{12,8},{16,20},{20,16},{24,28},{28,24},{1,5},{5... | collective-permute-start | bytes 7077896 | tf_op jit(solution)/shard_map/ppermute | solution.py:263
  558.1 73.9 %collective-permute-start.73 = (bf16[512,2048]{1,0:T(8,128)(2,1)}, bf16[512,2048]{1,0:T(8,128)(2,1)}, u32[]{:S(2)}, u32[]{:S(2)}) collective-permute-start(bf16[512,2048]{1,0:T(8,128)(2,1)} %pad_maximum_fusion.8), channel_id=1, source_target_pairs={{0,8},{4,20},{8,0},{12,28},{16,24},{20,4},{24,16},{28,12},{1,9},{5... | collective-permute-start | bytes 6291464 | tf_op jit(solution)/shard_map/ppermute | solution.py:273
  587.8 34.8 %collective-permute-start.44 = (bf16[256,2048]{1,0:T(8,128)(2,1)}, bf16[256,2048]{1,0:T(8,128)(2,1)S(1)}, u32[]{:S(2)}, u32[]{:S(2)}) collective-permute-start(bf16[256,2048]{1,0:T(8,128)(2,1)} %add_convert_fusion.1), channel_id=1, source_target_pairs={{0,1},{1,2},{2,3},{3,0},{4,5},{5,6},{6,7},{7,4},{8,9},{9,10},{10,1... | collective-permute-start | bytes 3145736 | tf_op jit(solution)/shard_map/ppermute | solution.py:268
  591.0 109.9 %collective-permute-start.64 = (bf16[768,2048]{1,0:T(8,128)(2,1)}, bf16[768,2048]{1,0:T(8,128)(2,1)}, u32[]{:S(2)}, u32[]{:S(2)}) collective-permute-start(bf16[768,2048]{1,0:T(8,128)(2,1)} %convolution_convert_fusion.1), channel_id=1, source_target_pairs={{0,4},{4,0},{8,12},{12,8},{16,20},{20,16},{24,28},{28,24},{1,5},{5... | collective-permute-start | bytes 9437192 | tf_op jit(solution)/shard_map/ppermute | solution.py:263
  601.5 101.6 %collective-permute-start.55 = (bf16[512,2048]{1,0:T(8,128)(2,1)}, bf16[512,2048]{1,0:T(8,128)(2,1)}, u32[]{:S(2)}, u32[]{:S(2)}) collective-permute-start(bf16[512,2048]{1,0:T(8,128)(2,1)} %pad_maximum_fusion.5), channel_id=1, source_target_pairs={{0,8},{4,20},{8,0},{12,28},{16,24},{20,4},{24,16},{28,12},{1,9},{5... | collective-permute-start | bytes 6291464 | tf_op jit(solution)/shard_map/ppermute | solution.py:273
  632.0 45.3 %collective-permute-start.45 = (bf16[256,2048]{1,0:T(8,128)(2,1)S(1)}, bf16[256,2048]{1,0:T(8,128)(2,1)S(1)}, u32[]{:S(2)}, u32[]{:S(2)}) collective-permute-start(bf16[256,2048]{1,0:T(8,128)(2,1)S(1)} %add_convert_fusion), channel_id=1, source_target_pairs={{0,1},{1,2},{2,3},{3,0},{4,5},{5,6},{6,7},{7,4},{8,9},{9,10},{10,1... | collective-permute-start | bytes 3145736 | tf_op jit(solution)/shard_map/ppermute | solution.py:268
  656.8 38.7 %collective-permute-start.74 = (bf16[256,2048]{1,0:T(8,128)(2,1)}, bf16[256,2048]{1,0:T(8,128)(2,1)S(1)}, u32[]{:S(2)}, u32[]{:S(2)}) collective-permute-start(bf16[256,2048]{1,0:T(8,128)(2,1)} %fusion.28), channel_id=1, source_target_pairs={{0,4},{4,0},{8,12},{12,8},{16,20},{20,16},{24,28},{28,24},{1,5},{5... | collective-permute-start | bytes 3145736 | tf_op jit(solution)/shard_map/ppermute | solution.py:263
  657.9 69.9 %collective-permute-start.59 = (bf16[512,2048]{1,0:T(8,128)(2,1)}, bf16[512,2048]{1,0:T(8,128)(2,1)}, u32[]{:S(2)}, u32[]{:S(2)}) collective-permute-start(bf16[512,2048]{1,0:T(8,128)(2,1)} %pad_maximum_fusion.6), channel_id=1, source_target_pairs={{0,8},{4,20},{8,0},{12,28},{16,24},{20,4},{24,16},{28,12},{1,9},{5... | collective-permute-start | bytes 6291464 | tf_op jit(solution)/shard_map/ppermute | solution.py:273
  677.3 48.6 %collective-permute-start.51 = (bf16[512,1536]{1,0:T(8,128)(2,1)}, bf16[512,1536]{1,0:T(8,128)(2,1)}, u32[]{:S(2)}, u32[]{:S(2)}) collective-permute-start(bf16[512,1536]{1,0:T(8,128)(2,1)} %pad_maximum_fusion.9), channel_id=1, source_target_pairs={{0,8},{4,20},{8,0},{12,28},{16,24},{20,4},{24,16},{28,12},{1,9},{5... | collective-permute-start | bytes 4718600 | tf_op jit(solution)/shard_map/ppermute | solution.py:273
  705.3 46.1 %collective-permute-start.56 = (bf16[256,2048]{1,0:T(8,128)(2,1)S(1)}, bf16[256,2048]{1,0:T(8,128)(2,1)S(1)}, u32[]{:S(2)}, u32[]{:S(2)}) collective-permute-start(bf16[256,2048]{1,0:T(8,128)(2,1)S(1)} %fusion.42), channel_id=1, source_target_pairs={{0,4},{4,0},{8,12},{12,8},{16,20},{20,16},{24,28},{28,24},{1,5},{5... | collective-permute-start | bytes 3145736 | tf_op jit(solution)/shard_map/ppermute | solution.py:263
  743.8 40.8 %collective-permute-start.48 = (bf16[256,2048]{1,0:T(8,128)(2,1)S(1)}, bf16[256,2048]{1,0:T(8,128)(2,1)}, u32[]{:S(2)}, u32[]{:S(2)}) collective-permute-start(bf16[256,2048]{1,0:T(8,128)(2,1)S(1)} %collective-permute-done.47), channel_id=1, source_target_pairs={{0,1},{1,2},{2,3},{3,0},{4,5},{5,6},{6,7},{7,4},{8,9},{9,10},{10,1... | collective-permute-start | bytes 3145736 | tf_op jit(solution)/shard_map/ppermute | solution.py:268
  (131 other events, 2058.9 us)

commit v2 on v1

v2 whole, which is shorter than its diff:
```python
import jax
import jax.numpy as jnp
import numpy as np
from jax import lax
from jax.experimental import pallas as pl
from jax.experimental.pallas import tpu as pltpu
from jax.sharding import PartitionSpec as P

HEAD_DIM = 64
BLOCK = 256
LANES = 128
norm_epsilon = 1e-05
rope_theta = 130000.0
clip_tau = 2.0
neg_big = -1e30
f32 = jnp.float32
bf16 = jnp.bfloat16


def mm(a, b):
    return lax.dot_general(a, b, (((1,), (0,)), ((), ())), preferred_element_type=f32)


def mm_nt(a, b):
    return lax.dot_general(a, b, (((1,), (1,)), ((), ())), preferred_element_type=f32)


def mm_tn(a, b):
    return lax.dot_general(a, b, (((0,), (0,)), ((), ())), preferred_element_type=f32)


def rope_tables(length):
    half_dim = HEAD_DIM // 2
    inverse = rope_theta ** (-(2.0 * np.arange(half_dim)) / HEAD_DIM)
    angles = np.tile(np.arange(length)[:, None] * inverse[None, :], (1, LANES // half_dim))
    return jnp.asarray(np.cos(angles), f32), jnp.asarray(np.sin(angles), f32)


def first_half(shape):
    return lax.broadcasted_iota(jnp.int32, shape, 1) % HEAD_DIM < HEAD_DIM // 2


def rotate(values, cosine, sine):
    ahead = pltpu.roll(values, LANES - HEAD_DIM // 2, 1)
    behind = pltpu.roll(values, HEAD_DIM // 2, 1)
    return values * cosine + jnp.where(first_half(values.shape), -ahead, behind) * sine


def unrotate(grads, cosine, sine):
    sined = grads * sine
    ahead = pltpu.roll(sined, LANES - HEAD_DIM // 2, 1)
    behind = pltpu.roll(sined, HEAD_DIM // 2, 1)
    return grads * cosine + jnp.where(first_half(grads.shape), ahead, -behind)


def of_head(values, head):
    lane = lax.broadcasted_iota(jnp.int32, values.shape, 1)
    return jnp.where(lane // HEAD_DIM == head, values, jnp.zeros_like(values))


def hide(scores, ends, start):
    tail = scores[start:]
    key = lax.broadcasted_iota(jnp.int32, tail.shape, 0) + start
    tail = jnp.where(key < ends, tail, neg_big)
    return jnp.concatenate([scores[:start], tail], 0) if start else tail


def fold(combine, values):
    while values.shape[0] % 16 == 0:
        near = values.shape[0] // 2
        values = combine(values[:near], values[near:])
    return values


def forward_kernel(
    q_ref, k_ref, v_ref, cos_ref, sin_ref, end_ref, qo_ref, ko_ref, vo_ref, att_ref, stat_ref
):
    length = q_ref.shape[0]
    cosine, sine = cos_ref[...], sin_ref[...]
    qo_ref[...] = (rotate(q_ref[...], cosine, sine).astype(bf16) * HEAD_DIM ** (-0.5)).astype(bf16)
    ko_ref[...] = rotate(k_ref[...], cosine, sine).astype(bf16)
    values = v_ref[...].astype(bf16)
    vo_ref[...] = values
    lane = lax.broadcasted_iota(jnp.int32, values.shape, 1)
    sides = [jnp.where(lane // HEAD_DIM == head, values, jnp.ones_like(values)) for head in range(2)]
    for start in range(0, length, BLOCK):
        keys = min(length, start + 2 * BLOCK)
        here = slice(start, start + BLOCK)
        tile, ends = qo_ref[here, :], end_ref[:, here]
        mixed = []
        for head in range(2):
            scores = hide(mm_nt(ko_ref[:keys, :], of_head(tile, head)), ends, start)
            peak = jnp.max(fold(jnp.maximum, scores), 0, keepdims=True)
            expo = jnp.exp(scores - peak).astype(bf16)
            product = mm_tn(expo, sides[head][:keys])
            mixed.append(product / pltpu.roll(product, HEAD_DIM, 1))
            row = HEAD_DIM * (1 - head)
            total = jnp.transpose(product)[row : row + 1]
            stat_ref[0, head : head + 1, here] = peak + jnp.log(total)
            stat_ref[0, 2 + head : 3 + head, here] = peak
        att_ref[here, :] = jnp.where(lane[:BLOCK] < HEAD_DIM, mixed[0], mixed[1]).astype(bf16)


def backward_kernel(
    q_ref, k_ref, v_ref, att_ref, da_ref, stat_ref, cos_ref, sin_ref, end_ref, dq_ref, dk_ref, dv_ref, dk_sum, dv_sum
):
    length = q_ref.shape[0]
    turned = jnp.transpose(k_ref[...].astype(f32)).astype(bf16)
    dk_sum[...] = jnp.zeros_like(dk_sum)
    dv_sum[...] = jnp.zeros_like(dv_sum)
    for start in range(0, length, BLOCK):
        keys = min(length, start + 2 * BLOCK)
        here = slice(start, start + BLOCK)
        tile, d_tile = q_ref[here, :], da_ref[here, :]
        ends = end_ref[:, here]
        both = jnp.transpose(att_ref[here, :].astype(f32) * d_tile.astype(f32))
        d_mixed, probs_both, ds_both, tiles, d_tiles = [], [], [], [], []
        for head in range(2):
            tile_head, d_head = of_head(tile, head), of_head(d_tile, head)
            span = slice(head * HEAD_DIM, (head + 1) * HEAD_DIM)
            center = jnp.sum(both[span, :], 0, keepdims=True)
            scores = hide(mm_nt(k_ref[:keys, :], tile_head), ends, start)
            probs = jnp.exp(scores - stat_ref[0, head : head + 1, here])
            d_probs = mm_nt(v_ref[:keys, :], d_head)
            d_scores = (probs * (d_probs - center)).astype(bf16)
            d_mixed.append(mm(turned[span, :keys], d_scores))
            probs_both.append(probs.astype(bf16))
            ds_both.append(d_scores)
            tiles.append(tile_head)
            d_tiles.append(d_head)
        dv_sum[:keys, :] += mm(jnp.concatenate(probs_both, 1), jnp.concatenate(d_tiles, 0))
        dk_sum[:keys, :] += mm(jnp.concatenate(ds_both, 1), jnp.concatenate(tiles, 0))
        d_queries = jnp.transpose(jnp.concatenate(d_mixed, 0)) * HEAD_DIM ** (-0.5)
        dq_ref[here, :] = unrotate(d_queries, cos_ref[here, :], sin_ref[here, :]).astype(bf16)
    dk_ref[...] = unrotate(dk_sum[...], cos_ref[...], sin_ref[...]).astype(bf16)
    dv_ref[...] = dv_sum[...].astype(bf16)


def last_visible(block_row):
    return jnp.sum(block_row[:, None] <= block_row[None, :], 0, dtype=jnp.int32)[None]


def attend_forward(qkv, ends, cosine, sine):
    length, columns = qkv.shape[0], qkv.shape[1] // 3
    pairs = columns // LANES
    spec = lambda base: pl.BlockSpec((length, LANES), lambda p: (0, base + p))
    fixed = lambda shape: pl.BlockSpec(shape, lambda p: (0, 0))
    whole = jax.ShapeDtypeStruct((length, columns), bf16)
    return pl.pallas_call(
        forward_kernel,
        grid=(pairs,),
        in_specs=[spec(0), spec(pairs), spec(2 * pairs)] + [fixed((length, LANES))] * 2 + [fixed((1, length))],
        out_specs=[spec(0)] * 4 + [pl.BlockSpec((1, 8, length), lambda p: (p, 0, 0))],
        out_shape=[whole] * 4 + [jax.ShapeDtypeStruct((pairs, 8, length), f32)],
        compiler_params=pltpu.CompilerParams(vmem_limit_bytes=48 * 2**20),
        cost_estimate=pl.CostEstimate(flops=4 * length * length * columns, bytes_accessed=10 * length * columns * 2, transcendentals=length * length * columns // HEAD_DIM),
        name="attend_forward",
    )(qkv, qkv, qkv, cosine, sine, ends)


def attend_backward(queries, keys, values, attended, d_attended, stats, ends, cosine, sine):
    length, columns = queries.shape
    pairs = columns // LANES
    spec = pl.BlockSpec((length, LANES), lambda p: (0, p))
    fixed = lambda shape: pl.BlockSpec(shape, lambda p: (0, 0))
    whole = jax.ShapeDtypeStruct((length, columns), bf16)
    return pl.pallas_call(
        backward_kernel,
        grid=(pairs,),
        in_specs=[spec] * 5 + [pl.BlockSpec((1, 8, length), lambda p: (p, 0, 0))] + [fixed((length, LANES))] * 2 + [fixed((1, length))],
        out_specs=[spec] * 3,
        out_shape=[whole] * 3,
        scratch_shapes=[pltpu.VMEM((length, LANES), f32)] * 2,
        compiler_params=pltpu.CompilerParams(vmem_limit_bytes=48 * 2**20),
        cost_estimate=BESIDE,
        name="attend_backward",
    )(queries, keys, values, attended, d_attended, stats, cosine, sine, ends)


def norm_kernel(order_ref, value_ref, hat_ref, same_ref, true_ref, *, count):
    values = value_ref[...].astype(f32)
    block = value_ref.shape[1] // count
    inverse = lax.rsqrt(jnp.mean(values * values, -1, keepdims=True) + norm_epsilon)
    true_ref[...] = (values * inverse).astype(bf16)
    for place in range(count):
        source = pl.ds(pl.multiple_of(order_ref[place] * block, block), block)
        target = slice(place * block, (place + 1) * block)
        same_ref[:, target] = value_ref[:, source]
        hat_ref[:, target] = true_ref[:, source]


def normed_in_order(values, order):
    rows, width = values.shape
    spec = pl.BlockSpec((BLOCK, width), lambda i, order: (i, 0))
    return pl.pallas_call(
        lambda *refs: norm_kernel(*refs, count=order.shape[0]),
        grid_spec=pltpu.PrefetchScalarGridSpec(
            num_scalar_prefetch=1, grid=(rows // BLOCK,), in_specs=[spec], out_specs=[spec] * 3
        ),
        out_shape=[jax.ShapeDtypeStruct(values.shape, bf16)] * 3,
        compiler_params=pltpu.CompilerParams(vmem_limit_bytes=32 * 2**20),
        name="norm_in_order",
    )(order, values)


def move_kernel(order_ref, value_ref, out_ref, *, count):
    block = value_ref.shape[1] // count
    for place in range(count):
        source = pl.ds(pl.multiple_of(order_ref[place] * block, block), block)
        out_ref[:, place * block : (place + 1) * block] = value_ref[:, source]


def in_order(values, order):
    rows, width = values.shape
    spec = pl.BlockSpec((min(rows, BLOCK), width), lambda i, order: (i, 0))
    return pl.pallas_call(
        lambda *refs: move_kernel(*refs, count=order.shape[0]),
        grid_spec=pltpu.PrefetchScalarGridSpec(
            num_scalar_prefetch=1, grid=(rows // min(rows, BLOCK),), in_specs=[spec], out_specs=spec
        ),
        out_shape=jax.ShapeDtypeStruct(values.shape, values.dtype),
        name="in_order",
    )(order, values)


def resid_kernel(place_ref, order_ref, part_ref, left_ref, right_ref, resid_ref, hat_ref, true_ref, *, count):
    resid = part_ref[...] + mm_nt(left_ref[...], right_ref[...])
    block = resid.shape[1] // count
    inverse = lax.rsqrt(jnp.mean(resid * resid, -1, keepdims=True) + norm_epsilon)
    hat_ref[...] = (resid * inverse).astype(bf16)
    for place in range(count):
        source = pl.ds(pl.multiple_of(order_ref[place] * block, block), block)
        true_ref[:, place * block : (place + 1) * block] = hat_ref[:, source]

    @pl.when(pl.program_id(0) == place_ref[0])
    def _():
        resid_ref[...] = resid


def resid_and_norm(part, left, right, place, order, rows):
    tokens, width = part.shape
    spec = pl.BlockSpec((rows, width), lambda i, place, order: (i, 0))
    return pl.pallas_call(
        lambda *refs: resid_kernel(*refs, count=order.shape[0]),
        grid_spec=pltpu.PrefetchScalarGridSpec(
            num_scalar_prefetch=2,
            grid=(tokens // rows,),
            in_specs=[
                spec,
                pl.BlockSpec((rows, left.shape[1]), lambda i, place, order: (i, 0)),
                pl.BlockSpec(right.shape, lambda i, place, order: (0, 0)),
            ],
            out_specs=[pl.BlockSpec((rows, width), lambda i, place, order: (0, 0)), spec, spec],
        ),
        out_shape=[
            jax.ShapeDtypeStruct((rows, width), f32),
            jax.ShapeDtypeStruct(part.shape, bf16),
            jax.ShapeDtypeStruct(part.shape, bf16),
        ],
        compiler_params=pltpu.CompilerParams(vmem_limit_bytes=40 * 2**20),
        cost_estimate=pl.CostEstimate(
            flops=2 * tokens * width * left.shape[1], bytes_accessed=10 * tokens * width, transcendentals=0
        ),
        name="resid_and_norm",
    )(place.reshape(1), order, part, left, right)


def stack_kernel(*refs, groups):
    *refs, held, arrived, left = refs
    pieces, wholes = refs[:-groups], refs[-groups:]
    inward, outward = [], []
    start = 0
    for index, piece in enumerate(pieces):
        rows = piece.shape[0] // groups
        inward.append(
            pltpu.make_async_copy(piece, held.at[pl.ds(groups * start, groups * rows)], arrived.at[index])
        )
        outward.append(
            [
                pltpu.make_async_copy(
                    held.at[pl.ds(groups * start + group * rows, rows)],
                    whole.at[pl.ds(start, rows)],
                    left.at[index, group],
                )
                for group, whole in enumerate(wholes)
            ]
        )
        start += rows
    for copy in inward:
        copy.start()
    for one, several in zip(inward, outward):
        one.wait()
        for copy in several:
            copy.start()
    for several in outward:
        for copy in several:
            copy.wait()


def stack(pieces, groups):
    rows, width = sum(piece.shape[0] for piece in pieces), pieces[0].shape[1]
    dtype = pieces[0].dtype
    anywhere = pl.BlockSpec(memory_space=pl.ANY)
    return pl.pallas_call(
        lambda *refs: stack_kernel(*refs, groups=groups),
        in_specs=[anywhere] * len(pieces),
        out_specs=[anywhere] * groups,
        out_shape=[jax.ShapeDtypeStruct((rows // groups, width), dtype)] * groups,
        scratch_shapes=[
            pltpu.VMEM((rows, width), dtype),
            pltpu.SemaphoreType.DMA((len(pieces),)),
            pltpu.SemaphoreType.DMA((len(pieces), groups)),
        ],
        compiler_params=pltpu.CompilerParams(vmem_limit_bytes=32 * 2**20),
        cost_estimate=pl.CostEstimate(flops=0, bytes_accessed=rows * width // 8, transcendentals=0),
        name="stack",
    )(*pieces)


BESIDE = pl.CostEstimate(flops=4 * 2**30, bytes_accessed=2**20, transcendentals=0)


def grad_kernel(left_ref, right_ref, *refs, far):
    near_ref, far_ref = refs[-2:]
    product = mm_tn(left_ref[...], right_ref[...]).astype(bf16)

    @pl.when(pl.program_id(0) < far)
    def _():
        far_ref[...] = product

    @pl.when(pl.program_id(0) >= far)
    def _():
        near_ref[...] = product


def grad_beside(left, right, share, which, groups, into):
    (depth, rows), columns = left.shape, right.shape[1]
    near, far = share[0], share[1] - share[0]
    tile = rows // share[1]
    anywhere = pl.BlockSpec(memory_space=pl.ANY)
    return pl.pallas_call(
        lambda *refs: grad_kernel(*refs, far=far),
        grid=(near + far,),
        in_specs=[
            pl.BlockSpec((depth, tile), lambda i: (0, jnp.where(i < far, near + i, i - far))),
            pl.BlockSpec(right.shape, lambda i: (0, 0)),
        ]
        + [anywhere] * len(into),
        out_specs=[
            pl.BlockSpec((tile, columns), lambda i: (jnp.maximum(i - far, 0) * groups + which, 0)),
            pl.BlockSpec((tile, columns), lambda i: (jnp.minimum(i, far - 1) * groups + which, 0)),
        ],
        out_shape=[
            jax.ShapeDtypeStruct((near * groups * tile, columns), bf16),
            jax.ShapeDtypeStruct((far * groups * tile, columns), bf16),
        ],
        input_output_aliases={2 + k: k for k in range(len(into))},
        compiler_params=pltpu.CompilerParams(vmem_limit_bytes=56 * 2**20),
        cost_estimate=BESIDE,
        name="grad_beside",
    )(left, right, *into)


def tn_kernel(left_ref, right_ref, out_ref):
    out_ref[...] = mm_tn(left_ref[...], right_ref[...]).astype(bf16)


def plain_beside(left, right):
    (depth, rows), columns = left.shape, right.shape[1]
    tile = 2 * BLOCK
    return pl.pallas_call(
        tn_kernel,
        grid=(rows // tile,),
        in_specs=[
            pl.BlockSpec((depth, tile), lambda i: (0, i)),
            pl.BlockSpec(right.shape, lambda i: (0, 0)),
        ],
        out_specs=pl.BlockSpec((tile, columns), lambda i: (i, 0)),
        out_shape=jax.ShapeDtypeStruct((rows, columns), bf16),
        compiler_params=pltpu.CompilerParams(vmem_limit_bytes=56 * 2**20),
        cost_estimate=BESIDE,
        name="plain_beside",
    )(left, right)


def nt_kernel(left_ref, right_ref, out_ref):
    out_ref[...] = mm_nt(left_ref[...], right_ref[...]).astype(bf16)


def product_beside(left, right):
    (rows, depth), columns = left.shape, right.shape[0]
    tile = 2 * BLOCK
    return pl.pallas_call(
        nt_kernel,
        grid=(columns // tile,),
        in_specs=[
            pl.BlockSpec(left.shape, lambda i: (0, 0)),
            pl.BlockSpec((tile, depth), lambda i: (i, 0)),
        ],
        out_specs=pl.BlockSpec((rows, tile), lambda i: (0, i)),
        out_shape=jax.ShapeDtypeStruct((rows, columns), bf16),
        compiler_params=pltpu.CompilerParams(vmem_limit_bytes=56 * 2**20),
        cost_estimate=BESIDE,
        name="product_beside",
    )(left, right)


def mid_kernel(hat_ref, up_ref, gate_ref, dh_ref, hidden_ref, dg_ref, du_ref):
    up = mm(hat_ref[...], up_ref[...])
    gate, d_hidden = gate_ref[...], dh_ref[...]
    sigma = 1.0 / (1.0 + jnp.exp(-gate))
    swish = gate * sigma
    hidden_ref[...] = (swish * up).astype(bf16)
    dg_ref[...] = (d_hidden * up * (sigma + swish * (1.0 - sigma))).astype(bf16)
    du_ref[...] = (d_hidden * swish).astype(bf16)


def mid_layer(hat, up_weight, gate, d_hidden):
    (rows, depth), columns = hat.shape, up_weight.shape[1]
    tile = min(2 * BLOCK, columns)
    spec = pl.BlockSpec((rows, tile), lambda i: (0, i))
    return pl.pallas_call(
        mid_kernel,
        grid=(columns // tile,),
        in_specs=[
            pl.BlockSpec(hat.shape, lambda i: (0, 0)),
            pl.BlockSpec((depth, tile), lambda i: (0, i)),
            spec,
            spec,
        ],
        out_specs=[spec] * 3,
        out_shape=[jax.ShapeDtypeStruct((rows, columns), bf16)] * 3,
        compiler_params=pltpu.CompilerParams(vmem_limit_bytes=56 * 2**20),
        cost_estimate=pl.CostEstimate(
            flops=2 * rows * depth * columns, bytes_accessed=20 * rows * columns, transcendentals=rows * columns
        ),
        name="mid_layer",
    )(hat, up_weight, gate, d_hidden)


def pair_kernel(a_ref, b_ref, c_ref, d_ref, out_ref):
    out_ref[...] = (mm_nt(a_ref[...], b_ref[...]) + mm_nt(c_ref[...], d_ref[...])).astype(bf16)


def pair_product(a, b, c, d):
    (rows, depth), columns = a.shape, b.shape[0]
    tile = 2 * BLOCK
    whole = pl.BlockSpec(a.shape, lambda i: (0, 0))
    part = pl.BlockSpec((tile, depth), lambda i: (i, 0))
    return pl.pallas_call(
        pair_kernel,
        grid=(columns // tile,),
        in_specs=[whole, part, whole, part],
        out_specs=pl.BlockSpec((rows, tile), lambda i: (0, i)),
        out_shape=jax.ShapeDtypeStruct((rows, columns), bf16),
        compiler_params=pltpu.CompilerParams(vmem_limit_bytes=56 * 2**20),
        cost_estimate=pl.CostEstimate(
            flops=4 * rows * depth * columns, bytes_accessed=12 * rows * columns, transcendentals=0
        ),
        name="pair_product",
    )(a, b, c, d)


def after(value, *others):
    return lax.optimization_barrier((value, *others))[0]


def flip(value, mask):
    count = lax.axis_size("dp")
    return lax.ppermute(value, "dp", [(i, i ^ mask) for i in range(count)])


def shift(value, step):
    count = lax.axis_size("tensor")
    return lax.ppermute(value, "tensor", [(i, (i + step) % count) for i in range(count)])


def cross(value, forward):
    masks = (2, 4) if forward else (4, 2)
    return lax.ppermute(value, "dp", [(i, i ^ masks[i % 2]) for i in range(8)])


def gather_order(here, count):
    if count != 8:
        return here ^ jnp.arange(count, dtype=jnp.int32)
    first = jnp.where(here % 2 == 0, 2, 4)
    masks = [0, 1, first, first ^ 1, 6, 7 ^ first, 6 ^ first, 7]
    return here ^ jnp.stack([jnp.asarray(mask, jnp.int32) for mask in masks])


class Order:
    def __init__(self):
        self.last = ()

    def run(self, work, *inputs):
        inputs, _ = lax.optimization_barrier((inputs, self.last))
        result = work(*inputs)
        self.last = jax.tree.leaves(result)
        return result

    def wait(self, *moving):
        moving, _ = lax.optimization_barrier((moving, self.last))
        self.last = jax.tree.leaves(moving)
        return moving if len(moving) > 1 else moving[0]


def double(own):
    bit = 1
    while bit < lax.axis_size("dp"):
        own = jnp.concatenate([own, flip(own, bit)], 0)
        bit *= 2
    return own


class Gather:
    def __init__(self, order, own):
        self.order, self.own, self.count = order, own, lax.axis_size("dp")

    def pair(self):
        if self.count == 8:
            self.beside = flip(self.own, 1)

    def begin(self, own_too=True):
        if self.count == 8:
            if own_too:
                self.own, self.beside = self.order.wait(self.own, self.beside)
                self.first = cross(self.own, True)
            else:
                self.beside = self.order.wait(self.beside)
            self.second = cross(self.beside, True)

    def early(self):
        if self.count == 8:
            self.first = cross(self.own, True)

    def middle(self, with_second=False):
        if self.count == 8:
            if with_second:
                self.first, self.second = self.order.wait(self.first, self.second)
            else:
                self.first = self.order.wait(self.first)
            self.third = cross(self.first, False)

    def late(self):
        if self.count == 8:
            self.second, self.third = self.order.wait(self.second, self.third)
            self.flipped = [flip(piece, 1) for piece in (self.first, self.second, self.third)]

    def end(self, groups=1):
        if self.count == 8:
            flipped = self.order.wait(*self.flipped)
            pieces = (self.own, self.beside, self.first, self.second, self.third, *flipped)
            whole = self.order.run(lambda *pieces: stack(pieces, groups), *pieces)
            return whole if groups > 1 else whole[0]
        return double(self.own)


class Ring:
    def __init__(self, order, terms, owner_part):
        self.order, self.count = order, lax.axis_size("tensor")
        self.terms, self.part, self.stage = terms, owner_part, 1
        sent = order.run(lambda terms: self.part(terms, 1), terms)
        self.moving = shift(sent, 1)

    def step(self):
        if self.stage == self.count:
            return
        self.stage += 1
        arrived = self.arrived = self.order.wait(self.moving)

        def add(arrived, terms):
            total = arrived.astype(f32) + self.part(terms, self.stage % self.count).astype(f32)
            return total.astype(bf16) if self.stage < self.count else total

        total = self.order.run(add, arrived, self.terms)
        if self.stage < self.count:
            self.moving = shift(total, 1)
        else:
            self.result = total

    def finish(self):
        while self.stage < self.count:
            self.step()
        return self.result


class Line:
    def __init__(self, order, terms, owner_part):
        self.order, self.terms, self.part = order, terms, owner_part
        self.count, self.place, self.stage = lax.axis_size("tensor"), lax.axis_index("tensor"), 0
        self.step()

    def send(self, value, up):
        pairs = [(i, i + 1) for i in range(self.count - 1) if i < self.stage]
        if not up:
            pairs = [(self.count - 1 - i, self.count - 1 - j) for i, j in pairs]
        return lax.ppermute(value, "tensor", pairs)

    def step(self):
        if self.stage == self.count:
            return
        arrived = self.order.wait(*self.moving) if self.stage else ()
        self.stage += 1
        if self.stage == self.count:
            self.result = self.order.run(
                lambda terms, up, down: self.part(terms, 0).astype(f32)
                + up.astype(f32)
                + down.astype(f32),
                self.terms,
                *arrived,
            )
            return
        ahead = self.count - self.stage
        owners = jnp.minimum(self.place + ahead, self.count - 1), jnp.maximum(self.place - ahead, 0)

        def add(terms, *arrived):
            values = [self.part(terms, (self.place - owner) % self.count) for owner in owners]
            if arrived:
                values = [a.astype(f32) + b.astype(f32) for a, b in zip(values, arrived)]
            return [value.astype(bf16) for value in values]

        up, down = self.order.run(add, self.terms, *arrived)
        self.moving = self.send(up, True), self.send(down, False)

    def finish(self):
        while self.stage < self.count:
            self.step()
        return self.result


class Spread:
    def __init__(self, order, own):
        self.order, self.own = order, own
        self.count, self.place, self.stage = lax.axis_size("tensor"), lax.axis_index("tensor"), 0
        self.arrived = [(own, own)]
        self.go()

    def go(self):
        up, down = self.arrived[-1]
        pairs = [(i, i + 1) for i in range(self.count - 1) if i >= self.stage]
        back = [(self.count - 1 - i, self.count - 1 - j) for i, j in pairs]
        self.moving = lax.ppermute(up, "tensor", pairs), lax.ppermute(down, "tensor", back)
        self.stage += 1

    def step(self):
        if len(self.arrived) < self.count:
            self.arrived.append(self.order.wait(*self.moving))
            if self.stage < self.count - 1:
                self.go()

    def whole(self, dtype):
        rows, width = self.own.shape
        result = jnp.zeros((rows * self.count, width), dtype)
        for t in range(self.count):
            value = self.own
            if t:
                up, down = self.arrived[t][0], self.arrived[self.count - t][1]
                value = jnp.where(self.place >= t, up, down)
            start = (self.place - t) % self.count * rows
            result = lax.dynamic_update_slice(result, value.astype(dtype), (start, 0))
        return result


def local(
    layer_input,
    output_cotangent,
    block_ids,
    attention_gain,
    query_weight,
    key_weight,
    value_weight,
    output_weight,
    feedforward_gain,
    gate_weight,
    up_weight,
    down_weight,
):
    tokens, width = layer_input.shape
    here = lax.axis_index("dp")
    place = lax.axis_index("tensor")
    dp_count = lax.axis_size("dp")
    ring = lax.axis_size("tensor")
    part = tokens // ring
    columns = query_weight.shape[1]
    heads_here = columns // HEAD_DIM
    heads = heads_here * ring

    near_order = gather_order(here, dp_count)
    true_order = jnp.argsort(near_order).astype(jnp.int32)

    def token_part(values, owner):
        return lax.dynamic_slice_in_dim(values, owner * part, part, 0)

    gain_one = attention_gain.astype(f32)[:, None]
    gain_two = feedforward_gain.astype(f32)[:, None]
    qkv_weight = jnp.concatenate([query_weight, key_weight, value_weight], 1).astype(f32)
    order = Order()
    run, wait = order.run, order.wait

    def ring_part(values, t):
        return token_part(values, (place - t) % ring)

    qkv_gather = Gather(order, run(lambda w, g: (w * g).astype(bf16), qkv_weight, gain_one))
    qkv_gather.early()
    qkv_gather.pair()
    out_moving = [shift(output_weight, step) for step in range(1, ring)]
    gate_own = run(lambda w, g: (w.astype(f32) * g).astype(bf16), gate_weight, gain_two)
    up_own = run(lambda w, g: (w.astype(f32) * g).astype(bf16), up_weight, gain_two)
    qkv_gather.begin(False)
    hat, inputs, hat_true = run(normed_in_order, layer_input, near_order)
    qkv_gather.middle(True)
    out_pieces = wait(*out_moving)
    both_own = run(
        lambda down, *pieces: (jnp.transpose(jnp.concatenate(pieces, 0)), jnp.transpose(down)),
        down_weight,
        output_weight,
        *out_pieces,
    )
    paired = dp_count == 8 and both_own[0].shape == both_own[1].shape
    both_gather = Gather(order, jnp.concatenate(both_own, 0) if paired else both_own[0])
    both_gather.pair()
    gate_gather, up_gather = Gather(order, gate_own), Gather(order, up_own)
    qkv_gather.late()
    both_gather.begin()
    qkv_all = qkv_gather.end()

    qkv = run(mm, hat, qkv_all)
    cosine, sine = rope_tables(tokens)
    ends = last_visible(block_ids[0])
    queries, keys, values, attended, stats = run(attend_forward, qkv, ends, cosine, sine)
    moving = shift(attended, 1)
    pieces = [attended]
    gate_gather.pair()
    up_gather.pair()
    cot = run(in_order, output_cotangent, near_order)
    both_gather.middle()
    while len(pieces) < ring - 1:
        pieces.append(wait(moving))
        moving = shift(pieces[-1], 1)
        if len(pieces) == 2:
            gate_gather.begin()
            gate_gather.middle()
    both_gather.late()
    up_gather.begin()
    if paired:
        out_all, down_all = both_gather.end(2)
    else:
        out_all, down_all = both_gather.end(), double(both_own[1])
    most = jnp.concatenate(pieces, 1)
    resid_most = run(
        lambda inputs, most, weight: inputs.astype(f32) + mm_nt(most, weight[:, : most.shape[1]]),
        inputs,
        most,
        out_all,
    )
    pieces.append(wait(moving))
    gate_gather.late()

    resid_part, hat_two, hat_two_true = run(
        lambda most, last, weight, place: resid_and_norm(
            most, last, weight[:, weight.shape[1] - columns :], place, true_order, part
        ),
        resid_most,
        pieces[-1],
        out_all,
        place,
    )
    up_gather.middle()
    d_hidden = run(mm, cot, down_all)
    gate_all = gate_gather.end()
    gate = run(mm, hat_two, gate_all)
    up_gather.late()
    up_all = up_gather.end()

    hidden, d_gate, d_up = run(mid_layer, hat_two, up_all, gate, d_hidden)
    d_mid = run(pair_product, d_gate, gate_all, d_up, up_all)

    def scaled(total, weight, gain):
        total = total.astype(f32)
        return total * gain, jnp.sum(total * weight.astype(f32), 1)

    def to_sum(grad, *before):
        grad = after(grad, *before) if before else grad
        return lax.psum_scatter(grad, "dp", scatter_dimension=0, tiled=True)

    back = Ring(order, d_mid, ring_part)
    local_peak = jnp.max(stats[:, 2:4], -1).reshape(heads_here)
    peaks = [local_peak, 1]

    def peak_step():
        if peaks[1] < dp_count:
            peaks[0] = jnp.maximum(peaks[0], wait(flip(peaks[0], peaks[1])))
            peaks[1] *= 2

    gate_grad = run(plain_beside, hat_two_true, d_gate)
    peak_step()
    back.step()
    gate_moving = to_sum(gate_grad, back.arrived)
    up_grad = run(plain_beside, hat_two_true, d_up)
    peak_step()
    back.step()
    up_moving = to_sum(up_grad, gate_grad, back.arrived)
    mlp = run(product_beside, hidden, down_all)
    down_grad = run(plain_beside, output_cotangent, hidden)
    peak_step()
    scaled_two = back.finish()
    down_moving = to_sum(down_grad, up_grad, back.arrived)
    while peaks[1] < dp_count:
        peak_step()
    local_peak = peaks[0]
    forth = Ring(order, mlp, ring_part)

    def first_norm_back(scaled, resid, cot):
        inverse = lax.rsqrt(jnp.mean(resid * resid, -1, keepdims=True) + norm_epsilon)
        back = resid * inverse**3 * jnp.mean(scaled * resid, -1, keepdims=True)
        return token_part(cot, place).astype(f32) + inverse * scaled - back

    d_resid = run(first_norm_back, scaled_two, resid_part, cot)
    d_attn = d_resid.astype(bf16)
    d_att = run(lambda a, b: mm(a, b).astype(bf16), d_attn, out_all)
    d_moving = [shift(d_att[:, t * columns : (t + 1) * columns], -t) for t in range(1, ring)]
    def unite(*pieces):
        whole = jnp.zeros((tokens, columns), bf16)
        for t, piece in enumerate(pieces):
            whole = lax.dynamic_update_slice(whole, piece, ((place + t) % ring * part, 0))
        return whole

    d_pieces = wait(*d_moving)
    d_attended = run(unite, d_att[:, :columns], *d_pieces)

    def in_true_order(*pieces):
        parts = [token_part(piece, place) for piece in pieces[::-1]]
        both = jnp.concatenate(parts + parts, 0)
        whole = lax.dynamic_slice_in_dim(both, (ring - 1 - place) * part, tokens, 0)
        return jnp.concatenate(jnp.split(whole, ring, 0), 1)

    forth.step()

    def in_true_order(*pieces):
        parts = [token_part(piece, place) for piece in pieces[::-1]]
        both = jnp.concatenate(parts + parts, 0)
        whole = lax.dynamic_slice_in_dim(both, (ring - 1 - place) * part, tokens, 0)
        return jnp.concatenate(jnp.split(whole, ring, 0), 1)

    parts = run(
        attend_backward, queries, keys, values, attended, d_attended, stats, ends, cosine, sine
    )
    forth.step()
    d_qkv, d_in = run(
        lambda weight, *parts: (
            jnp.concatenate(parts, 1),
            mm_nt(jnp.concatenate(parts, 1), weight).astype(bf16),
        ),
        qkv_all,
        *parts,
    )
    qkv_grad = run(plain_beside, hat_true, d_qkv)
    out_part = run(
        lambda a, b, c: in_order((a + b).astype(bf16), c), resid_part, forth.finish(), true_order
    )
    qkv_moving = to_sum(qkv_grad, down_grad, forth.arrived)
    layer_out = Spread(order, out_part)
    att_part = run(in_true_order, *pieces)
    d_attn_true = run(in_order, d_attn, true_order)
    out_grad = run(plain_beside, d_attn_true, att_part)
    layer_out.step()
    back = Line(order, d_in, ring_part)
    out_moving = to_sum(out_grad, qkv_grad, *layer_out.arrived[1])
    back.step()
    layer_out.step()
    back.step()
    while len(layer_out.arrived) < ring:
        layer_out.step()
    scaled_one = back.finish()

    def second_norm_back(scaled, inputs, d_resid, true_order):
        values = token_part(inputs, place).astype(f32)
        inverse = lax.rsqrt(jnp.mean(values * values, -1, keepdims=True) + norm_epsilon)
        back = values * inverse**3 * jnp.mean(scaled * values, -1, keepdims=True)
        return in_order((d_resid + inverse * scaled - back).astype(bf16), true_order)

    in_part = run(second_norm_back, scaled_one, inputs, d_resid, true_order)
    moving, in_pieces = shift(in_part, 1), [in_part]
    layer_output = run(lambda: layer_out.whole(bf16))
    input_grad = jnp.zeros((tokens, width), f32)

    def place_piece(whole, piece):
        start = (place - len(in_pieces) + 1) % ring * part
        return lax.dynamic_update_slice(whole, piece.astype(f32), (start, 0))

    input_grad = run(place_piece, input_grad, in_part)
    while len(in_pieces) < ring:
        in_pieces.append(wait(moving))
        if len(in_pieces) < ring:
            moving = shift(in_pieces[-1], 1)
            input_grad = run(place_piece, input_grad, in_pieces[-1])
            if len(in_pieces) == 2:
                gate_result = run(scaled, wait(gate_moving), gate_weight, gain_two)
                up_result = run(scaled, wait(up_moving), up_weight, gain_two)
                down_result = run(lambda a: jnp.transpose(a.astype(f32)), wait(down_moving))
            else:
                qkv_result = run(scaled, wait(qkv_moving), qkv_weight, gain_one)
                out_rows = run(jnp.transpose, wait(out_moving))

    small = jnp.concatenate(
        [
            qkv_result[1],
            gate_result[1] + up_result[1],
            local_peak,
            jnp.zeros((LANES - heads_here,), f32),
        ]
    )
    small_moving = [shift(small, step) for step in range(1, ring)]

    def heads_of(owner):
        return lax.dynamic_slice_in_dim(out_rows, owner * columns, columns, 0)

    out_moving = [shift(heads_of((place + step) % ring), step) for step in range(1, ring)]
    input_grad = run(place_piece, input_grad, in_pieces[-1])
    smalls = [small, *wait(*small_moving)]
    share = width // dp_count
    peak_pieces = [piece[2 * share : 2 * share + heads_here] for piece in smalls]
    gain_sum = jnp.take(jnp.stack(smalls), (place - jnp.arange(ring)) % ring, axis=0)
    gain_sum = jnp.sum(gain_sum[:, : 2 * share].reshape(ring, 2, share), 0)
    output_grad = heads_of(place).astype(f32)
    for moved in wait(*out_moving):
        output_grad = output_grad + moved.astype(f32)
    qkv_grad = qkv_result[0]

    spots = (place - jnp.arange(heads) // heads_here) % ring * heads_here
    head_maxima = jnp.concatenate(peak_pieces)[spots + jnp.arange(heads) % heads_here]
    factor = jnp.sqrt(clip_tau / jnp.maximum(local_peak, clip_tau))
    factors = jnp.repeat(factor, HEAD_DIM)[None, :]
    query_clipped = (query_weight.astype(f32) * factors).astype(bf16)
    key_clipped = (key_weight.astype(f32) * factors).astype(bf16)

    return (
        layer_output,
        input_grad,
        gain_sum[0],
        qkv_grad[:, :columns],
        qkv_grad[:, columns : 2 * columns],
        qkv_grad[:, 2 * columns :],
        output_grad,
        gain_sum[1],
        gate_result[0],
        up_result[0],
        down_result,
        head_maxima,
        query_clipped,
        key_clipped,
    )


def solution(mesh):
    in_specs = (
        P("dp", None),
        P("dp", None),
        P("dp", None),
        P("dp"),
        P("dp", "tensor"),
        P("dp", "tensor"),
        P("dp", "tensor"),
        P("tensor", "dp"),
        P("dp"),
        P("dp", "tensor"),
        P("dp", "tensor"),
        P("tensor", "dp"),
    )
    out_specs = (
        P("dp", None),
        P("dp", None),
        P("dp"),
        P("dp", "tensor"),
        P("dp", "tensor"),
        P("dp", "tensor"),
        P("tensor", "dp"),
        P("dp"),
        P("dp", "tensor"),
        P("dp", "tensor"),
        P("tensor", "dp"),
        P(),
        P("dp", "tensor"),
        P("dp", "tensor"),
    )
    return jax.shard_map(local, mesh=mesh, in_specs=in_specs, out_specs=out_specs, check_vma=False)
```

time: 808 us -> 718 us (0.89)
  matrix products: 228 us -> 60.6 us
  Pallas kernels: 70.4 us -> 204 us
  local copies, waits for them, and re-layouts: 98.2 us -> 51 us
  other arithmetic: 94 us -> 64.8 us
  starting transfers between devices: 62.8 us -> 79.5 us
  between operations: 2.5 us -> 15.4 us
  waiting for transfers between devices: 238 us -> 229 us
    pallas_call x4 -> x17, Pallas kernels: 27.8 us -> 159 us  [the longest x5 59.2 us: plain_beside(): pl.pallas_call(tn_kernel, grid=(rows // tile,), in_specs=[pl.BlockSpec((d...]
    dot_general x17 -> x2, matrix products: 119 us -> 19.1 us  [mm_nt(): lax.dot_general(a, b, (((1,), (1,)), ((), ())), preferred_element_type=f32)]
    dot_general x10 -> x0, matrix products: 54.6 us -> none  [mm_tn(): lax.dot_general(a, b, (((0,), (0,)), ((), ())), preferred_element_type=f32)]
    ppermute x0 -> x12, waiting for transfers between devices: none -> 45.9 us  [the longest x6 37 us: send(): return lax.ppermute(value, 'tensor', pairs)]
    ppermute x33 -> x24, waiting for transfers between devices: 172 us -> 133 us  [shift(): lax.ppermute(value, 'tensor', [(i, (i + step) % count) for i in range(cou...]
    unnamed x193 -> x130, local copies, waits for them, and re-layouts: 60.1 us -> 24.9 us
    ppermute x0 -> x12, starting transfers between devices: none -> 28.7 us  [the longest x6 19.8 us: send(): return lax.ppermute(value, 'tensor', pairs)]
    ppermute x25 -> x12, waiting for transfers between devices: 59.5 us -> 43.5 us  [cross(): return lax.ppermute(value, 'dp', [(i, i ^ masks[i % 2]) for i in range(8)])]
  transfers between devices with their start and end apart: 81 -> 72, of which waited for: 31 -> 26; matrix products, arithmetic and copies ran while one was open for 42% -> 21% of each run, Pallas kernels for 9% -> 22%
where the time goes in v2:
time: 718 us; the launch traced here: 704 us
  waiting for transfers between devices  229 us (32%)
  Pallas kernels  204 us (28%)
  starting transfers between devices  79.5 us (11%)
  other arithmetic  64.8 us (9%)
  matrix products  60.6 us (8%)
  local copies, waits for them, and re-layouts  51 us (7%)
  between operations  15.4 us (2%)
    ppermute x24, waiting for transfers between devices, shift(): lax.ppermute(value, 'tensor', [(i, (i + step) % count) for i in range(cou...  133 us
    pallas_call x5, Pallas kernels, plain_beside(): pl.pallas_call(tn_kernel, grid=(rows // tile,), in_specs=[pl.BlockSpec((d...  59.2 us
    ppermute x12, waiting for transfers between devices, cross(): return lax.ppermute(value, 'dp', [(i, i ^ masks[i % 2]) for i in range(8)])  43.5 us
    dot_general x4, matrix products, mm(): lax.dot_general(a, b, (((1,), (0,)), ((), ())), preferred_element_type=f32)  41.5 us
    ppermute x6, waiting for transfers between devices, send(): return lax.ppermute(value, 'tensor', pairs)  37 us
    ppermute x24, starting transfers between devices, shift(): lax.ppermute(value, 'tensor', [(i, (i + step) % count) for i in range(cou...  28.1 us
    unnamed x130, local copies, waits for them, and re-layouts  24.9 us
    pallas_call x1, Pallas kernels, pair_product(): pl.pallas_call(pair_kernel, grid=(columns // tile,), in_specs=[whole, par...  23.9 us
  transfers between devices with their start and end apart: 72, of which 26 were waited for; matrix products, arithmetic and copies ran while one was open for 21% of the time, Pallas kernels for 22%

profile of v2, /device:TPU:0, one launch (start us, length us, event | category | flops | bytes accessed | tf_op | source)
XLA Modules:
  0.0 704.5 jit_solution(3389196385122337779)
XLA Ops:
  42.1 10.6 %collective-permute-done.3.refs_4_ = bf16[256,1536]{1,0:T(8,128)(2,1)S(1)} collective-permute-done((bf16[256,1536]{1,0:T(8,128)(2,1)}, bf16[256,1536]{1,0:T(8,128)(2,1)S(1)}, u32[]{:S(2)}, u32[]{:S(2)}) %collective-permute-start.3) | collective-permute-done | bytes 786464 | tf_op jit(solution)/shard_map/ppermute | solution.py:480
  58.2 8.5 %fusion.27.q_ref.k_ref.v_ref = f32[1024,1536]{1,0:T(8,128)} fusion(bf16[1024,2048]{1,0:T(8,128)(2,1)S(1)} %copy-done.27, bf16[2048,1536]{1,0:T(8,128)(2,1)S(1)} %stack.44), kind=kOutput, calls=%fused_computation.134 | convolution fusion | flops 6442450944 | bytes 16777216 | tf_op jit(solution)/shard_map/dot_general | solution.py:21
  66.8 17.9 %attend_forward.1 = (bf16[1024,512]{1,0:T(8,128)(2,1)S(1)}, bf16[1024,512]{1,0:T(8,128)(2,1)S(1)}, bf16[1024,512]{1,0:T(8,128)(2,1)S(1)}, bf16[1024,512]{1,0:T(8,128)(2,1)}, f32[4,8,1024]{2,1,0:T(8,128)S(1)}) custom-call(f32[1024,1536]{1,0:T(8,128)} %fusion.27.q_ref.k_ref.v_ref, f32[1024,1536]{1,0:T(8,128)} %fusion.27.q_ref.k_ref.v_ref, ...), custom_call_target="tpu_custom_call" | custom-call | flops 2147483648 | bytes 10485760 | tf_op jit(solution)/shard_map/attend_forward/pallas_call | solution.py:149
  102.3 16.2 %collective-permute-done.11 = bf16[1024,512]{1,0:T(8,128)(2,1)} collective-permute-done((bf16[1024,512]{1,0:T(8,128)(2,1)}, bf16[1024,512]{1,0:T(8,128)(2,1)}, u32[]{:S(2)}, u32[]{:S(2)}) %collective-permute-start.11) | collective-permute-done | bytes 1048608 | tf_op jit(solution)/shard_map/ppermute | solution.py:475
  120.7 33.0 %collective-permute-done.15.refs_2_ = bf16[256,2048]{1,0:T(8,128)(2,1)S(1)} collective-permute-done((bf16[256,2048]{1,0:T(8,128)(2,1)}, bf16[256,2048]{1,0:T(8,128)(2,1)S(1)}, u32[]{:S(2)}, u32[]{:S(2)}) %collective-permute-start.15) | collective-permute-done | bytes 1048608 | tf_op jit(solution)/shard_map/ppermute | solution.py:480
  164.4 12.1 %stack.45 = (bf16[2048,2048]{1,0:T(8,128)(2,1)}, bf16[2048,2048]{1,0:T(8,128)(2,1)}) custom-call(bf16[512,2048]{1,0:T(8,128)(2,1)S(1)} %pad_maximum_fusion.1.refs_0_, bf16[512,2048]{1,0:T(8,128)(2,1)} %collective-permute-done.10.refs_1_, bf16[512,2048]{1,0:T(8,128)(2,1)} %collective-permute-done.12.refs_2_, ...), custom_call_target="tpu_custom_call" | custom-call | bytes 1048576 | tf_op jit(solution)/shard_map/stack/pallas_call | solution.py:304
  176.5 10.8 %convert_add_fusion.refs_2_ = f32[1024,2048]{1,0:T(8,128)} fusion(bf16[1024,2048]{1,0:T(8,128)(2,1)S(1)} %copy-done.10, bf16[1024,1536]{1,0:T(8,128)(2,1)S(1)} %pad_maximum_fusion, bf16[2048,2048]{1,0:T(8,128)(2,1)} %get-tuple-element.427), kind=kOutput, calls=%fused_computation.2 | convolution fusion | flops 6446645248 | bytes 22020096 | tf_op jit(solution)/shard_map/dot_general | solution.py:25
  192.0 7.4 %resid_and_norm.1 = (f32[256,2048]{1,0:T(8,128)S(1)}, bf16[1024,2048]{1,0:T(8,128)(2,1)S(1)}, bf16[1024,2048]{1,0:T(8,128)(2,1)S(1)}) custom-call(s32[1]{0:T(128)} %bitcast.13.refs_0_, s32[8]{0:T(128)S(1)} %get-tuple-element.495.refs_1_.refs_0_, f32[1024,2048]{1,0:T(8,128)} %convert_add_fusion.refs_2_, ...), custom_call_target="tpu_custom_call" | custom-call | flops 2147483648 | bytes 20971520 | tf_op jit(solution)/shard_map/resid_and_norm/pallas_call | solution.py:243
  200.8 15.9 %fusion.28.dh_ref = f32[1024,2048]{1,0:T(8,128)} fusion(bf16[1024,2048]{1,0:T(8,128)(2,1)} %in_order.4, bf16[2048,2048]{1,0:T(8,128)(2,1)} %get-tuple-element.415.right_ref), kind=kOutput, calls=%fused_computation.135 | convolution fusion | flops 8589934592 | bytes 20971520 | tf_op jit(solution)/shard_map/dot_general | solution.py:21
  219.5 11.0 %fusion.29.gate_ref = f32[1024,2048]{1,0:T(8,128)} fusion(bf16[1024,2048]{1,0:T(8,128)(2,1)S(1)} %copy-done.25, bf16[2048,2048]{1,0:T(8,128)(2,1)S(1)} %stack.46.b_ref), kind=kOutput, calls=%fused_computation.136 | convolution fusion | flops 8589934592 | bytes 20971520 | tf_op jit(solution)/shard_map/dot_general | solution.py:21
  241.8 20.2 %mid_layer.1 = (bf16[1024,2048]{1,0:T(8,128)(2,1)}, bf16[1024,2048]{1,0:T(8,128)(2,1)}, bf16[1024,2048]{1,0:T(8,128)(2,1)}) custom-call(bf16[1024,2048]{1,0:T(8,128)(2,1)} %copy-done.24, bf16[2048,2048]{1,0:T(8,128)(2,1)} %copy-done.2, f32[1024,2048]{1,0:T(8,128)} %fusion.29.gate_ref, f32[1024,2048]{1,0:T(8,128)} %fusion.28.dh_ref), custom_call_target="tpu_custom_call" | custom-call | flops 8589934592 | bytes 41943040 | tf_op jit(solution)/shard_map/mid_layer/pallas_call | solution.py:422
  262.0 23.9 %pair_product.1 = bf16[1024,2048]{1,0:T(8,128)(2,1)} custom-call(bf16[1024,2048]{1,0:T(8,128)(2,1)} %get-tuple-element.403.a_ref.right_ref, bf16[2048,2048]{1,0:T(8,128)(2,1)} %copy-done.1, bf16[1024,2048]{1,0:T(8,128)(2,1)} %get-tuple-element.409.c_ref.right_ref, bf16[2048,2048]{1,0:T(8,128)(2,1)} %copy-done.2), custom_call_target="tpu_custom_call" | custom-call | flops 17179869184 | bytes 25165824 | tf_op jit(solution)/shard_map/pair_product/pallas_call | solution.py:450
  287.7 13.4 %plain_beside.5 = bf16[2048,2048]{1,0:T(8,128)(2,1)} custom-call(bf16[1024,2048]{1,0:T(8,128)(2,1)} %copy-done, bf16[1024,2048]{1,0:T(8,128)(2,1)} %get-tuple-element.403.a_ref.right_ref), custom_call_target="tpu_custom_call" | custom-call | flops 4294967296 | bytes 1048576 | tf_op jit(solution)/shard_map/plain_beside/pallas_call | solution.py:371
  301.2 13.3 %collective-permute-done.34 = bf16[256,2048]{1,0:T(8,128)(2,1)} collective-permute-done((bf16[256,2048]{1,0:T(8,128)(2,1)S(1)}, bf16[256,2048]{1,0:T(8,128)(2,1)}, u32[]{:S(2)}, u32[]{:S(2)}) %collective-permute-start.34) | collective-permute-done | bytes 1048608 | tf_op jit(solution)/shard_map/ppermute | solution.py:475
  317.9 14.0 %plain_beside.6 = bf16[2048,2048]{1,0:T(8,128)(2,1)} custom-call(bf16[1024,2048]{1,0:T(8,128)(2,1)} %copy-done, bf16[1024,2048]{1,0:T(8,128)(2,1)} %get-tuple-element.409.c_ref.right_ref), custom_call_target="tpu_custom_call" | custom-call | flops 4294967296 | bytes 1048576 | tf_op jit(solution)/shard_map/plain_beside/pallas_call | solution.py:371
  331.9 12.1 %collective-permute-done.36 = bf16[256,2048]{1,0:T(8,128)(2,1)S(1)} collective-permute-done((bf16[256,2048]{1,0:T(8,128)(2,1)}, bf16[256,2048]{1,0:T(8,128)(2,1)S(1)}, u32[]{:S(2)}, u32[]{:S(2)}) %collective-permute-start.36) | collective-permute-done | bytes 1048608 | tf_op jit(solution)/shard_map/ppermute | solution.py:475
  348.0 13.7 %product_beside.1 = bf16[1024,2048]{1,0:T(8,128)(2,1)} custom-call(bf16[1024,2048]{1,0:T(8,128)(2,1)} %get-tuple-element.417.left_ref.right_ref, bf16[2048,2048]{1,0:T(8,128)(2,1)} %get-tuple-element.415.right_ref), custom_call_target="tpu_custom_call" | custom-call | flops 4294967296 | bytes 1048576 | tf_op jit(solution)/shard_map/product_beside/pallas_call | solution.py:393
  361.7 13.5 %plain_beside.7 = bf16[2048,2048]{1,0:T(8,128)(2,1)} custom-call(bf16[1024,2048]{1,0:T(8,128)(2,1)} %left_ref, bf16[1024,2048]{1,0:T(8,128)(2,1)} %get-tuple-element.417.left_ref.right_ref), custom_call_target="tpu_custom_call" | custom-call | flops 4294967296 | bytes 1048576 | tf_op jit(solution)/shard_map/plain_beside/pallas_call | solution.py:371
  382.9 6.1 convolution_convert_fusion.1
  396.1 14.1 %collective-permute-done.41 = bf16[256,512]{1,0:T(8,128)(2,1)S(1)} collective-permute-done((bf16[256,512]{1,0:T(8,128)(2,1)}, bf16[256,512]{1,0:T(8,128)(2,1)S(1)}, u32[]{:S(2)}, u32[]{:S(2)}) %collective-permute-start.41) | collective-permute-done | bytes 262176 | tf_op jit(solution)/shard_map/ppermute | solution.py:475
  410.2 16.9 %collective-permute-done.42 = bf16[256,512]{1,0:T(8,128)(2,1)S(1)} collective-permute-done((bf16[256,512]{1,0:T(8,128)(2,1)}, bf16[256,512]{1,0:T(8,128)(2,1)S(1)}, u32[]{:S(2)}, u32[]{:S(2)}) %collective-permute-start.42) | collective-permute-done | bytes 262176 | tf_op jit(solution)/shard_map/ppermute | solution.py:475
  430.6 23.3 %attend_backward.1 = (bf16[1024,512]{1,0:T(8,128)(2,1)S(1)}, bf16[1024,512]{1,0:T(8,128)(2,1)S(1)}, bf16[1024,512]{1,0:T(8,128)(2,1)S(1)}) custom-call(bf16[1024,512]{1,0:T(8,128)(2,1)S(1)} %copy-done.29, bf16[1024,512]{1,0:T(8,128)(2,1)} %copy-done.30, bf16[1024,512]{1,0:T(8,128)(2,1)} %copy-done.31, bf16[1024,512]{1,0:T(8,128)(2,1)} %get-tuple-element.468.att_ref, ...), custom_call_target="tpu_custom_call" | custom-call | flops 4294967296 | bytes 1048576 | tf_op jit(solution)/shard_map/attend_backward/pallas_call | solution.py:167
  460.4 8.2 %convolution_convert_fusion = bf16[1024,2048]{1,0:T(8,128)(2,1)} fusion(bf16[1024,1536]{1,0:T(8,128)(2,1)S(1)} %constant_dynamic-update-slice_fusion.right_ref, bf16[2048,1536]{1,0:T(8,128)(2,1)S(1)} %bitcast.48), kind=kOutput, calls=%fused_computation.6 | convolution fusion | flops 6444548096 | bytes 13631488 | tf_op jit(solution)/shard_map/dot_general | solution.py:25
  468.6 11.8 %plain_beside.8 = bf16[2048,1536]{1,0:T(8,128)(2,1)} custom-call(bf16[1024,2048]{1,0:T(8,128)(2,1)} %copy-done.23, bf16[1024,1536]{1,0:T(8,128)(2,1)} %copy-done.50), custom_call_target="tpu_custom_call" | custom-call | flops 4294967296 | bytes 1048576 | tf_op jit(solution)/shard_map/plain_beside/pallas_call | solution.py:371
  504.6 6.5 plain_beside.9
  529.6 13.6 %collective-permute-done.50 = bf16[256,2048]{1,0:T(8,128)(2,1)} collective-permute-done((bf16[256,2048]{1,0:T(8,128)(2,1)S(1)}, bf16[256,2048]{1,0:T(8,128)(2,1)}, u32[]{:S(2)}, u32[]{:S(2)}) %collective-permute-start.50) | collective-permute-done | bytes 1048608 | tf_op jit(solution)/shard_map/ppermute | solution.py:597
  563.5 7.8 %collective-permute-done.54 = bf16[256,2048]{1,0:T(8,128)(2,1)} collective-permute-done((bf16[256,2048]{1,0:T(8,128)(2,1)}, bf16[256,2048]{1,0:T(8,128)(2,1)}, u32[]{:S(2)}, u32[]{:S(2)}) %collective-permute-start.54) | collective-permute-done | bytes 1048608 | tf_op jit(solution)/shard_map/ppermute | solution.py:597
  573.6 6.9 collective-permute-start.56
  585.8 10.8 %collective-permute-done.56 = bf16[256,2048]{1,0:T(8,128)(2,1)S(1)} collective-permute-done((bf16[256,2048]{1,0:T(8,128)(2,1)S(1)}, bf16[256,2048]{1,0:T(8,128)(2,1)S(1)}, u32[]{:S(2)}, u32[]{:S(2)}) %collective-permute-start.56) | collective-permute-done | bytes 1048608 | tf_op jit(solution)/shard_map/ppermute | solution.py:597
  616.7 13.6 %collective-permute-done.58 = bf16[256,2048]{1,0:T(8,128)(2,1)} collective-permute-done((bf16[256,2048]{1,0:T(8,128)(2,1)}, bf16[256,2048]{1,0:T(8,128)(2,1)}, u32[]{:S(2)}, u32[]{:S(2)}) %collective-permute-start.58) | collective-permute-done | bytes 1048608 | tf_op jit(solution)/shard_map/ppermute | solution.py:475
  640.8 13.0 %collective-permute-done.59 = bf16[256,2048]{1,0:T(8,128)(2,1)S(1)} collective-permute-done((bf16[256,2048]{1,0:T(8,128)(2,1)}, bf16[256,2048]{1,0:T(8,128)(2,1)S(1)}, u32[]{:S(2)}, u32[]{:S(2)}) %collective-permute-start.59) | collective-permute-done | bytes 1048608 | tf_op jit(solution)/shard_map/ppermute | solution.py:475
  665.6 8.5 %collective-permute-done.60 = bf16[256,2048]{1,0:T(8,128)(2,1)} collective-permute-done((bf16[256,2048]{1,0:T(8,128)(2,1)S(1)}, bf16[256,2048]{1,0:T(8,128)(2,1)}, u32[]{:S(2)}, u32[]{:S(2)}) %collective-permute-start.60) | collective-permute-done | bytes 1048608 | tf_op jit(solution)/shard_map/ppermute | solution.py:475
  (366 shorter events, 260.4 us)
Async XLA Ops:
  7.2 626.0 %reduce-scatter.10.cloned.1.call-start = ((), (), s32[]{:S(2)}) async-start(), calls=%async_computation.7 | async-start | bytes 9437184 | tf_op jit(solution)/shard_map/reduce_scatter | solution.py:784
  53.7 47.3 %collective-permute-start.12 = (bf16[512,2048]{1,0:T(8,128)(2,1)S(1)}, bf16[512,2048]{1,0:T(8,128)(2,1)}, u32[]{:S(2)}, u32[]{:S(2)}) collective-permute-start(bf16[512,2048]{1,0:T(8,128)(2,1)S(1)} %pad_maximum_fusion.1.refs_0_), channel_id=1, source_target_pairs={{0,8},{4,20},{8,0},{12,28},{16,24},{20,4},{24,16},{28,12},{1,9},{5... | collective-permute-start | bytes 6291464 | tf_op jit(solution)/shard_map/ppermute | solution.py:480
  87.6 30.9 %collective-permute-start.11 = (bf16[1024,512]{1,0:T(8,128)(2,1)}, bf16[1024,512]{1,0:T(8,128)(2,1)}, u32[]{:S(2)}, u32[]{:S(2)}) collective-permute-start(bf16[1024,512]{1,0:T(8,128)(2,1)} %get-tuple-element.468.att_ref), channel_id=1, source_target_pairs={{0,1},{1,2},{2,3},{3,0},{4,5},{5,6},{6,7},{7,4},{8,9},{9,10},{10,1... | collective-permute-start | bytes 3145736 | tf_op jit(solution)/shard_map/ppermute | solution.py:475
  93.7 60.0 %collective-permute-start.16 = (bf16[512,2048]{1,0:T(8,128)(2,1)}, bf16[512,2048]{1,0:T(8,128)(2,1)}, u32[]{:S(2)}, u32[]{:S(2)}) collective-permute-start(bf16[512,2048]{1,0:T(8,128)(2,1)} %collective-permute-done.10.refs_1_), channel_id=1, source_target_pairs={{0,8},{4,20},{8,0},{12,28},{16,24},{20,4},{24,16},{28,12},{1,9},{5... | collective-permute-start | bytes 6291464 | tf_op jit(solution)/shard_map/ppermute | solution.py:480
  101.0 52.7 %collective-permute-start.17 = (bf16[512,2048]{1,0:T(8,128)(2,1)}, bf16[512,2048]{1,0:T(8,128)(2,1)}, u32[]{:S(2)}, u32[]{:S(2)}) collective-permute-start(bf16[512,2048]{1,0:T(8,128)(2,1)} %collective-permute-done.12.refs_2_), channel_id=1, source_target_pairs={{0,16},{4,12},{8,24},{12,4},{16,0},{20,28},{24,8},{28,20},{1,17},{... | collective-permute-start | bytes 6291464 | tf_op jit(solution)/shard_map/ppermute | solution.py:480
  118.5 35.2 %collective-permute-start.15 = (bf16[256,2048]{1,0:T(8,128)(2,1)}, bf16[256,2048]{1,0:T(8,128)(2,1)S(1)}, u32[]{:S(2)}, u32[]{:S(2)}) collective-permute-start(bf16[256,2048]{1,0:T(8,128)(2,1)} %multiply_convert_fusion.1.refs_0_), channel_id=1, source_target_pairs={{0,8},{4,20},{8,0},{12,28},{16,24},{20,4},{24,16},{28,12},{1,9},{5... | collective-permute-start | bytes 3145736 | tf_op jit(solution)/shard_map/ppermute | solution.py:480
  120.0 33.7 %collective-permute-start.13 = (bf16[1024,512]{1,0:T(8,128)(2,1)}, bf16[1024,512]{1,0:T(8,128)(2,1)S(1)}, u32[]{:S(2)}, u32[]{:S(2)}) collective-permute-start(bf16[1024,512]{1,0:T(8,128)(2,1)} %collective-permute-done.11), channel_id=1, source_target_pairs={{0,1},{1,2},{2,3},{3,0},{4,5},{5,6},{6,7},{7,4},{8,9},{9,10},{10,1... | collective-permute-start | bytes 3145736 | tf_op jit(solution)/shard_map/ppermute | solution.py:475
  120.7 40.7 %collective-permute-start.18 = (bf16[512,2048]{1,0:T(8,128)(2,1)}, bf16[512,2048]{1,0:T(8,128)(2,1)}, u32[]{:S(2)}, u32[]{:S(2)}) collective-permute-start(bf16[512,2048]{1,0:T(8,128)(2,1)} %collective-permute-done.12.refs_2_), channel_id=1, source_target_pairs={{0,4},{4,0},{8,12},{12,8},{16,20},{20,16},{24,28},{28,24},{1,5},{5... | collective-permute-start | bytes 6291464 | tf_op jit(solution)/shard_map/ppermute | solution.py:470
  156.1 33.7 %collective-permute-start.23 = (bf16[256,2048]{1,0:T(8,128)(2,1)}, bf16[256,2048]{1,0:T(8,128)(2,1)S(1)}, u32[]{:S(2)}, u32[]{:S(2)}) collective-permute-start(bf16[256,2048]{1,0:T(8,128)(2,1)} %collective-permute-done.14.refs_1_), channel_id=1, source_target_pairs={{0,8},{4,20},{8,0},{12,28},{16,24},{20,4},{24,16},{28,12},{1,9},{5... | collective-permute-start | bytes 3145736 | tf_op jit(solution)/shard_map/ppermute | solution.py:480
  161.0 27.2 %collective-permute-start.22 = (bf16[1024,512]{1,0:T(8,128)(2,1)S(1)}, bf16[1024,512]{1,0:T(8,128)(2,1)S(1)}, u32[]{:S(2)}, u32[]{:S(2)}) collective-permute-start(bf16[1024,512]{1,0:T(8,128)(2,1)S(1)} %copy-done.45), channel_id=1, source_target_pairs={{0,1},{1,2},{2,3},{3,0},{4,5},{5,6},{6,7},{7,4},{8,9},{9,10},{10,1... | collective-permute-start | bytes 3145736 | tf_op jit(solution)/shard_map/ppermute | solution.py:475
  161.4 28.4 %collective-permute-start.24 = (bf16[256,2048]{1,0:T(8,128)(2,1)S(1)}, bf16[256,2048]{1,0:T(8,128)(2,1)S(1)}, u32[]{:S(2)}, u32[]{:S(2)}) collective-permute-start(bf16[256,2048]{1,0:T(8,128)(2,1)S(1)} %copy-done.13), channel_id=1, source_target_pairs={{0,16},{4,12},{8,24},{12,4},{16,0},{20,28},{24,8},{28,20},{1,17},{... | collective-permute-start | bytes 3145736 | tf_op jit(solution)/shard_map/ppermute | solution.py:480
  162.9 53.8 %collective-permute-start.28 = (bf16[256,2048]{1,0:T(8,128)(2,1)S(1)}, bf16[256,2048]{1,0:T(8,128)(2,1)S(1)}, u32[]{:S(2)}, u32[]{:S(2)}) collective-permute-start(bf16[256,2048]{1,0:T(8,128)(2,1)S(1)} %copy-done.13), channel_id=1, source_target_pairs={{0,4},{4,0},{8,12},{12,8},{16,20},{20,16},{24,28},{28,24},{1,5},{5... | collective-permute-start | bytes 3145736 | tf_op jit(solution)/shard_map/ppermute | solution.py:470
  162.9 36.6 %collective-permute-start.25 = (bf16[256,2048]{1,0:T(8,128)(2,1)S(1)}, bf16[256,2048]{1,0:T(8,128)(2,1)}, u32[]{:S(2)}, u32[]{:S(2)}) collective-permute-start(bf16[256,2048]{1,0:T(8,128)(2,1)S(1)} %multiply_convert_fusion.refs_0_), channel_id=1, source_target_pairs={{0,8},{4,20},{8,0},{12,28},{16,24},{20,4},{24,16},{28,12},{1,9},{5... | collective-permute-start | bytes 3145736 | tf_op jit(solution)/shard_map/ppermute | solution.py:480
  188.3 42.2 %collective-permute-start.26 = (bf16[256,2048]{1,0:T(8,128)(2,1)}, bf16[256,2048]{1,0:T(8,128)(2,1)}, u32[]{:S(2)}, u32[]{:S(2)}) collective-permute-start(bf16[256,2048]{1,0:T(8,128)(2,1)} %collective-permute-done.21.refs_1_), channel_id=1, source_target_pairs={{0,8},{4,20},{8,0},{12,28},{16,24},{20,4},{24,16},{28,12},{1,9},{5... | collective-permute-start | bytes 3145736 | tf_op jit(solution)/shard_map/ppermute | solution.py:480
  189.8 27.0 %collective-permute-start.29 = (bf16[256,2048]{1,0:T(8,128)(2,1)S(1)}, bf16[256,2048]{1,0:T(8,128)(2,1)S(1)}, u32[]{:S(2)}, u32[]{:S(2)}) collective-permute-start(bf16[256,2048]{1,0:T(8,128)(2,1)S(1)} %collective-permute-done.23.refs_3_), channel_id=1, source_target_pairs={{0,4},{4,0},{8,12},{12,8},{16,20},{20,16},{24,28},{28,24},{1,5},{5... | collective-permute-start | bytes 3145736 | tf_op jit(solution)/shard_map/ppermute | solution.py:470
  189.8 27.0 %collective-permute-start.30 = (bf16[256,2048]{1,0:T(8,128)(2,1)S(1)}, bf16[256,2048]{1,0:T(8,128)(2,1)S(1)}, u32[]{:S(2)}, u32[]{:S(2)}) collective-permute-start(bf16[256,2048]{1,0:T(8,128)(2,1)S(1)} %collective-permute-done.24.refs_4_), channel_id=1, source_target_pairs={{0,4},{4,0},{8,12},{12,8},{16,20},{20,16},{24,28},{28,24},{1,5},{5... | collective-permute-start | bytes 3145736 | tf_op jit(solution)/shard_map/ppermute | solution.py:470
  199.5 31.0 %collective-permute-start.27 = (bf16[256,2048]{1,0:T(8,128)(2,1)}, bf16[256,2048]{1,0:T(8,128)(2,1)}, u32[]{:S(2)}, u32[]{:S(2)}) collective-permute-start(bf16[256,2048]{1,0:T(8,128)(2,1)} %collective-permute-done.25.refs_2_), channel_id=1, source_target_pairs={{0,16},{4,12},{8,24},{12,4},{16,0},{20,28},{24,8},{28,20},{1,17},{... | collective-permute-start | bytes 3145736 | tf_op jit(solution)/shard_map/ppermute | solution.py:480
  287.2 27.3 %collective-permute-start.34 = (bf16[256,2048]{1,0:T(8,128)(2,1)S(1)}, bf16[256,2048]{1,0:T(8,128)(2,1)}, u32[]{:S(2)}, u32[]{:S(2)}) collective-permute-start(bf16[256,2048]{1,0:T(8,128)(2,1)S(1)} %constant_dynamic-slice_fusion.7), channel_id=1, source_target_pairs={{0,1},{1,2},{2,3},{3,0},{4,5},{5,6},{6,7},{7,4},{8,9},{9,10},{10,1... | collective-permute-start | bytes 3145736 | tf_op jit(solution)/shard_map/ppermute | solution.py:475
  314.5 321.8 %reduce-scatter.8.cloned.1.call-start = ((), (), s32[]{:S(2)}) async-start(), calls=%async_computation.6 | async-start | bytes 9437184 | tf_op jit(solution)/shard_map/reduce_scatter | solution.py:784
  317.5 26.6 %collective-permute-start.36 = (bf16[256,2048]{1,0:T(8,128)(2,1)}, bf16[256,2048]{1,0:T(8,128)(2,1)S(1)}, u32[]{:S(2)}, u32[]{:S(2)}) collective-permute-start(bf16[256,2048]{1,0:T(8,128)(2,1)} %add_convert_fusion.8), channel_id=1, source_target_pairs={{0,1},{1,2},{2,3},{3,0},{4,5},{5,6},{6,7},{7,4},{8,9},{9,10},{10,1... | collective-permute-start | bytes 3145736 | tf_op jit(solution)/shard_map/ppermute | solution.py:475
  344.1 295.3 %reduce-scatter.6.cloned.1.call-start = ((), (), s32[]{:S(2)}) async-start(), calls=%async_computation.5 | async-start | bytes 9437184 | tf_op jit(solution)/shard_map/reduce_scatter | solution.py:784
  346.8 28.5 %collective-permute-start.38 = (bf16[256,2048]{1,0:T(8,128)(2,1)}, bf16[256,2048]{1,0:T(8,128)(2,1)S(1)}, u32[]{:S(2)}, u32[]{:S(2)}) collective-permute-start(bf16[256,2048]{1,0:T(8,128)(2,1)} %add_convert_fusion.7), channel_id=1, source_target_pairs={{0,1},{1,2},{2,3},{3,0},{4,5},{5,6},{6,7},{7,4},{8,9},{9,10},{10,1... | collective-permute-start | bytes 3145736 | tf_op jit(solution)/shard_map/ppermute | solution.py:475
  346.8 28.4 %collective-permute-start.39 = (f32[8]{0:T(128)S(1)}, f32[8]{0:T(128)S(1)}, u32[]{:S(2)}, u32[]{:S(2)}) collective-permute-start(f32[8]{0:T(128)S(1)} %max.22), channel_id=1, source_target_pairs={{0,16},{4,20},{8,24},{12,28},{16,0},{20,4},{24,8},{28,12},{1,17},{... | collective-permute-start | bytes 104 | tf_op jit(solution)/shard_map/ppermute | solution.py:470
  375.2 281.9 %reduce-scatter.12.cloned.1.call-start = ((), (), s32[]{:S(2)}) async-start(), calls=%async_computation.8 | async-start | bytes 7077888 | tf_op jit(solution)/shard_map/reduce_scatter | solution.py:784
  379.2 48.1 %collective-permute-start.40 = (bf16[256,2048]{1,0:T(8,128)(2,1)}, bf16[256,2048]{1,0:T(8,128)(2,1)}, u32[]{:S(2)}, u32[]{:S(2)}) collective-permute-start(bf16[256,2048]{1,0:T(8,128)(2,1)} %constant_dynamic-slice_fusion.6), channel_id=1, source_target_pairs={{0,1},{1,2},{2,3},{3,0},{4,5},{5,6},{6,7},{7,4},{8,9},{9,10},{10,1... | collective-permute-start | bytes 3145736 | tf_op jit(solution)/shard_map/ppermute | solution.py:475
  393.7 33.4 %collective-permute-start.42 = (bf16[256,512]{1,0:T(8,128)(2,1)}, bf16[256,512]{1,0:T(8,128)(2,1)S(1)}, u32[]{:S(2)}, u32[]{:S(2)}) collective-permute-start(bf16[256,512]{1,0:T(8,128)(2,1)} %get-tuple-element.605), channel_id=1, source_target_pairs={{0,2},{1,3},{2,0},{3,1},{4,6},{5,7},{6,4},{7,5},{8,10},{9,11},{10,... | collective-permute-start | bytes 786440 | tf_op jit(solution)/shard_map/ppermute | solution.py:475
  394.1 33.0 %collective-permute-start.43 = (bf16[256,512]{1,0:T(8,128)(2,1)}, bf16[256,512]{1,0:T(8,128)(2,1)S(1)}, u32[]{:S(2)}, u32[]{:S(2)}) collective-permute-start(bf16[256,512]{1,0:T(8,128)(2,1)} %get-tuple-element.604), channel_id=1, source_target_pairs={{0,1},{1,2},{2,3},{3,0},{4,5},{5,6},{6,7},{7,4},{8,9},{9,10},{10,1... | collective-permute-start | bytes 786440 | tf_op jit(solution)/shard_map/ppermute | solution.py:475
  430.5 27.0 %collective-permute-start.44 = (bf16[256,2048]{1,0:T(8,128)(2,1)S(1)}, bf16[256,2048]{1,0:T(8,128)(2,1)S(1)}, u32[]{:S(2)}, u32[]{:S(2)}) collective-permute-start(bf16[256,2048]{1,0:T(8,128)(2,1)S(1)} %add_convert_fusion.6), channel_id=1, source_target_pairs={{0,1},{1,2},{2,3},{3,0},{4,5},{5,6},{6,7},{7,4},{8,9},{9,10},{10,1... | collective-permute-start | bytes 3145736 | tf_op jit(solution)/shard_map/ppermute | solution.py:475
  460.1 26.2 %collective-permute-start.45 = (bf16[256,2048]{1,0:T(8,128)(2,1)}, bf16[256,2048]{1,0:T(8,128)(2,1)S(1)}, u32[]{:S(2)}, u32[]{:S(2)}) collective-permute-start(bf16[256,2048]{1,0:T(8,128)(2,1)} %add_convert_fusion.5), channel_id=1, source_target_pairs={{0,1},{1,2},{2,3},{3,0},{4,5},{5,6},{6,7},{7,4},{8,9},{9,10},{10,1... | collective-permute-start | bytes 3145736 | tf_op jit(solution)/shard_map/ppermute | solution.py:475
  486.4 191.3 %reduce-scatter.14.cloned.1.call-start = ((), (), s32[]{:S(2)}) async-start(), calls=%async_computation.9 | async-start | bytes 9437184 | tf_op jit(solution)/shard_map/reduce_scatter | solution.py:784
  526.3 29.4 %collective-permute-start.48 = (bf16[256,2048]{1,0:T(8,128)(2,1)}, bf16[256,2048]{1,0:T(8,128)(2,1)}, u32[]{:S(2)}, u32[]{:S(2)}) collective-permute-start(bf16[256,2048]{1,0:T(8,128)(2,1)} %collective-permute-done.46), channel_id=1, source_target_pairs={{1,2},{2,3},{5,6},{6,7},{9,10},{10,11},{13,14},{14,15},{17,18},{18... | collective-permute-start | bytes 3145736 | tf_op jit(solution)/shard_map/ppermute | solution.py:642
  528.1 27.6 %collective-permute-start.49 = (bf16[256,2048]{1,0:T(8,128)(2,1)S(1)}, bf16[256,2048]{1,0:T(8,128)(2,1)}, u32[]{:S(2)}, u32[]{:S(2)}) collective-permute-start(bf16[256,2048]{1,0:T(8,128)(2,1)S(1)} %collective-permute-done.47), channel_id=1, source_target_pairs={{2,1},{1,0},{6,5},{5,4},{10,9},{9,8},{14,13},{13,12},{18,17},{17,1... | collective-permute-start | bytes 3145736 | tf_op jit(solution)/shard_map/ppermute | solution.py:642
  (99 other events, 1168.4 us)
Sparse Core Ops, SparseCore 0:
  314.6 68.3 reduce-scatter.9
  386.9 71.2 reduce-scatter.7
  461.6 71.2 reduce-scatter.5
  536.6 61.7 reduce-scatter.11
  601.7 71.2 reduce-scatter.13

commit v3 on v2

--- a/solution.py
+++ b/solution.py
@@ -733,15 +733,15 @@
     gate_gather.pair()
     up_gather.pair()
     cot = run(in_order, output_cotangent, near_order)
-    both_gather.middle()
+    both_gather.middle(True)
     while len(pieces) < ring - 1:
         pieces.append(wait(moving))
         moving = shift(pieces[-1], 1)
         if len(pieces) == 2:
             gate_gather.begin()
-            gate_gather.middle()
+            gate_gather.middle(True)
+    up_gather.begin()
     both_gather.late()
-    up_gather.begin()
     if paired:
         out_all, down_all = both_gather.end(2)
     else:
@@ -768,8 +768,8 @@
     up_gather.middle()
     d_hidden = run(mm, cot, down_all)
     gate_all = gate_gather.end()
+    up_gather.late()
     gate = run(mm, hat_two, gate_all)
-    up_gather.late()
     up_all = up_gather.end()
 
     hidden, d_gate, d_up = run(mid_layer, hat_two, up_all, gate, d_hidden)

time: 718 us -> 713 us (level)
  waiting for transfers between devices: 229 us -> 217 us
  starting transfers between devices: 79.5 us -> 86.9 us
    unnamed x130 -> x134, local copies, waits for them, and re-layouts: 24.9 us -> 24.2 us
  transfers between devices with their start and end apart: 72 -> 72, of which waited for: 26 -> 24; matrix products, arithmetic and copies ran while one was open for 21% -> 21% of each run, Pallas kernels for 22% -> 22%
where the time goes in v3:
time: 713 us; the launch traced here: 699 us
  waiting for transfers between devices  217 us (30%)
  Pallas kernels  202 us (28%)
  starting transfers between devices  86.9 us (12%)
  other arithmetic  65.6 us (9%)
  matrix products  61.7 us (9%)
  local copies, waits for them, and re-layouts  50.3 us (7%)
  between operations  15.4 us (2%)
    ppermute x24, waiting for transfers between devices, shift(): lax.ppermute(value, 'tensor', [(i, (i + step) % count) for i in range(cou...  129 us
    pallas_call x5, Pallas kernels, plain_beside(): pl.pallas_call(tn_kernel, grid=(rows // tile,), in_specs=[pl.BlockSpec((d...  59.1 us
    dot_general x4, matrix products, mm(): lax.dot_general(a, b, (((1,), (0,)), ((), ())), preferred_element_type=f32)  41.6 us
    ppermute x12, waiting for transfers between devices, cross(): return lax.ppermute(value, 'dp', [(i, i ^ masks[i % 2]) for i in range(8)])  39.5 us
    ppermute x6, waiting for transfers between devices, send(): return lax.ppermute(value, 'tensor', pairs)  38.2 us
    ppermute x24, starting transfers between devices, shift(): lax.ppermute(value, 'tensor', [(i, (i + step) % count) for i in range(cou...  33.8 us
    unnamed x134, local copies, waits for them, and re-layouts  24.2 us
    pallas_call x1, Pallas kernels, pair_product(): pl.pallas_call(pair_kernel, grid=(columns // tile,), in_specs=[whole, par...  23.8 us
  transfers between devices with their start and end apart: 72, of which 24 were waited for; matrix products, arithmetic and copies ran while one was open for 21% of the time, Pallas kernels for 22%

profile of v3, /device:TPU:0, one launch (start us, length us, event | category | flops | bytes accessed | tf_op | source)
XLA Modules:
  0.0 699.0 jit_solution(103921707787938193)
XLA Ops:
  42.1 10.6 %collective-permute-done.3.refs_4_ = bf16[256,1536]{1,0:T(8,128)(2,1)S(1)} collective-permute-done((bf16[256,1536]{1,0:T(8,128)(2,1)}, bf16[256,1536]{1,0:T(8,128)(2,1)S(1)}, u32[]{:S(2)}, u32[]{:S(2)}) %collective-permute-start.3) | collective-permute-done | bytes 786464 | tf_op jit(solution)/shard_map/ppermute | solution.py:480
  58.2 8.5 %fusion.27.q_ref.k_ref.v_ref = f32[1024,1536]{1,0:T(8,128)} fusion(bf16[1024,2048]{1,0:T(8,128)(2,1)S(1)} %copy-done.29, bf16[2048,1536]{1,0:T(8,128)(2,1)S(1)} %stack.44), kind=kOutput, calls=%fused_computation.134 | convolution fusion | flops 6442450944 | bytes 16777216 | tf_op jit(solution)/shard_map/dot_general | solution.py:21
  66.8 17.9 %attend_forward.1 = (bf16[1024,512]{1,0:T(8,128)(2,1)S(1)}, bf16[1024,512]{1,0:T(8,128)(2,1)S(1)}, bf16[1024,512]{1,0:T(8,128)(2,1)S(1)}, bf16[1024,512]{1,0:T(8,128)(2,1)}, f32[4,8,1024]{2,1,0:T(8,128)S(1)}) custom-call(f32[1024,1536]{1,0:T(8,128)} %fusion.27.q_ref.k_ref.v_ref, f32[1024,1536]{1,0:T(8,128)} %fusion.27.q_ref.k_ref.v_ref, ...), custom_call_target="tpu_custom_call" | custom-call | flops 2147483648 | bytes 10485760 | tf_op jit(solution)/shard_map/attend_forward/pallas_call | solution.py:149
  103.8 14.7 %collective-permute-done.11 = bf16[1024,512]{1,0:T(8,128)(2,1)} collective-permute-done((bf16[1024,512]{1,0:T(8,128)(2,1)}, bf16[1024,512]{1,0:T(8,128)(2,1)}, u32[]{:S(2)}, u32[]{:S(2)}) %collective-permute-start.11) | collective-permute-done | bytes 1048608 | tf_op jit(solution)/shard_map/ppermute | solution.py:475
  121.3 16.8 %collective-permute-done.16.refs_2_ = bf16[256,2048]{1,0:T(8,128)(2,1)S(1)} collective-permute-done((bf16[256,2048]{1,0:T(8,128)(2,1)}, bf16[256,2048]{1,0:T(8,128)(2,1)S(1)}, u32[]{:S(2)}, u32[]{:S(2)}) %collective-permute-start.16) | collective-permute-done | bytes 1048608 | tf_op jit(solution)/shard_map/ppermute | solution.py:480
  140.0 9.3 %collective-permute-done.17.refs_3_ = bf16[256,2048]{1,0:T(8,128)(2,1)S(1)} collective-permute-done((bf16[256,2048]{1,0:T(8,128)(2,1)}, bf16[256,2048]{1,0:T(8,128)(2,1)S(1)}, u32[]{:S(2)}, u32[]{:S(2)}) %collective-permute-start.17) | collective-permute-done | bytes 1048608 | tf_op jit(solution)/shard_map/ppermute | solution.py:480
  166.6 12.1 %stack.45 = (bf16[2048,2048]{1,0:T(8,128)(2,1)}, bf16[2048,2048]{1,0:T(8,128)(2,1)}) custom-call(bf16[512,2048]{1,0:T(8,128)(2,1)S(1)} %pad_maximum_fusion.1.refs_0_, bf16[512,2048]{1,0:T(8,128)(2,1)} %collective-permute-done.10.refs_1_, bf16[512,2048]{1,0:T(8,128)(2,1)} %collective-permute-done.12.refs_2_, ...), custom_call_target="tpu_custom_call" | custom-call | bytes 1048576 | tf_op jit(solution)/shard_map/stack/pallas_call | solution.py:304
  178.7 11.8 %convert_add_fusion.refs_2_ = f32[1024,2048]{1,0:T(8,128)} fusion(bf16[1024,2048]{1,0:T(8,128)(2,1)S(1)} %copy-done.10, bf16[1024,1536]{1,0:T(8,128)(2,1)} %pad_maximum_fusion, bf16[2048,2048]{1,0:T(8,128)(2,1)} %get-tuple-element.431), kind=kOutput, calls=%fused_computation.2 | convolution fusion | flops 6446645248 | bytes 22020096 | tf_op jit(solution)/shard_map/dot_general | solution.py:25
  192.8 7.4 %resid_and_norm.1 = (f32[256,2048]{1,0:T(8,128)S(1)}, bf16[1024,2048]{1,0:T(8,128)(2,1)S(1)}, bf16[1024,2048]{1,0:T(8,128)(2,1)S(1)}) custom-call(s32[1]{0:T(128)} %bitcast.13.refs_0_, s32[8]{0:T(128)S(1)} %get-tuple-element.499.refs_1_.refs_0_, f32[1024,2048]{1,0:T(8,128)} %convert_add_fusion.refs_2_, ...), custom_call_target="tpu_custom_call" | custom-call | flops 2147483648 | bytes 20971520 | tf_op jit(solution)/shard_map/resid_and_norm/pallas_call | solution.py:243
  201.3 16.1 %fusion.28.dh_ref = f32[1024,2048]{1,0:T(8,128)} fusion(bf16[1024,2048]{1,0:T(8,128)(2,1)} %in_order.4, bf16[2048,2048]{1,0:T(8,128)(2,1)} %get-tuple-element.419.right_ref), kind=kOutput, calls=%fused_computation.135 | convolution fusion | flops 8589934592 | bytes 20971520 | tf_op jit(solution)/shard_map/dot_general | solution.py:21
  220.6 10.9 %fusion.29.gate_ref = f32[1024,2048]{1,0:T(8,128)} fusion(bf16[1024,2048]{1,0:T(8,128)(2,1)S(1)} %get-tuple-element.394.hat_ref, bf16[2048,2048]{1,0:T(8,128)(2,1)S(1)} %stack.46.b_ref), kind=kOutput, calls=%fused_computation.136 | convolution fusion | flops 8589934592 | bytes 20971520 | tf_op jit(solution)/shard_map/dot_general | solution.py:21
  236.1 20.2 %mid_layer.1 = (bf16[1024,2048]{1,0:T(8,128)(2,1)}, bf16[1024,2048]{1,0:T(8,128)(2,1)}, bf16[1024,2048]{1,0:T(8,128)(2,1)}) custom-call(bf16[1024,2048]{1,0:T(8,128)(2,1)} %copy-done.30, bf16[2048,2048]{1,0:T(8,128)(2,1)} %copy-done.2, f32[1024,2048]{1,0:T(8,128)} %fusion.29.gate_ref, f32[1024,2048]{1,0:T(8,128)} %fusion.28.dh_ref), custom_call_target="tpu_custom_call" | custom-call | flops 8589934592 | bytes 41943040 | tf_op jit(solution)/shard_map/mid_layer/pallas_call | solution.py:422
  256.3 23.8 %pair_product.1 = bf16[1024,2048]{1,0:T(8,128)(2,1)} custom-call(bf16[1024,2048]{1,0:T(8,128)(2,1)} %get-tuple-element.407.a_ref.right_ref, bf16[2048,2048]{1,0:T(8,128)(2,1)} %copy-done.1, bf16[1024,2048]{1,0:T(8,128)(2,1)} %get-tuple-element.413.c_ref.right_ref, bf16[2048,2048]{1,0:T(8,128)(2,1)} %copy-done.2), custom_call_target="tpu_custom_call" | custom-call | flops 17179869184 | bytes 25165824 | tf_op jit(solution)/shard_map/pair_product/pallas_call | solution.py:450
  282.1 13.4 %plain_beside.5 = bf16[2048,2048]{1,0:T(8,128)(2,1)} custom-call(bf16[1024,2048]{1,0:T(8,128)(2,1)} %copy-done, bf16[1024,2048]{1,0:T(8,128)(2,1)} %get-tuple-element.407.a_ref.right_ref), custom_call_target="tpu_custom_call" | custom-call | flops 4294967296 | bytes 1048576 | tf_op jit(solution)/shard_map/plain_beside/pallas_call | solution.py:371
  295.6 13.4 %collective-permute-done.34 = bf16[256,2048]{1,0:T(8,128)(2,1)} collective-permute-done((bf16[256,2048]{1,0:T(8,128)(2,1)S(1)}, bf16[256,2048]{1,0:T(8,128)(2,1)}, u32[]{:S(2)}, u32[]{:S(2)}) %collective-permute-start.34) | collective-permute-done | bytes 1048608 | tf_op jit(solution)/shard_map/ppermute | solution.py:475
  313.4 14.5 %plain_beside.6 = bf16[2048,2048]{1,0:T(8,128)(2,1)} custom-call(bf16[1024,2048]{1,0:T(8,128)(2,1)} %copy-done, bf16[1024,2048]{1,0:T(8,128)(2,1)} %get-tuple-element.413.c_ref.right_ref), custom_call_target="tpu_custom_call" | custom-call | flops 4294967296 | bytes 1048576 | tf_op jit(solution)/shard_map/plain_beside/pallas_call | solution.py:371
  327.9 10.8 %collective-permute-done.36 = bf16[256,2048]{1,0:T(8,128)(2,1)S(1)} collective-permute-done((bf16[256,2048]{1,0:T(8,128)(2,1)}, bf16[256,2048]{1,0:T(8,128)(2,1)S(1)}, u32[]{:S(2)}, u32[]{:S(2)}) %collective-permute-start.36) | collective-permute-done | bytes 1048608 | tf_op jit(solution)/shard_map/ppermute | solution.py:475
  342.0 13.7 %product_beside.1 = bf16[1024,2048]{1,0:T(8,128)(2,1)} custom-call(bf16[1024,2048]{1,0:T(8,128)(2,1)} %get-tuple-element.421.left_ref.right_ref, bf16[2048,2048]{1,0:T(8,128)(2,1)} %get-tuple-element.419.right_ref), custom_call_target="tpu_custom_call" | custom-call | flops 4294967296 | bytes 1048576 | tf_op jit(solution)/shard_map/product_beside/pallas_call | solution.py:393
  355.8 13.5 %plain_beside.7 = bf16[2048,2048]{1,0:T(8,128)(2,1)} custom-call(bf16[1024,2048]{1,0:T(8,128)(2,1)} %left_ref, bf16[1024,2048]{1,0:T(8,128)(2,1)} %get-tuple-element.421.left_ref.right_ref), custom_call_target="tpu_custom_call" | custom-call | flops 4294967296 | bytes 1048576 | tf_op jit(solution)/shard_map/plain_beside/pallas_call | solution.py:371
  390.3 13.5 %collective-permute-done.41 = bf16[256,512]{1,0:T(8,128)(2,1)S(1)} collective-permute-done((bf16[256,512]{1,0:T(8,128)(2,1)}, bf16[256,512]{1,0:T(8,128)(2,1)S(1)}, u32[]{:S(2)}, u32[]{:S(2)}) %collective-permute-start.41) | collective-permute-done | bytes 262176 | tf_op jit(solution)/shard_map/ppermute | solution.py:475
  403.8 16.9 %collective-permute-done.42 = bf16[256,512]{1,0:T(8,128)(2,1)S(1)} collective-permute-done((bf16[256,512]{1,0:T(8,128)(2,1)}, bf16[256,512]{1,0:T(8,128)(2,1)S(1)}, u32[]{:S(2)}, u32[]{:S(2)}) %collective-permute-start.42) | collective-permute-done | bytes 262176 | tf_op jit(solution)/shard_map/ppermute | solution.py:475
  424.1 23.3 %attend_backward.1 = (bf16[1024,512]{1,0:T(8,128)(2,1)S(1)}, bf16[1024,512]{1,0:T(8,128)(2,1)S(1)}, bf16[1024,512]{1,0:T(8,128)(2,1)S(1)}) custom-call(bf16[1024,512]{1,0:T(8,128)(2,1)S(1)} %copy-done.32, bf16[1024,512]{1,0:T(8,128)(2,1)} %copy-done.33, bf16[1024,512]{1,0:T(8,128)(2,1)} %copy-done.34, bf16[1024,512]{1,0:T(8,128)(2,1)} %get-tuple-element.472.att_ref, ...), custom_call_target="tpu_custom_call" | custom-call | flops 4294967296 | bytes 1048576 | tf_op jit(solution)/shard_map/attend_backward/pallas_call | solution.py:167
  453.8 8.2 %convolution_convert_fusion = bf16[1024,2048]{1,0:T(8,128)(2,1)} fusion(bf16[1024,1536]{1,0:T(8,128)(2,1)S(1)} %constant_dynamic-update-slice_fusion.right_ref, bf16[2048,1536]{1,0:T(8,128)(2,1)S(1)} %bitcast.48), kind=kOutput, calls=%fused_computation.6 | convolution fusion | flops 6444548096 | bytes 13631488 | tf_op jit(solution)/shard_map/dot_general | solution.py:25
  462.1 11.1 %plain_beside.8 = bf16[2048,1536]{1,0:T(8,128)(2,1)} custom-call(bf16[1024,2048]{1,0:T(8,128)(2,1)} %copy-done.27, bf16[1024,1536]{1,0:T(8,128)(2,1)} %copy-done.52), custom_call_target="tpu_custom_call" | custom-call | flops 4294967296 | bytes 1048576 | tf_op jit(solution)/shard_map/plain_beside/pallas_call | solution.py:371
  473.1 6.7 collective-permute-done.45
  498.0 6.6 plain_beside.9
  523.9 13.8 %collective-permute-done.50 = bf16[256,2048]{1,0:T(8,128)(2,1)} collective-permute-done((bf16[256,2048]{1,0:T(8,128)(2,1)S(1)}, bf16[256,2048]{1,0:T(8,128)(2,1)}, u32[]{:S(2)}, u32[]{:S(2)}) %collective-permute-start.50) | collective-permute-done | bytes 1048608 | tf_op jit(solution)/shard_map/ppermute | solution.py:597
  558.0 8.2 %collective-permute-done.54 = bf16[256,2048]{1,0:T(8,128)(2,1)} collective-permute-done((bf16[256,2048]{1,0:T(8,128)(2,1)}, bf16[256,2048]{1,0:T(8,128)(2,1)}, u32[]{:S(2)}, u32[]{:S(2)}) %collective-permute-start.54) | collective-permute-done | bytes 1048608 | tf_op jit(solution)/shard_map/ppermute | solution.py:597
  580.2 11.4 %collective-permute-done.56 = bf16[256,2048]{1,0:T(8,128)(2,1)S(1)} collective-permute-done((bf16[256,2048]{1,0:T(8,128)(2,1)S(1)}, bf16[256,2048]{1,0:T(8,128)(2,1)S(1)}, u32[]{:S(2)}, u32[]{:S(2)}) %collective-permute-start.56) | collective-permute-done | bytes 1048608 | tf_op jit(solution)/shard_map/ppermute | solution.py:597
  611.9 13.1 %collective-permute-done.58 = bf16[256,2048]{1,0:T(8,128)(2,1)} collective-permute-done((bf16[256,2048]{1,0:T(8,128)(2,1)}, bf16[256,2048]{1,0:T(8,128)(2,1)}, u32[]{:S(2)}, u32[]{:S(2)}) %collective-permute-start.58) | collective-permute-done | bytes 1048608 | tf_op jit(solution)/shard_map/ppermute | solution.py:475
  635.6 12.9 %collective-permute-done.59 = bf16[256,2048]{1,0:T(8,128)(2,1)S(1)} collective-permute-done((bf16[256,2048]{1,0:T(8,128)(2,1)}, bf16[256,2048]{1,0:T(8,128)(2,1)S(1)}, u32[]{:S(2)}, u32[]{:S(2)}) %collective-permute-start.59) | collective-permute-done | bytes 1048608 | tf_op jit(solution)/shard_map/ppermute | solution.py:475
  659.8 9.3 %collective-permute-done.60 = bf16[256,2048]{1,0:T(8,128)(2,1)} collective-permute-done((bf16[256,2048]{1,0:T(8,128)(2,1)S(1)}, bf16[256,2048]{1,0:T(8,128)(2,1)}, u32[]{:S(2)}, u32[]{:S(2)}) %collective-permute-start.60) | collective-permute-done | bytes 1048608 | tf_op jit(solution)/shard_map/ppermute | solution.py:475
  (370 shorter events, 269.5 us)
Async XLA Ops:
  7.2 620.8 %reduce-scatter.10.cloned.1.call-start = ((), (), s32[]{:S(2)}) async-start(), calls=%async_computation.7 | async-start | bytes 9437184 | tf_op jit(solution)/shard_map/reduce_scatter | solution.py:784
  53.7 45.8 %collective-permute-start.12 = (bf16[512,2048]{1,0:T(8,128)(2,1)S(1)}, bf16[512,2048]{1,0:T(8,128)(2,1)}, u32[]{:S(2)}, u32[]{:S(2)}) collective-permute-start(bf16[512,2048]{1,0:T(8,128)(2,1)S(1)} %pad_maximum_fusion.1.refs_0_), channel_id=1, source_target_pairs={{0,8},{4,20},{8,0},{12,28},{16,24},{20,4},{24,16},{28,12},{1,9},{5... | collective-permute-start | bytes 6291464 | tf_op jit(solution)/shard_map/ppermute | solution.py:480
  55.3 47.1 %collective-permute-start.13 = (bf16[512,2048]{1,0:T(8,128)(2,1)}, bf16[512,2048]{1,0:T(8,128)(2,1)}, u32[]{:S(2)}, u32[]{:S(2)}) collective-permute-start(bf16[512,2048]{1,0:T(8,128)(2,1)} %collective-permute-done.10.refs_1_), channel_id=1, source_target_pairs={{0,8},{4,20},{8,0},{12,28},{16,24},{20,4},{24,16},{28,12},{1,9},{5... | collective-permute-start | bytes 6291464 | tf_op jit(solution)/shard_map/ppermute | solution.py:480
  87.6 30.9 %collective-permute-start.11 = (bf16[1024,512]{1,0:T(8,128)(2,1)}, bf16[1024,512]{1,0:T(8,128)(2,1)}, u32[]{:S(2)}, u32[]{:S(2)}) collective-permute-start(bf16[1024,512]{1,0:T(8,128)(2,1)} %get-tuple-element.472.att_ref), channel_id=1, source_target_pairs={{0,1},{1,2},{2,3},{3,0},{4,5},{5,6},{6,7},{7,4},{8,9},{9,10},{10,1... | collective-permute-start | bytes 3145736 | tf_op jit(solution)/shard_map/ppermute | solution.py:475
  102.4 47.9 %collective-permute-start.18 = (bf16[512,2048]{1,0:T(8,128)(2,1)}, bf16[512,2048]{1,0:T(8,128)(2,1)}, u32[]{:S(2)}, u32[]{:S(2)}) collective-permute-start(bf16[512,2048]{1,0:T(8,128)(2,1)} %collective-permute-done.12.refs_2_), channel_id=1, source_target_pairs={{0,16},{4,12},{8,24},{12,4},{16,0},{20,28},{24,8},{28,20},{1,17},{... | collective-permute-start | bytes 6291464 | tf_op jit(solution)/shard_map/ppermute | solution.py:480
  120.0 29.3 %collective-permute-start.17 = (bf16[256,2048]{1,0:T(8,128)(2,1)}, bf16[256,2048]{1,0:T(8,128)(2,1)S(1)}, u32[]{:S(2)}, u32[]{:S(2)}) collective-permute-start(bf16[256,2048]{1,0:T(8,128)(2,1)} %collective-permute-done.15.refs_1_), channel_id=1, source_target_pairs={{0,8},{4,20},{8,0},{12,28},{16,24},{20,4},{24,16},{28,12},{1,9},{5... | collective-permute-start | bytes 3145736 | tf_op jit(solution)/shard_map/ppermute | solution.py:480
  120.5 28.8 %collective-permute-start.14 = (bf16[1024,512]{1,0:T(8,128)(2,1)}, bf16[1024,512]{1,0:T(8,128)(2,1)S(1)}, u32[]{:S(2)}, u32[]{:S(2)}) collective-permute-start(bf16[1024,512]{1,0:T(8,128)(2,1)} %collective-permute-done.11), channel_id=1, source_target_pairs={{0,1},{1,2},{2,3},{3,0},{4,5},{5,6},{6,7},{7,4},{8,9},{9,10},{10,1... | collective-permute-start | bytes 3145736 | tf_op jit(solution)/shard_map/ppermute | solution.py:475
  121.3 28.0 %collective-permute-start.19 = (bf16[256,2048]{1,0:T(8,128)(2,1)S(1)}, bf16[256,2048]{1,0:T(8,128)(2,1)S(1)}, u32[]{:S(2)}, u32[]{:S(2)}) collective-permute-start(bf16[256,2048]{1,0:T(8,128)(2,1)S(1)} %multiply_convert_fusion.refs_0_), channel_id=1, source_target_pairs={{0,4},{4,0},{8,12},{12,8},{16,20},{20,16},{24,28},{28,24},{1,5},{5... | collective-permute-start | bytes 3145736 | tf_op jit(solution)/shard_map/ppermute | solution.py:470
  138.1 26.4 %collective-permute-start.20 = (bf16[512,2048]{1,0:T(8,128)(2,1)}, bf16[512,2048]{1,0:T(8,128)(2,1)}, u32[]{:S(2)}, u32[]{:S(2)}) collective-permute-start(bf16[512,2048]{1,0:T(8,128)(2,1)} %collective-permute-done.12.refs_2_), channel_id=1, source_target_pairs={{0,4},{4,0},{8,12},{12,8},{16,20},{20,16},{24,28},{28,24},{1,5},{5... | collective-permute-start | bytes 6291464 | tf_op jit(solution)/shard_map/ppermute | solution.py:470
  153.6 36.9 %collective-permute-start.23 = (bf16[1024,512]{1,0:T(8,128)(2,1)}, bf16[1024,512]{1,0:T(8,128)(2,1)S(1)}, u32[]{:S(2)}, u32[]{:S(2)}) collective-permute-start(bf16[1024,512]{1,0:T(8,128)(2,1)} %copy-done.47), channel_id=1, source_target_pairs={{0,1},{1,2},{2,3},{3,0},{4,5},{5,6},{6,7},{7,4},{8,9},{9,10},{10,1... | collective-permute-start | bytes 3145736 | tf_op jit(solution)/shard_map/ppermute | solution.py:475
  159.8 30.6 %collective-permute-start.24 = (bf16[256,2048]{1,0:T(8,128)(2,1)}, bf16[256,2048]{1,0:T(8,128)(2,1)S(1)}, u32[]{:S(2)}, u32[]{:S(2)}) collective-permute-start(bf16[256,2048]{1,0:T(8,128)(2,1)} %copy-done.14), channel_id=1, source_target_pairs={{0,16},{4,12},{8,24},{12,4},{16,0},{20,28},{24,8},{28,20},{1,17},{... | collective-permute-start | bytes 3145736 | tf_op jit(solution)/shard_map/ppermute | solution.py:480
  164.4 35.8 %collective-permute-start.25 = (bf16[256,2048]{1,0:T(8,128)(2,1)S(1)}, bf16[256,2048]{1,0:T(8,128)(2,1)S(1)}, u32[]{:S(2)}, u32[]{:S(2)}) collective-permute-start(bf16[256,2048]{1,0:T(8,128)(2,1)S(1)} %multiply_convert_fusion.refs_0_), channel_id=1, source_target_pairs={{0,8},{4,20},{8,0},{12,28},{16,24},{20,4},{24,16},{28,12},{1,9},{5... | collective-permute-start | bytes 3145736 | tf_op jit(solution)/shard_map/ppermute | solution.py:480
  166.0 51.4 %collective-permute-start.28 = (bf16[256,2048]{1,0:T(8,128)(2,1)S(1)}, bf16[256,2048]{1,0:T(8,128)(2,1)S(1)}, u32[]{:S(2)}, u32[]{:S(2)}) collective-permute-start(bf16[256,2048]{1,0:T(8,128)(2,1)S(1)} %copy-done.15), channel_id=1, source_target_pairs={{0,4},{4,0},{8,12},{12,8},{16,20},{20,16},{24,28},{28,24},{1,5},{5... | collective-permute-start | bytes 3145736 | tf_op jit(solution)/shard_map/ppermute | solution.py:470
  166.0 54.0 %collective-permute-start.26 = (bf16[256,2048]{1,0:T(8,128)(2,1)S(1)}, bf16[256,2048]{1,0:T(8,128)(2,1)S(1)}, u32[]{:S(2)}, u32[]{:S(2)}) collective-permute-start(bf16[256,2048]{1,0:T(8,128)(2,1)S(1)} %copy-done.13), channel_id=1, source_target_pairs={{0,8},{4,20},{8,0},{12,28},{16,24},{20,4},{24,16},{28,12},{1,9},{5... | collective-permute-start | bytes 3145736 | tf_op jit(solution)/shard_map/ppermute | solution.py:480
  190.5 27.0 %collective-permute-start.29 = (bf16[256,2048]{1,0:T(8,128)(2,1)S(1)}, bf16[256,2048]{1,0:T(8,128)(2,1)}, u32[]{:S(2)}, u32[]{:S(2)}) collective-permute-start(bf16[256,2048]{1,0:T(8,128)(2,1)S(1)} %copy-done.17), channel_id=1, source_target_pairs={{0,4},{4,0},{8,12},{12,8},{16,20},{20,16},{24,28},{28,24},{1,5},{5... | collective-permute-start | bytes 3145736 | tf_op jit(solution)/shard_map/ppermute | solution.py:470
  190.7 26.8 %collective-permute-start.30 = (bf16[256,2048]{1,0:T(8,128)(2,1)S(1)}, bf16[256,2048]{1,0:T(8,128)(2,1)}, u32[]{:S(2)}, u32[]{:S(2)}) collective-permute-start(bf16[256,2048]{1,0:T(8,128)(2,1)S(1)} %collective-permute-done.24.refs_4_), channel_id=1, source_target_pairs={{0,4},{4,0},{8,12},{12,8},{16,20},{20,16},{24,28},{28,24},{1,5},{5... | collective-permute-start | bytes 3145736 | tf_op jit(solution)/shard_map/ppermute | solution.py:470
  281.5 27.5 %collective-permute-start.34 = (bf16[256,2048]{1,0:T(8,128)(2,1)S(1)}, bf16[256,2048]{1,0:T(8,128)(2,1)}, u32[]{:S(2)}, u32[]{:S(2)}) collective-permute-start(bf16[256,2048]{1,0:T(8,128)(2,1)S(1)} %constant_dynamic-slice_fusion.7), channel_id=1, source_target_pairs={{0,1},{1,2},{2,3},{3,0},{4,5},{5,6},{6,7},{7,4},{8,9},{9,10},{10,1... | collective-permute-start | bytes 3145736 | tf_op jit(solution)/shard_map/ppermute | solution.py:475
  308.9 322.1 %reduce-scatter.8.cloned.1.call-start = ((), (), s32[]{:S(2)}) async-start(), calls=%async_computation.6 | async-start | bytes 9437184 | tf_op jit(solution)/shard_map/reduce_scatter | solution.py:784
  311.9 26.7 %collective-permute-start.36 = (bf16[256,2048]{1,0:T(8,128)(2,1)}, bf16[256,2048]{1,0:T(8,128)(2,1)S(1)}, u32[]{:S(2)}, u32[]{:S(2)}) collective-permute-start(bf16[256,2048]{1,0:T(8,128)(2,1)} %add_convert_fusion.8), channel_id=1, source_target_pairs={{0,1},{1,2},{2,3},{3,0},{4,5},{5,6},{6,7},{7,4},{8,9},{9,10},{10,1... | collective-permute-start | bytes 3145736 | tf_op jit(solution)/shard_map/ppermute | solution.py:475
  338.7 295.4 %reduce-scatter.6.cloned.1.call-start = ((), (), s32[]{:S(2)}) async-start(), calls=%async_computation.5 | async-start | bytes 9437184 | tf_op jit(solution)/shard_map/reduce_scatter | solution.py:784
  341.4 27.9 %collective-permute-start.38 = (bf16[256,2048]{1,0:T(8,128)(2,1)}, bf16[256,2048]{1,0:T(8,128)(2,1)S(1)}, u32[]{:S(2)}, u32[]{:S(2)}) collective-permute-start(bf16[256,2048]{1,0:T(8,128)(2,1)} %add_convert_fusion.7), channel_id=1, source_target_pairs={{0,1},{1,2},{2,3},{3,0},{4,5},{5,6},{6,7},{7,4},{8,9},{9,10},{10,1... | collective-permute-start | bytes 3145736 | tf_op jit(solution)/shard_map/ppermute | solution.py:475
  341.4 27.9 %collective-permute-start.39 = (f32[8]{0:T(128)S(1)}, f32[8]{0:T(128)S(1)}, u32[]{:S(2)}, u32[]{:S(2)}) collective-permute-start(f32[8]{0:T(128)S(1)} %max.22), channel_id=1, source_target_pairs={{0,16},{4,20},{8,24},{12,28},{16,0},{20,4},{24,8},{28,12},{1,17},{... | collective-permute-start | bytes 104 | tf_op jit(solution)/shard_map/ppermute | solution.py:470
  369.3 282.5 %reduce-scatter.12.cloned.1.call-start = ((), (), s32[]{:S(2)}) async-start(), calls=%async_computation.8 | async-start | bytes 7077888 | tf_op jit(solution)/shard_map/reduce_scatter | solution.py:784
  373.3 47.7 %collective-permute-start.40 = (bf16[256,2048]{1,0:T(8,128)(2,1)}, bf16[256,2048]{1,0:T(8,128)(2,1)}, u32[]{:S(2)}, u32[]{:S(2)}) collective-permute-start(bf16[256,2048]{1,0:T(8,128)(2,1)} %constant_dynamic-slice_fusion.6), channel_id=1, source_target_pairs={{0,1},{1,2},{2,3},{3,0},{4,5},{5,6},{6,7},{7,4},{8,9},{9,10},{10,1... | collective-permute-start | bytes 3145736 | tf_op jit(solution)/shard_map/ppermute | solution.py:475
  387.8 32.9 %collective-permute-start.42 = (bf16[256,512]{1,0:T(8,128)(2,1)}, bf16[256,512]{1,0:T(8,128)(2,1)S(1)}, u32[]{:S(2)}, u32[]{:S(2)}) collective-permute-start(bf16[256,512]{1,0:T(8,128)(2,1)} %get-tuple-element.609), channel_id=1, source_target_pairs={{0,2},{1,3},{2,0},{3,1},{4,6},{5,7},{6,4},{7,5},{8,10},{9,11},{10,... | collective-permute-start | bytes 786440 | tf_op jit(solution)/shard_map/ppermute | solution.py:475
  388.3 32.4 %collective-permute-start.43 = (bf16[256,512]{1,0:T(8,128)(2,1)}, bf16[256,512]{1,0:T(8,128)(2,1)S(1)}, u32[]{:S(2)}, u32[]{:S(2)}) collective-permute-start(bf16[256,512]{1,0:T(8,128)(2,1)} %get-tuple-element.608), channel_id=1, source_target_pairs={{0,1},{1,2},{2,3},{3,0},{4,5},{5,6},{6,7},{7,4},{8,9},{9,10},{10,1... | collective-permute-start | bytes 786440 | tf_op jit(solution)/shard_map/ppermute | solution.py:475
  424.0 26.9 %collective-permute-start.44 = (bf16[256,2048]{1,0:T(8,128)(2,1)S(1)}, bf16[256,2048]{1,0:T(8,128)(2,1)S(1)}, u32[]{:S(2)}, u32[]{:S(2)}) collective-permute-start(bf16[256,2048]{1,0:T(8,128)(2,1)S(1)} %add_convert_fusion.6), channel_id=1, source_target_pairs={{0,1},{1,2},{2,3},{3,0},{4,5},{5,6},{6,7},{7,4},{8,9},{9,10},{10,1... | collective-permute-start | bytes 3145736 | tf_op jit(solution)/shard_map/ppermute | solution.py:475
  453.6 26.2 %collective-permute-start.45 = (bf16[256,2048]{1,0:T(8,128)(2,1)}, bf16[256,2048]{1,0:T(8,128)(2,1)S(1)}, u32[]{:S(2)}, u32[]{:S(2)}) collective-permute-start(bf16[256,2048]{1,0:T(8,128)(2,1)} %add_convert_fusion.5), channel_id=1, source_target_pairs={{0,1},{1,2},{2,3},{3,0},{4,5},{5,6},{6,7},{7,4},{8,9},{9,10},{10,1... | collective-permute-start | bytes 3145736 | tf_op jit(solution)/shard_map/ppermute | solution.py:475
  479.8 192.7 %reduce-scatter.14.cloned.1.call-start = ((), (), s32[]{:S(2)}) async-start(), calls=%async_computation.9 | async-start | bytes 9437184 | tf_op jit(solution)/shard_map/reduce_scatter | solution.py:784
  520.6 29.6 %collective-permute-start.48 = (bf16[256,2048]{1,0:T(8,128)(2,1)}, bf16[256,2048]{1,0:T(8,128)(2,1)}, u32[]{:S(2)}, u32[]{:S(2)}) collective-permute-start(bf16[256,2048]{1,0:T(8,128)(2,1)} %collective-permute-done.46), channel_id=1, source_target_pairs={{1,2},{2,3},{5,6},{6,7},{9,10},{10,11},{13,14},{14,15},{17,18},{18... | collective-permute-start | bytes 3145736 | tf_op jit(solution)/shard_map/ppermute | solution.py:642
  522.4 27.8 %collective-permute-start.49 = (bf16[256,2048]{1,0:T(8,128)(2,1)S(1)}, bf16[256,2048]{1,0:T(8,128)(2,1)}, u32[]{:S(2)}, u32[]{:S(2)}) collective-permute-start(bf16[256,2048]{1,0:T(8,128)(2,1)S(1)} %collective-permute-done.47), channel_id=1, source_target_pairs={{2,1},{1,0},{6,5},{5,4},{10,9},{9,8},{14,13},{13,12},{18,17},{17,1... | collective-permute-start | bytes 3145736 | tf_op jit(solution)/shard_map/ppermute | solution.py:642
  550.2 25.9 %collective-permute-start.52 = (bf16[256,2048]{1,0:T(8,128)(2,1)}, bf16[256,2048]{1,0:T(8,128)(2,1)S(1)}, u32[]{:S(2)}, u32[]{:S(2)}) collective-permute-start(bf16[256,2048]{1,0:T(8,128)(2,1)} %collective-permute-done.48), channel_id=1, source_target_pairs={{2,3},{6,7},{10,11},{14,15},{18,19},{22,23},{26,27},{30,31}} | collective-permute-start | bytes 3145736 | tf_op jit(solution)/shard_map/ppermute | solution.py:642
  (101 other events, 1249.8 us)
Sparse Core Ops, SparseCore 0:
  309.1 68.4 reduce-scatter.9
  381.4 71.2 reduce-scatter.7
  456.2 71.2 reduce-scatter.5
  531.1 61.7 reduce-scatter.11
  596.2 71.2 reduce-scatter.13
